TPU v7x, 512 devices: a whole 4x4x16 slice. The times are simulated.
512 devices in a mesh: ga: 64 (over y, z_lo, x), col: 8 (over z_hi, core).
Axes of the slice: x: 4, y: 4, z: 16 (z_hi: 4, z_lo: 4; z = z_hi * 4 + z_lo), core: 2. Of those that a mesh axis runs over, the one named last changes fastest.
Arguments:
- valence: bfloat16 [128, 64, 4096], P('col', 'ga'), may hold values from -6 to 6
- conduction: bfloat16 [256, 64, 4096], P('col', 'ga'), may hold values from -6 to 6
- band_index: int32 [1], replicated, may hold values from 0 to 127
- occ_valence: int32 [128], replicated, may hold values from 1 to 2
- occ_conduction: int32 [256], P('col'), may hold values from 0 to 1
- gap_energy: float32 [256], P('col'), may hold values from 0.5 to 20
- row_map: int32 [8192], P('ga'), may hold values from 0 to 4095
- col_map: int32 [4096], P('ga'), may hold values from 0 to 4095
Outputs:
- chi_panel: float32 [2, 8192, 4096], P(None, 'ga', 'col')
Inputs may be any that keep to these rules, and one draw needn't show every extreme that they name: `row_map`: maps give positions inside the slab of the row block that holds the entry; entries may repeat.
All inputs are finite; a program needn't handle non-finite values.
Results may differ from a plain program's by a relative error of at most 0.025.
Values may be sent and summed in bfloat16 or wider, within the bound.
No kernel may reach another device: no remote copies, remote signals or barrier semaphores. Data moves between devices by JAX's collectives and lax.ppermute only.
A program may use at most 64 MiB of HBM per device.

v0:
```python
import math

import jax
import jax.numpy as jnp
from jax import lax
from jax.sharding import PartitionSpec as P

NX = 64
NY = 64
NZ = 64


middle = lax.Precision.HIGH


def from_root(value, axis, source):
    kept = jnp.where(lax.axis_index(axis) == source, value, 0).astype(value.dtype)
    return lax.psum(kept, axis)


def dft_tables(length):
    index = jnp.arange(length, dtype=jnp.int32)
    phase = index[:, None] * index[None, :] % length
    angle = phase.astype(jnp.float32) * (2.0 * math.pi / length)
    factor = 1.0 / math.sqrt(length)
    return (jnp.cos(angle) * factor, jnp.sin(angle) * factor)


def split_table(table):
    upper_part = table.astype(jnp.bfloat16)
    lower_part = (table - upper_part.astype(jnp.float32)).astype(jnp.bfloat16)
    return (upper_part, lower_part)


def exact_product(planes, table):
    upper_part, lower_part = split_table(table)
    first_term = jnp.einsum("byz,zk->byk", planes, upper_part, preferred_element_type=jnp.float32)
    second_term = jnp.einsum("byz,zk->byk", planes, lower_part, preferred_element_type=jnp.float32)
    return first_term + second_term


def rotate(cos_table, sin_table, real_part, imag_part, form):
    real_out = jnp.einsum(form, cos_table, real_part, precision=middle) + jnp.einsum(
        form, sin_table, imag_part, precision=middle
    )
    imag_out = jnp.einsum(form, cos_table, imag_part, precision=middle) - jnp.einsum(
        form, sin_table, real_part, precision=middle
    )
    return (real_out, imag_out)


def shards(
    valence, conduction, band_index, occ_valence, occ_conduction, gap_energy, row_map, col_map
):
    nv_local = valence.shape[0]
    chosen = band_index[0]
    owner_col = chosen // nv_local
    local_band = chosen % nv_local
    own_band = lax.dynamic_index_in_dim(valence, local_band, 0, keepdims=False)
    valence_band = from_root(own_band, "col", owner_col)
    nc_local = conduction.shape[0]
    x_local = conduction.shape[1]
    pair = (valence_band[None].astype(jnp.float32) * conduction.astype(jnp.float32)).astype(
        jnp.bfloat16
    )
    planes = pair.reshape(nc_local * x_local, NY, NZ)
    cos_z, sin_z = dft_tables(NZ)
    real_z = exact_product(planes, cos_z)
    imag_z = -exact_product(planes, sin_z)
    cos_y, sin_y = dft_tables(NY)
    real_y, imag_y = rotate(cos_y, sin_y, real_z, imag_z, "ky,byz->bkz")
    half = (
        jnp.concatenate([real_y, imag_y], axis=-1)
        .astype(jnp.bfloat16)
        .reshape(nc_local, x_local, NY, 2 * NZ)
    )
    cos_x, sin_x = dft_tables(NX)
    block = lax.all_to_all(half, "ga", split_axis=2, concat_axis=1, tiled=True)
    real_in = block[..., :NZ].astype(jnp.float32)
    imag_in = block[..., NZ:].astype(jnp.float32)
    real_x, imag_x = rotate(cos_x, sin_x, real_in, imag_in, "kx,bxyz->bkyz")
    spectra = jnp.stack([real_x, imag_x], axis=1).reshape(block.shape[0], 2, -1)
    row_vals = jnp.take(spectra, row_map, axis=2)
    col_vals = jnp.take(spectra, col_map, axis=2)
    weight = 2.0 * (occ_conduction - occ_valence[chosen]).astype(jnp.float32) / gap_energy
    row_real = (row_vals[:, 0, :] * weight[:, None]).T
    row_imag = (row_vals[:, 1, :] * weight[:, None]).T
    upper = jnp.concatenate([row_real, row_imag], axis=1)
    bottom = jnp.concatenate([row_imag, -row_real], axis=1)
    weighted = jnp.concatenate([upper, bottom], axis=0).astype(jnp.bfloat16)
    columns = jnp.concatenate([col_vals[:, 0, :].T, col_vals[:, 1, :].T], axis=1).astype(
        jnp.bfloat16
    )
    rows_dev = row_map.shape[0]
    ga_count = lax.axis_size("ga")
    col_count = lax.axis_size("col")
    scale = 1.0 / math.sqrt(nc_local * col_count)
    panel_dev = columns.shape[0]
    piece = lax.all_gather(columns, "ga", axis=0, tiled=True)
    count = piece.shape[0] // panel_dev
    product = jnp.einsum("rc,pc->rp", weighted, piece, preferred_element_type=jnp.float32)
    placed = product.reshape(2 * rows_dev, count, panel_dev).transpose(0, 2, 1)
    partial_value = placed
    partial_value = partial_value.reshape(2, rows_dev, panel_dev * ga_count)
    summed = lax.psum_scatter(
        partial_value.astype(jnp.bfloat16), "col", scatter_dimension=2, tiled=True
    ).astype(jnp.float32)
    return summed * scale


def solution(mesh):
    return jax.shard_map(
        shards,
        mesh=mesh,
        in_specs=(
            P("col", "ga", None),
            P("col", "ga", None),
            P(),
            P(),
            P("col"),
            P("col"),
            P("ga"),
            P("ga"),
        ),
        out_specs=P(None, "ga", "col"),
        check_vma=False,
    )
```

profile of v0, /device:TPU:1, one launch (start us, length us, event | category | flops | bytes accessed | tf_op | source)
XLA Modules:
  0.0 421.0 jit_solution(17863495932740836894)
XLA Ops:
  7.2 0.9 fusion.36
  8.1 24.3 %psum.7 = bf16[4096]{0:T(1024)(128)(2,1)S(1)} all-reduce(bf16[4096]{0:T(1024)(128)(2,1)S(1)} %fusion.36), channel_id=1, replica_groups=mesh['ga'=64,'col'=8] {'col'}, use_global_device_ids=true, to_apply=%region_0.1 | all-reduce | flops 4096 | bytes 16384 | tf_op jit(solution)/shard_map/psum | solution.py:18
  32.4 1.0 multiply_convert_fusion
  33.4 0.5 reshape.98
  34.0 0.4 fusion.43
  34.4 0.4 fusion.41
  34.8 0.4 convolution_add_fusion.3
  35.2 0.7 fusion.30
  35.9 0.4 fusion.2
  36.3 0.7 fusion.28
  37.1 0.7 fusion.6
  37.8 0.7 fusion.5
  38.6 0.3 pad_maximum_fusion.1
  38.9 1.1 copy.60
  40.0 8.9 %all-to-all-start = ((bf16[32,1,64,128]{3,0,1,2:T(8,128)(2,1)}), bf16[32,1,64,128]{3,0,1,2:T(8,128)(2,1)S(1)}, u32[]{:S(2)}, u32[]{:S(2)}) async-start(bf16[32,1,64,128]{3,0,1,2:T(8,128)(2,1)} %copy.60), calls=%async_computation | async-start | bytes 1048576 | tf_op jit(solution)/shard_map/all_to_all | solution.py:78
  49.0 0.2 all-reduce.3.cloned.1.call-start
  49.2 0.6 dynamic_slice.8
  49.9 0.6 multiply_divide_fusion
  50.5 11.7 %all-to-all-done = bf16[32,1,64,128]{3,0,1,2:T(8,128)(2,1)S(1)} async-done(((bf16[32,1,64,128]{3,0,1,2:T(8,128)(2,1)}), bf16[32,1,64,128]{3,0,1,2:T(8,128)(2,1)S(1)}, u32[]{:S(2)}, u32[]{:S(2)}) %all-to-all-start) | async-done | bytes 524320 | tf_op jit(solution)/shard_map/all_to_all | solution.py:78
  62.2 0.7 copy.61
  62.9 0.6 fusion.7
  63.5 0.6 fusion.8
  64.0 0.6 fusion.1
  64.6 1.3 copy.62
  65.9 2.4 stack.9
  68.3 0.6 fusion
  68.9 0.3 copy.63
  69.2 0.4 stack.10
  69.6 0.3 copy-done
  70.0 4.4 %copy.64 = f32[32,2,4096]{0,1,2:T(2,128)} copy(f32[32,2,4096]{2,0,1:T(8,128)S(1)} %pad_maximum_fusion) | data formatting | bytes 2097152 | tf_op jit(solution)/shard_map/stack | solution.py:82
  74.4 2.9 gather_fusion
  77.3 0.2 select_bitcast_fusion
  77.5 0.1 fusion.112
  77.7 2.8 gather_fusion.1
  80.5 0.1 fusion.35
  80.7 0.1 copy.68
  80.8 0.1 copy.69
  80.9 0.1 copy.70
  81.0 159.2 %all_gather.3 = bf16[4096,64]{1,0:T(8,128)(2,1)S(1)} all-gather(bf16[64,64]{1,0:T(8,128)(2,1)S(1)} %copy.70), channel_id=1, replica_groups=mesh['ga'=64,'col'=8] {'ga'}, dimensions={0}, use_global_device_ids=true | all-gather | bytes 532480 | tf_op jit(solution)/shard_map/all_gather | solution.py:99
  240.2 0.8 convolution_convert_fusion
  241.0 2.5 copy.71
  243.4 2.8 copy.72
  246.2 2.1 convert_element_type.113
  248.3 1.3 dynamic-slice
  250.2 161.8 %all-reduce.3.cloned.1.call-done = bf16[2,128,4096]{1,0,2:T(2,128)(2,1)} async-done(((bf16[2,128,4096]{1,0,2:T(2,128)(2,1)}), bf16[2,128,4096]{1,0,2:T(2,128)(2,1)}) %all-reduce.3.cloned.1.call-update) | async-done | bytes 2097168
  412.0 1.1 constant_dynamic-slice_fusion
  413.2 0.2 copy.73
  413.3 0.9 convert_multiply_fusion
  (23 shorter events, 0.2 us)
Async XLA Ops:
  38.5 10.7 %copy-start.3 = (s32[128]{0:T(128)S(1)}, s32[128]{0:T(128)}, u32[]{:S(2)}) copy-start(s32[128]{0:T(128)} %param.11) | copy-start | bytes 1540
  38.5 11.3 %copy-start.4 = (s32[128]{0:T(128)S(1)}, s32[128]{0:T(128)}, u32[]{:S(2)}) copy-start(s32[128]{0:T(128)} %param.14) | copy-start | bytes 1540
  38.6 11.3 %copy-start.5 = (s32[64]{0:T(128)S(1)}, s32[64]{0:T(128)}, u32[]{:S(2)}) copy-start(s32[64]{0:T(128)} %param.15) | copy-start | bytes 772
  38.6 11.3 %copy-start.1 = (f32[32]{0:T(128)S(1)}, f32[32]{0:T(128)}, u32[]{:S(2)}) copy-start(f32[32]{0:T(128)} %param.13) | copy-start | bytes 388
  38.6 11.3 %copy-start.2 = (s32[32]{0:T(128)S(1)}, s32[32]{0:T(128)}, u32[]{:S(2)}) copy-start(s32[32]{0:T(128)} %param.12) | copy-start | bytes 388
  40.0 22.1 %all-to-all-start = ((bf16[32,1,64,128]{3,0,1,2:T(8,128)(2,1)}), bf16[32,1,64,128]{3,0,1,2:T(8,128)(2,1)S(1)}, u32[]{:S(2)}, u32[]{:S(2)}) async-start(bf16[32,1,64,128]{3,0,1,2:T(8,128)(2,1)} %copy.60), calls=%async_computation | async-start | bytes 1048576 | tf_op jit(solution)/shard_map/all_to_all | solution.py:78
  49.0 363.1 %all-reduce.3.cloned.1.call-start = ((), (), s32[]{:S(2)}) async-start(), calls=%async_computation.1 | async-start | bytes 4194304
  68.9 1.0 copy-start
Sparse Core Ops, SparseCore 0:
  248.4 163.6 all-reduce.2
where the time goes:
time: 423 us; the launch traced here: 421 us
  blocking collectives  183 us (43%)
  waiting for transfers between devices  174 us (41%)
  local copies, waits for them, and re-layouts  28.2 us (7%)
  between operations  15.1 us (4%)
  starting transfers between devices  9.16 us (2%)
  matrix products  7.54 us (2%)
    unnamed x2, waiting for transfers between devices  162 us
    all_gather x1, blocking collectives, shards(): piece = lax.all_gather(columns, 'ga', axis=0, tiled=True)  159 us
    psum x1, blocking collectives, from_root(): return lax.psum(kept, axis)  24.3 us
    all_to_all x1, waiting for transfers between devices, shards(): block = lax.all_to_all(half, 'ga', split_axis=2, concat_axis=1, tiled=True)  11.7 us
    all_to_all x1, starting transfers between devices, shards(): block = lax.all_to_all(half, 'ga', split_axis=2, concat_axis=1, tiled=True)  8.94 us
  transfers between devices with their start and end apart: 2, of which 2 were waited for; matrix products, arithmetic and copies ran while one was open for 1% of the time, Pallas kernels for 0%

commit v1 on v0

v1 whole, which is shorter than its diff:
```python
import math

import jax
import jax.numpy as jnp
import numpy as np
from jax import lax
from jax.experimental import pallas as pl
from jax.experimental.pallas import tpu as pltpu
from jax.sharding import Mesh
from jax.sharding import PartitionSpec as P

N = 64
BANDS = 32
ROWS = 128
COLS = 64
SPOTS = ROWS + COLS
LANES = 128
GA = ("y", "zl", "x")
COL = ("zh", "c")

f32 = jnp.float32
bf16 = jnp.bfloat16


def dot(left, right):
    return jnp.dot(left, right, preferred_element_type=f32)


def lane_index(shape):
    return lax.broadcasted_iota(jnp.int32, shape, len(shape) - 1)


def y_table():
    parity = np.arange(2)[:, None, None, None]
    ky = np.arange(N // 2)[None, :, None, None]
    imag = np.arange(2)[None, None, :, None]
    half = np.arange(N // 2)[None, None, None, :]
    turn = (ky * (2 * half + parity) + 16 * imag) % N
    return (np.cos(2.0 * np.pi * turn / N) / 8.0).reshape(LANES, N // 2).astype(np.float32)


def pair_y_kernel(v_ref, c_ref, e_ref, out_ref, by_band, by_ky):
    v = v_ref[...].astype(f32)
    for i in range(N // 2):
        bands = c_ref[:, i * LANES : (i + 1) * LANES].astype(f32)
        pair = (bands * v[i : i + 1, :]).astype(bf16).astype(f32)
        by_band[pl.ds(i, BANDS, stride=N // 2), :] = pair
    table = e_ref[...]
    low = lane_index((N, LANES)) < N
    for j in range(BANDS // 2):
        first = by_band[pl.ds(64 * j, 32), :]
        second = by_band[pl.ds(64 * j + 32, 32), :]
        both = dot(table, jnp.concatenate([first, second], axis=1).astype(bf16))
        even, odd = both[:N], both[N:]
        even = jnp.where(low, even[:, :LANES], pltpu.roll(even[:, LANES:], N, 1))
        odd = jnp.where(low, pltpu.roll(odd[:, :LANES], N, 1), odd[:, LANES:])
        by_ky[pl.ds(j, N, stride=16), :] = even + odd
        by_ky[pl.ds(1024 + j, N, stride=16), :] = even - odd
    out_ref[...] = by_ky[...].astype(bf16).reshape(N, 32, LANES)


def spots_kernel(r_ref, e_ref, pc_ref, ps_ref, w_ref, out_ref, planes):
    planes[...] = r_ref[...].reshape(N * 32, LANES).astype(f32)
    table = e_ref[...]
    cos_z = jnp.concatenate([pc_ref[...]] * 2, axis=1)
    sin_z = jnp.concatenate([ps_ref[...]] * 2, axis=1)
    column = lane_index((2 * LANES, LANES))
    band = lax.broadcasted_iota(jnp.int32, (2 * LANES, LANES), 0) // N
    total = jnp.zeros((2 * SPOTS, LANES), f32)
    for j in range(BANDS // 4):
        first = planes[pl.ds(2 * j, LANES, stride=16), :]
        second = planes[pl.ds(2 * j + 1, LANES, stride=16), :]
        at_x = dot(table, jnp.concatenate([first, second], axis=1).astype(bf16))
        real, imag = at_x[:SPOTS], at_x[SPOTS:]
        real_z = real * cos_z + imag * sin_z
        imag_z = imag * cos_z - real * sin_z
        terms = jnp.concatenate([real_z, imag_z], axis=0).astype(bf16)
        ones = jnp.where(column == band + 4 * j, 1.0, 0.0).astype(bf16)
        total = total + dot(terms, ones)
    joined = total[:SPOTS] + pltpu.roll(total[SPOTS:], BANDS, 1)
    joined = joined + pltpu.roll(joined, N, 1)
    out_ref[:ROWS, :] = (joined[:ROWS] * w_ref[0:1, :]).astype(bf16)
    out_ref[ROWS:, :] = (joined[ROWS:] * w_ref[1:2, :]).astype(bf16)


def panel_kernel(a_ref, b_ref, out_ref, spread, columns):
    spread[...] = b_ref[...].reshape(N * 32, LANES).astype(f32)
    for j in range(8):
        for q in range(4):
            columns[j * N : (j + 1) * N, q * LANES : (q + 1) * LANES] = spread[
                pl.ds(q * 8 + j, N, stride=32), :
            ].astype(bf16)
    real_lane = lane_index((ROWS, LANES)) % N < BANDS
    upper, lower = [], []
    for q in range(4):
        rows = a_ref[q, :ROWS, :]
        wide = rows.astype(f32)
        turned = jnp.where(
            real_lane, pltpu.roll(wide, LANES - BANDS, 1), -pltpu.roll(wide, BANDS, 1)
        )
        upper.append(rows)
        lower.append(turned.astype(bf16))
    both = jnp.concatenate(
        [jnp.concatenate(upper, axis=1), jnp.concatenate(lower, axis=1)], axis=0
    )
    for h in range(2):
        part = lax.dot_general(
            both,
            columns[h * 256 : (h + 1) * 256, :],
            (((1,), (1,)), ((), ())),
            preferred_element_type=f32,
        )
        part = part * (1.0 / 16.0)
        out_ref[0, :, h * 256 : (h + 1) * 256] = part[:ROWS]
        out_ref[1, :, h * 256 : (h + 1) * 256] = part[ROWS:]


def call(kernel, shape, dtype, scratch, *args):
    vmem = pl.BlockSpec(memory_space=pltpu.VMEM)
    return pl.pallas_call(
        kernel,
        out_shape=jax.ShapeDtypeStruct(shape, dtype),
        in_specs=[vmem] * len(args),
        out_specs=vmem,
        scratch_shapes=scratch,
        compiler_params=pltpu.CompilerParams(vmem_limit_bytes=32 * 1024 * 1024),
    )(*args)


def turns(count):
    return jnp.cos((count % N).astype(f32) * (2.0 * math.pi / N)) / 8.0


def shards(
    valence, conduction, band_index, occ_valence, occ_conduction, gap_energy, row_map, col_map
):
    chosen = band_index[0]
    core = lax.axis_index("c")
    mine = chosen // valence.shape[0] == lax.axis_index(COL)
    own = lax.dynamic_index_in_dim(valence, chosen % valence.shape[0], 0, keepdims=False)
    own = jnp.where(mine, own, 0).astype(bf16).reshape(32, LANES)
    v = lax.psum(lax.psum(own, "zh"), "c")

    half = call(
        pair_y_kernel,
        (N, 32, LANES),
        bf16,
        [pltpu.VMEM((1024, LANES), f32), pltpu.VMEM((2048, LANES), f32)],
        v,
        conduction.reshape(BANDS, N * N),
        jnp.asarray(y_table()).astype(bf16),
    )
    block = lax.all_to_all(half, GA, 0, 0, tiled=True)

    spots = jnp.concatenate([row_map, col_map])[:, None]
    kx, kz = spots // N, spots % N
    lane = lane_index((1, LANES))
    x, imag = lane // 2, lane % 2
    x_table = jnp.concatenate(
        [turns(kx * x + (N - 16) * imag), turns(kx * x + 16 * (1 - imag))], axis=0
    ).astype(bf16)
    z = lane % N
    cos_z, sin_z = turns(kz * z), turns(kz * z + N - 16)
    weight = 2.0 * (occ_conduction - occ_valence[chosen]).astype(f32) / gap_energy
    here = (lane // N == core).astype(f32)
    scales = jnp.concatenate([jnp.tile(weight, 4)[None] * here, here], axis=0)
    values = call(
        spots_kernel,
        (SPOTS, LANES),
        bf16,
        [pltpu.VMEM((2048, LANES), f32)],
        block,
        x_table,
        cos_z,
        sin_z,
        scales,
    )

    values = lax.psum(values, "c")
    rows = jnp.broadcast_to(values[None, :ROWS], (4, ROWS, LANES))
    cols = values[ROWS:].reshape(4, 16, LANES)
    bands = lax.all_to_all(jnp.concatenate([rows, cols], axis=1), "zh", 0, 0, tiled=True)
    own_cols = lax.dynamic_slice_in_dim(bands, ROWS + 8 * core, 8, axis=1).reshape(32, LANES)
    columns = lax.all_to_all(
        jnp.broadcast_to(own_cols[None], (N, 32, LANES)), GA, 0, 0, tiled=True
    )
    return call(
        panel_kernel,
        (2, ROWS, 8 * N),
        f32,
        [pltpu.VMEM((2048, LANES), f32), pltpu.VMEM((8 * N, 4 * LANES), bf16)],
        bands,
        columns,
    )


def solution(mesh):
    fine = Mesh(mesh.devices.reshape(4, 4, 4, 4, 2), ("y", "zl", "x", "zh", "c"))
    return jax.shard_map(
        shards,
        mesh=fine,
        in_specs=(
            P(COL, GA, None),
            P(COL, GA, None),
            P(),
            P(),
            P(COL),
            P(COL),
            P(GA),
            P(GA),
        ),
        out_specs=P(None, GA, COL),
        check_vma=False,
    )
```

time: 423 us -> 109 us (0.26)
  waiting for transfers between devices: 174 us -> 23.9 us
  blocking collectives: 183 us -> 52.7 us
  local copies, waits for them, and re-layouts: 28.2 us -> 5.63 us
  between operations: 15.1 us -> 0.86 us
  matrix products: 7.54 us -> 0 us
  starting transfers between devices: 9.16 us -> 15.4 us
  Pallas kernels: 0 us -> 5.21 us
    unnamed x2 -> x0, waiting for transfers between devices: 162 us -> none
    all_gather x1 -> x0, blocking collectives: 159 us -> none  [shards(): piece = lax.all_gather(columns, 'ga', axis=0, tiled=True)]
    all_to_all x0 -> x1, blocking collectives: none -> 22.5 us  [shards(): lax.all_to_all(jnp.broadcast_to(own_cols[None], (N, 32, LANES)), GA, 0, 0...]
    all_to_all x1 -> x2, waiting for transfers between devices: 11.7 us -> 23.9 us  [the longest x1 12.1 us: shards(): lax.all_to_all(jnp.concatenate([rows, cols], axis=1), 'zh', 0, 0, tiled=T...]
    dot_general x13 -> x0, matrix products: 7.54 us -> none  [the longest x2 1.3 us: rotate(): jnp.einsum(form, sin_table, imag_part, precision=middle)]
    convert_element_type x3 -> x0, local copies, waits for them, and re-layouts: 7.28 us -> none  [shards(): partial_value.astype(jnp.bfloat16)]
    another operation x3 -> x2, local copies, waits for them, and re-layouts: 7.14 us -> 0.09 us  [shards(): scales = jnp.concatenate([jnp.tile(weight, 4)[None] * here, here], axis=0)]
    all_to_all x1 -> x2, starting transfers between devices: 8.94 us -> 15.4 us  [the longest x1 9.02 us: shards(): block = lax.all_to_all(half, GA, 0, 0, tiled=True)]
  transfers between devices with their start and end apart: 2 -> 2, of which waited for: 2 -> 2; matrix products, arithmetic and copies ran while one was open for 1% -> 3% of each run, Pallas kernels for 0% -> 0%
where the time goes in v1:
time: 109 us; the launch traced here: 108 us
  blocking collectives  52.7 us (48%)
  waiting for transfers between devices  23.9 us (22%)
  starting transfers between devices  15.4 us (14%)
  local copies, waits for them, and re-layouts  5.63 us (5%)
  Pallas kernels  5.21 us (5%)
  other arithmetic  3.79 us (3%)
    psum x2, blocking collectives, shards(): v = lax.psum(lax.psum(own, 'zh'), 'c')  25 us
    all_to_all x1, blocking collectives, shards(): lax.all_to_all(jnp.broadcast_to(own_cols[None], (N, 32, LANES)), GA, 0, 0...  22.5 us
    all_to_all x1, waiting for transfers between devices, shards(): lax.all_to_all(jnp.concatenate([rows, cols], axis=1), 'zh', 0, 0, tiled=T...  12.1 us
    all_to_all x1, waiting for transfers between devices, shards(): block = lax.all_to_all(half, GA, 0, 0, tiled=True)  11.7 us
    all_to_all x1, starting transfers between devices, shards(): block = lax.all_to_all(half, GA, 0, 0, tiled=True)  9.02 us
    all_to_all x1, starting transfers between devices, shards(): lax.all_to_all(jnp.concatenate([rows, cols], axis=1), 'zh', 0, 0, tiled=T...  6.36 us
    psum x1, blocking collectives, shards(): values = lax.psum(values, 'c')  5.25 us
    pallas_call x3, Pallas kernels, call(): pl.pallas_call(kernel, out_shape=jax.ShapeDtypeStruct(shape, dtype), in_s...  5.21 us
  transfers between devices with their start and end apart: 2, of which 2 were waited for; matrix products, arithmetic and copies ran while one was open for 3% of the time, Pallas kernels for 0%

profile of v1, /device:TPU:1, one launch (start us, length us, event | category | flops | bytes accessed | tf_op | source)
XLA Modules:
  0.0 107.5 jit_solution(4286653124073046978)
XLA Ops:
  0.7 0.0 copy-start.1
  0.7 0.9 fusion.27
  1.6 20.2 %psum.21 = bf16[32,128]{1,0:T(8,128)(2,1)S(1)} all-reduce(bf16[32,128]{1,0:T(8,128)(2,1)S(1)} %bitcast.15), channel_id=1, replica_groups=mesh['y'=4,'zl'=4,'x'=4,'zh'=4,'c'=2] {'zh'}, use_global_device_ids=true, to_apply=%region_0.1 | all-reduce | flops 4096 | bytes 16384 | tf_op jit(solution)/shard_map/psum | solution.py:142
  21.8 4.9 %psum.22.v_ref = bf16[32,128]{1,0:T(8,128)(2,1)S(1)} all-reduce(bf16[32,128]{1,0:T(8,128)(2,1)S(1)} %psum.21), channel_id=1, replica_groups=mesh['y'=4,'zl'=4,'x'=4,'zh'=4,'c'=2] {'c'}, use_global_device_ids=true, to_apply=%region_1.2 | all-reduce | flops 4096 | bytes 16384 | tf_op jit(solution)/shard_map/psum | solution.py:142
  26.7 0.0 copy-done.1
  26.7 0.0 copy-start
  26.7 0.9 copy-done
  27.6 1.9 %shard_map.91 = bf16[64,32,128]{2,1,0:T(8,128)(2,1)} custom-call(bf16[32,128]{1,0:T(8,128)(2,1)S(1)} %psum.22.v_ref, bf16[32,4096]{1,0:T(8,128)(2,1)S(1)} %bitcast.13, bf16[128,32]{1,0:T(8,128)(2,1)S(1)} %copy-done.1), custom_call_target="tpu_custom_call" | custom-call | tf_op jit(solution)/shard_map/pallas_call | solution.py:120
  29.5 9.0 %all-to-all-start = ((bf16[64,32,128]{2,1,0:T(8,128)(2,1)}), bf16[64,32,128]{2,1,0:T(8,128)(2,1)S(1)}, u32[]{:S(2)}, u32[]{:S(2)}) async-start(bf16[64,32,128]{2,1,0:T(8,128)(2,1)} %shard_map.91), calls=%async_computation | async-start | bytes 1048576 | tf_op jit(solution)/shard_map/all_to_all | solution.py:153
  38.5 0.0 copy-start.5
  38.5 0.6 copy-done.5
  39.2 0.6 dynamic_slice.11
  39.8 0.0 copy-start.3
  39.8 0.0 copy-start.4
  39.8 0.7 copy-done.3
  40.4 0.0 copy-done.4
  40.4 0.6 multiply_divide_fusion
  41.0 0.1 broadcast_in_dim_tile.3
  41.1 0.0 copy-start.6
  41.1 0.6 copy-done.6
  41.8 0.0 copy-start.7
  41.8 0.6 copy-done.7
  42.5 0.8 fusion.10
  43.3 0.8 fusion.24
  44.1 11.7 %all-to-all-done.r_ref = bf16[64,32,128]{2,1,0:T(8,128)(2,1)S(1)} async-done(((bf16[64,32,128]{2,1,0:T(8,128)(2,1)}), bf16[64,32,128]{2,1,0:T(8,128)(2,1)S(1)}, u32[]{:S(2)}, u32[]{:S(2)}) %all-to-all-start) | async-done | bytes 524320 | tf_op jit(solution)/shard_map/all_to_all | solution.py:153
  55.8 1.6 %shard_map.92 = bf16[192,128]{1,0:T(8,128)(2,1)S(1)} custom-call(bf16[64,32,128]{2,1,0:T(8,128)(2,1)S(1)} %all-to-all-done.r_ref, bf16[384,128]{1,0:T(8,128)(2,1)S(1)} %pad_maximum_fusion.1.e_ref, f32[192,128]{1,0:T(8,128)S(1)} %get-tuple-element.6.pc_ref, f32[192,128]{1,0:T(8,128)S(1)} %get-tuple-element.5.ps_ref, f32[2,128]{1,0:T(2,128)S(1)} %pad_maximum_fusion.2.w_ref), custom_call_target="tpu_custom_call" | custom-call | tf_op jit(solution)/shard_map/pallas_call | solution.py:120
  57.5 5.2 %psum.23 = bf16[192,128]{1,0:T(8,128)(2,1)S(1)} all-reduce(bf16[192,128]{1,0:T(8,128)(2,1)S(1)} %shard_map.92), channel_id=1, replica_groups=mesh['y'=4,'zl'=4,'x'=4,'zh'=4,'c'=2] {'c'}, use_global_device_ids=true, to_apply=%region_2.3 | all-reduce | flops 24576 | bytes 98304 | tf_op jit(solution)/shard_map/psum | solution.py:179
  62.7 0.0 copy-start.2
  62.7 0.6 copy-done.2
  63.3 0.0 slice-start
  63.4 0.7 slice-done
  64.1 0.7 pad_maximum_fusion
  64.7 6.4 %all-to-all-start.1 = ((bf16[4,144,128]{2,1,0:T(8,128)(2,1)}), bf16[4,144,128]{2,1,0:T(8,128)(2,1)S(1)}, u32[]{:S(2)}, u32[]{:S(2)}) async-start(bf16[4,144,128]{2,1,0:T(8,128)(2,1)} %pad_maximum_fusion), calls=%async_computation.1 | async-start | bytes 294912 | tf_op jit(solution)/shard_map/all_to_all | solution.py:182
  71.1 12.1 %all-to-all-done.1.a_ref = bf16[4,144,128]{2,1,0:T(8,128)(2,1)S(1)} async-done(((bf16[4,144,128]{2,1,0:T(8,128)(2,1)}), bf16[4,144,128]{2,1,0:T(8,128)(2,1)S(1)}, u32[]{:S(2)}, u32[]{:S(2)}) %all-to-all-start.1) | async-done | bytes 147488 | tf_op jit(solution)/shard_map/all_to_all | solution.py:182
  83.2 0.1 broadcast_in_dim.21
  83.3 22.5 %all_to_all.15.b_ref = bf16[64,32,128]{2,1,0:T(8,128)(2,1)S(1)} all-to-all(bf16[64,32,128]{2,1,0:T(8,128)(2,1)S(1)} %broadcast_in_dim.21), channel_id=1, replica_groups=mesh['y'=4,'zl'=4,'x'=4,'zh'=4,'c'=2] {'y','zl','x'}, dimensions={0} | all-to-all | bytes 1048576 | tf_op jit(solution)/shard_map/all_to_all | solution.py:184
  105.8 1.7 %shard_map.93 = f32[2,128,512]{2,1,0:T(8,128)} custom-call(bf16[4,144,128]{2,1,0:T(8,128)(2,1)S(1)} %all-to-all-done.1.a_ref, bf16[64,32,128]{2,1,0:T(8,128)(2,1)S(1)} %all_to_all.15.b_ref), custom_call_target="tpu_custom_call" | custom-call | tf_op jit(solution)/shard_map/pallas_call | solution.py:120
  (14 shorter events, 0.1 us)
Async XLA Ops:
  0.7 26.0 %copy-start.1 = (bf16[128,32]{1,0:T(8,128)(2,1)S(1)}, bf16[128,32]{1,0:T(8,128)(2,1)}, u32[]{:S(2)}) copy-start(bf16[128,32]{1,0:T(8,128)(2,1)} %constant.164.e_ref) | copy-start | bytes 24580
  26.7 1.0 copy-start
  29.5 26.4 %all-to-all-start = ((bf16[64,32,128]{2,1,0:T(8,128)(2,1)}), bf16[64,32,128]{2,1,0:T(8,128)(2,1)S(1)}, u32[]{:S(2)}, u32[]{:S(2)}) async-start(bf16[64,32,128]{2,1,0:T(8,128)(2,1)} %shard_map.91), calls=%async_computation | async-start | bytes 1048576 | tf_op jit(solution)/shard_map/all_to_all | solution.py:153
  38.5 0.7 copy-start.5
  39.8 0.7 copy-start.3
  39.8 0.7 copy-start.4
  41.1 0.7 copy-start.6
  41.8 0.7 copy-start.7
  62.7 0.6 copy-start.2
  63.3 0.7 slice-start
  64.7 18.5 %all-to-all-start.1 = ((bf16[4,144,128]{2,1,0:T(8,128)(2,1)}), bf16[4,144,128]{2,1,0:T(8,128)(2,1)S(1)}, u32[]{:S(2)}, u32[]{:S(2)}) async-start(bf16[4,144,128]{2,1,0:T(8,128)(2,1)} %pad_maximum_fusion), calls=%async_computation.1 | async-start | bytes 294912 | tf_op jit(solution)/shard_map/all_to_all | solution.py:182

commit v2 on v1

--- a/solution.py
+++ b/solution.py
@@ -78,9 +78,13 @@
         ones = jnp.where(column == band + 4 * j, 1.0, 0.0).astype(bf16)
         total = total + dot(terms, ones)
     joined = total[:SPOTS] + pltpu.roll(total[SPOTS:], BANDS, 1)
-    joined = joined + pltpu.roll(joined, N, 1)
-    out_ref[:ROWS, :] = (joined[:ROWS] * w_ref[0:1, :]).astype(bf16)
-    out_ref[ROWS:, :] = (joined[ROWS:] * w_ref[1:2, :]).astype(bf16)
+    rows = joined[:ROWS] * w_ref[0:1, :]
+    rows = (rows[:N] + pltpu.roll(rows[N:], N, 1)).astype(bf16)
+    cols = joined[ROWS:]
+    cols = ((cols + pltpu.roll(cols, N, 1)) * w_ref[1:2, :]).astype(bf16)
+    for q in range(4):
+        out_ref[q, :N, :] = rows
+        out_ref[q, N:, :] = cols[16 * q : 16 * q + 16]
 
 
 def panel_kernel(a_ref, b_ref, out_ref, spread, columns):
@@ -92,13 +96,17 @@
             ].astype(bf16)
     real_lane = lane_index((ROWS, LANES)) % N < BANDS
     upper, lower = [], []
+    low = lane_index((N, LANES)) < N
     for q in range(4):
-        rows = a_ref[q, :ROWS, :]
-        wide = rows.astype(f32)
+        core0 = a_ref[0, q, :N, :].astype(f32)
+        core1 = a_ref[1, q, :N, :].astype(f32)
+        head = jnp.where(low, core0, pltpu.roll(core1, N, 1))
+        tail = jnp.where(low, pltpu.roll(core0, N, 1), core1)
+        rows = jnp.concatenate([head, tail], axis=0)
         turned = jnp.where(
-            real_lane, pltpu.roll(wide, LANES - BANDS, 1), -pltpu.roll(wide, BANDS, 1)
+            real_lane, pltpu.roll(rows, LANES - BANDS, 1), -pltpu.roll(rows, BANDS, 1)
         )
-        upper.append(rows)
+        upper.append(rows.astype(bf16))
         lower.append(turned.astype(bf16))
     both = jnp.concatenate(
         [jnp.concatenate(upper, axis=1), jnp.concatenate(lower, axis=1)], axis=0
@@ -163,10 +171,10 @@
     cos_z, sin_z = turns(kz * z), turns(kz * z + N - 16)
     weight = 2.0 * (occ_conduction - occ_valence[chosen]).astype(f32) / gap_energy
     here = (lane // N == core).astype(f32)
-    scales = jnp.concatenate([jnp.tile(weight, 4)[None] * here, here], axis=0)
+    scales = jnp.concatenate([jnp.tile(weight, 4)[None], here], axis=0)
     values = call(
         spots_kernel,
-        (SPOTS, LANES),
+        (4, N + 16, LANES),
         bf16,
         [pltpu.VMEM((2048, LANES), f32)],
         block,
@@ -176,11 +184,10 @@
         scales,
     )
 
-    values = lax.psum(values, "c")
-    rows = jnp.broadcast_to(values[None, :ROWS], (4, ROWS, LANES))
-    cols = values[ROWS:].reshape(4, 16, LANES)
-    bands = lax.all_to_all(jnp.concatenate([rows, cols], axis=1), "zh", 0, 0, tiled=True)
-    own_cols = lax.dynamic_slice_in_dim(bands, ROWS + 8 * core, 8, axis=1).reshape(32, LANES)
+    values = lax.all_to_all(values, "zh", 0, 0, tiled=True)
+    bands = lax.all_gather(values, "c")
+    own_cols = lax.dynamic_slice_in_dim(bands, N + 8 * core, 8, axis=2)
+    own_cols = (own_cols[0] + own_cols[1]).reshape(32, LANES)
     columns = lax.all_to_all(
         jnp.broadcast_to(own_cols[None], (N, 32, LANES)), GA, 0, 0, tiled=True
     )

time: 109 us -> 106 us (0.972)
  local copies, waits for them, and re-layouts: 5.63 us -> 4.31 us
    psum x1 -> x0, blocking collectives: 5.25 us -> none  [shards(): values = lax.psum(values, 'c')]
    all_gather x0 -> x1, blocking collectives: none -> 5.11 us  [shards(): bands = lax.all_gather(values, 'c')]
    unnamed x17 -> x15, local copies, waits for them, and re-layouts: 4.17 us -> 3.56 us
where the time goes in v2:
time: 106 us; the launch traced here: 105 us
  blocking collectives  52.3 us (49%)
  waiting for transfers between devices  23.5 us (22%)
  starting transfers between devices  15.4 us (15%)
  Pallas kernels  5.85 us (6%)
  local copies, waits for them, and re-layouts  4.31 us (4%)
  other arithmetic  3.12 us (3%)
    psum x2, blocking collectives, shards(): v = lax.psum(lax.psum(own, 'zh'), 'c')  25 us
    all_to_all x1, blocking collectives, shards(): lax.all_to_all(jnp.broadcast_to(own_cols[None], (N, 32, LANES)), GA, 0, 0...  22.2 us
    all_to_all x1, waiting for transfers between devices, shards(): values = lax.all_to_all(values, 'zh', 0, 0, tiled=True)  11.8 us
    all_to_all x1, waiting for transfers between devices, shards(): block = lax.all_to_all(half, GA, 0, 0, tiled=True)  11.8 us
    all_to_all x1, starting transfers between devices, shards(): block = lax.all_to_all(half, GA, 0, 0, tiled=True)  9.02 us
    all_to_all x1, starting transfers between devices, shards(): values = lax.all_to_all(values, 'zh', 0, 0, tiled=True)  6.36 us
    pallas_call x3, Pallas kernels, call(): pl.pallas_call(kernel, out_shape=jax.ShapeDtypeStruct(shape, dtype), in_s...  5.85 us
    all_gather x1, blocking collectives, shards(): bands = lax.all_gather(values, 'c')  5.11 us
  transfers between devices with their start and end apart: 2, of which 2 were waited for; matrix products, arithmetic and copies ran while one was open for 3% of the time, Pallas kernels for 0%

profile of v2, /device:TPU:1, one launch (start us, length us, event | category | flops | bytes accessed | tf_op | source)
XLA Modules:
  0.0 105.3 jit_solution(8622001955453821943)
XLA Ops:
  0.7 0.0 copy-start.1
  0.7 0.9 fusion.27
  1.6 20.2 %psum.14 = bf16[32,128]{1,0:T(8,128)(2,1)S(1)} all-reduce(bf16[32,128]{1,0:T(8,128)(2,1)S(1)} %bitcast.16), channel_id=1, replica_groups=mesh['y'=4,'zl'=4,'x'=4,'zh'=4,'c'=2] {'zh'}, use_global_device_ids=true, to_apply=%region_0.1 | all-reduce | flops 4096 | bytes 16384 | tf_op jit(solution)/shard_map/psum | solution.py:150
  21.8 4.9 %psum.15.v_ref = bf16[32,128]{1,0:T(8,128)(2,1)S(1)} all-reduce(bf16[32,128]{1,0:T(8,128)(2,1)S(1)} %psum.14), channel_id=1, replica_groups=mesh['y'=4,'zl'=4,'x'=4,'zh'=4,'c'=2] {'c'}, use_global_device_ids=true, to_apply=%region_1.2 | all-reduce | flops 4096 | bytes 16384 | tf_op jit(solution)/shard_map/psum | solution.py:150
  26.7 0.0 copy-done.1
  26.7 0.0 copy-start
  26.7 0.9 copy-done
  27.6 1.9 %shard_map.91 = bf16[64,32,128]{2,1,0:T(8,128)(2,1)} custom-call(bf16[32,128]{1,0:T(8,128)(2,1)S(1)} %psum.15.v_ref, bf16[32,4096]{1,0:T(8,128)(2,1)S(1)} %bitcast.15, bf16[128,32]{1,0:T(8,128)(2,1)S(1)} %copy-done.1), custom_call_target="tpu_custom_call" | custom-call | tf_op jit(solution)/shard_map/pallas_call | solution.py:128
  29.5 9.0 %all-to-all-start = ((bf16[64,32,128]{2,1,0:T(8,128)(2,1)}), bf16[64,32,128]{2,1,0:T(8,128)(2,1)S(1)}, u32[]{:S(2)}, u32[]{:S(2)}) async-start(bf16[64,32,128]{2,1,0:T(8,128)(2,1)} %shard_map.91), calls=%async_computation | async-start | bytes 1048576 | tf_op jit(solution)/shard_map/all_to_all | solution.py:161
  38.5 0.0 copy-start.4
  38.5 0.6 copy-done.4
  39.2 0.6 dynamic_slice.11
  39.8 0.0 copy-start.2
  39.8 0.0 copy-start.3
  39.8 0.7 copy-done.2
  40.4 0.0 copy-done.3
  40.4 0.6 multiply_divide_fusion
  41.0 0.1 broadcast_in_dim_tile.3
  41.1 0.0 copy-start.5
  41.1 0.6 copy-done.5
  41.8 0.0 copy-start.6
  41.8 0.6 copy-done.6
  42.5 0.8 fusion.10
  43.3 0.8 fusion.24
  44.1 11.8 %all-to-all-done.r_ref = bf16[64,32,128]{2,1,0:T(8,128)(2,1)S(1)} async-done(((bf16[64,32,128]{2,1,0:T(8,128)(2,1)}), bf16[64,32,128]{2,1,0:T(8,128)(2,1)S(1)}, u32[]{:S(2)}, u32[]{:S(2)}) %all-to-all-start) | async-done | bytes 524320 | tf_op jit(solution)/shard_map/all_to_all | solution.py:161
  55.8 2.2 %shard_map.92 = bf16[4,80,128]{2,1,0:T(8,128)(2,1)} custom-call(bf16[64,32,128]{2,1,0:T(8,128)(2,1)S(1)} %all-to-all-done.r_ref, bf16[384,128]{1,0:T(8,128)(2,1)S(1)} %pad_maximum_fusion.e_ref, f32[192,128]{1,0:T(8,128)S(1)} %get-tuple-element.6.pc_ref, f32[192,128]{1,0:T(8,128)S(1)} %get-tuple-element.5.ps_ref, f32[2,128]{1,0:T(2,128)S(1)} %pad_maximum_fusion.1.w_ref), custom_call_target="tpu_custom_call" | custom-call | tf_op jit(solution)/shard_map/pallas_call | solution.py:128
  58.1 6.4 %all-to-all-start.1 = ((bf16[4,80,128]{2,1,0:T(8,128)(2,1)}), bf16[4,80,128]{2,1,0:T(8,128)(2,1)S(1)}, u32[]{:S(2)}, u32[]{:S(2)}) async-start(bf16[4,80,128]{2,1,0:T(8,128)(2,1)} %shard_map.92), calls=%async_computation.1 | async-start | bytes 163840 | tf_op jit(solution)/shard_map/all_to_all | solution.py:187
  64.5 11.8 %all-to-all-done.1 = bf16[4,80,128]{2,1,0:T(8,128)(2,1)S(1)} async-done(((bf16[4,80,128]{2,1,0:T(8,128)(2,1)}), bf16[4,80,128]{2,1,0:T(8,128)(2,1)S(1)}, u32[]{:S(2)}, u32[]{:S(2)}) %all-to-all-start.1) | async-done | bytes 81952 | tf_op jit(solution)/shard_map/all_to_all | solution.py:187
  76.2 5.1 %all-gather = bf16[8,80,128]{2,1,0:T(8,128)(2,1)S(1)} all-gather(bf16[4,80,128]{2,1,0:T(8,128)(2,1)S(1)} %all-to-all-done.1), channel_id=2, replica_groups=mesh['y'=4,'zl'=4,'x'=4,'zh'=4,'c'=2] {'c'}, dimensions={0}, use_global_device_ids=true | all-gather | bytes 245760 | tf_op jit(solution)/shard_map/all_gather | solution.py:188
  81.3 0.1 broadcast_in_dim.11
  81.4 22.2 %all_to_all.15.b_ref = bf16[64,32,128]{2,1,0:T(8,128)(2,1)S(1)} all-to-all(bf16[64,32,128]{2,1,0:T(8,128)(2,1)S(1)} %broadcast_in_dim.11), channel_id=1, replica_groups=mesh['y'=4,'zl'=4,'x'=4,'zh'=4,'c'=2] {'y','zl','x'}, dimensions={0} | all-to-all | bytes 1048576 | tf_op jit(solution)/shard_map/all_to_all | solution.py:191
  103.6 1.7 %shard_map.93 = f32[2,128,512]{2,1,0:T(8,128)} custom-call(bf16[2,4,80,128]{3,2,1,0:T(8,128)(2,1)S(1)} %bitcast.14, bf16[64,32,128]{2,1,0:T(8,128)(2,1)S(1)} %all_to_all.15.b_ref), custom_call_target="tpu_custom_call" | custom-call | tf_op jit(solution)/shard_map/pallas_call | solution.py:128
  (11 shorter events, 0.1 us)
Async XLA Ops:
  0.7 26.0 %copy-start.1 = (bf16[128,32]{1,0:T(8,128)(2,1)S(1)}, bf16[128,32]{1,0:T(8,128)(2,1)}, u32[]{:S(2)}) copy-start(bf16[128,32]{1,0:T(8,128)(2,1)} %constant.160.e_ref) | copy-start | bytes 24580
  26.7 1.0 copy-start
  29.5 26.4 %all-to-all-start = ((bf16[64,32,128]{2,1,0:T(8,128)(2,1)}), bf16[64,32,128]{2,1,0:T(8,128)(2,1)S(1)}, u32[]{:S(2)}, u32[]{:S(2)}) async-start(bf16[64,32,128]{2,1,0:T(8,128)(2,1)} %shard_map.91), calls=%async_computation | async-start | bytes 1048576 | tf_op jit(solution)/shard_map/all_to_all | solution.py:161
  38.5 0.7 copy-start.4
  39.8 0.7 copy-start.2
  39.8 0.7 copy-start.3
  41.1 0.7 copy-start.5
  41.8 0.7 copy-start.6
  58.1 18.1 %all-to-all-start.1 = ((bf16[4,80,128]{2,1,0:T(8,128)(2,1)}), bf16[4,80,128]{2,1,0:T(8,128)(2,1)S(1)}, u32[]{:S(2)}, u32[]{:S(2)}) async-start(bf16[4,80,128]{2,1,0:T(8,128)(2,1)} %shard_map.92), calls=%async_computation.1 | async-start | bytes 163840 | tf_op jit(solution)/shard_map/all_to_all | solution.py:187

commit v3 on v2

--- a/solution.py
+++ b/solution.py
@@ -15,6 +15,8 @@
 COLS = 64
 SPOTS = ROWS + COLS
 LANES = 128
+WIDE = 40
+NARROW = 24
 GA = ("y", "zl", "x")
 COL = ("zh", "c")
 
@@ -44,19 +46,22 @@
     for i in range(N // 2):
         bands = c_ref[:, i * LANES : (i + 1) * LANES].astype(f32)
         pair = (bands * v[i : i + 1, :]).astype(bf16).astype(f32)
-        by_band[pl.ds(i, BANDS, stride=N // 2), :] = pair
+        by_band[pl.ds(i, BANDS, stride=WIDE), :] = pair
     table = e_ref[...]
     low = lane_index((N, LANES)) < N
     for j in range(BANDS // 2):
-        first = by_band[pl.ds(64 * j, 32), :]
-        second = by_band[pl.ds(64 * j + 32, 32), :]
+        first = by_band[pl.ds(2 * WIDE * j, 32), :]
+        second = by_band[pl.ds(2 * WIDE * j + WIDE, 32), :]
         both = dot(table, jnp.concatenate([first, second], axis=1).astype(bf16))
         even, odd = both[:N], both[N:]
         even = jnp.where(low, even[:, :LANES], pltpu.roll(even[:, LANES:], N, 1))
         odd = jnp.where(low, pltpu.roll(odd[:, :LANES], N, 1), odd[:, LANES:])
-        by_ky[pl.ds(j, N, stride=16), :] = even + odd
-        by_ky[pl.ds(1024 + j, N, stride=16), :] = even - odd
-    out_ref[...] = by_ky[...].astype(bf16).reshape(N, 32, LANES)
+        by_ky[pl.ds(j, N, stride=NARROW), :] = even + odd
+        by_ky[pl.ds(N * NARROW + j, N, stride=NARROW), :] = even - odd
+    for ky in range(N):
+        real = by_ky[pl.ds(2 * ky * NARROW, 16), :]
+        imag = by_ky[pl.ds((2 * ky + 1) * NARROW, 16), :]
+        out_ref[ky] = jnp.concatenate([real, imag], axis=0).astype(bf16)
 
 
 def spots_kernel(r_ref, e_ref, pc_ref, ps_ref, w_ref, out_ref, planes):
@@ -87,13 +92,12 @@
         out_ref[q, N:, :] = cols[16 * q : 16 * q + 16]
 
 
-def panel_kernel(a_ref, b_ref, out_ref, spread, columns):
-    spread[...] = b_ref[...].reshape(N * 32, LANES).astype(f32)
-    for j in range(8):
-        for q in range(4):
-            columns[j * N : (j + 1) * N, q * LANES : (q + 1) * LANES] = spread[
-                pl.ds(q * 8 + j, N, stride=32), :
-            ].astype(bf16)
+def panel_kernel(a_ref, b_ref, out_ref, spread):
+    for y in range(4):
+        for x in range(4):
+            for zl in range(4):
+                at = (16 * y + 4 * zl + x) * WIDE
+                spread[pl.ds(at, 32), :] = b_ref[4 * y + x, 32 * zl : 32 * zl + 32, :].astype(f32)
     real_lane = lane_index((ROWS, LANES)) % N < BANDS
     upper, lower = [], []
     low = lane_index((N, LANES)) < N
@@ -112,9 +116,13 @@
         [jnp.concatenate(upper, axis=1), jnp.concatenate(lower, axis=1)], axis=0
     )
     for h in range(2):
+        columns = []
+        for j in range(4 * h, 4 * h + 4):
+            parts = [spread[pl.ds(8 * q + j, N, stride=WIDE), :] for q in range(4)]
+            columns.append(jnp.concatenate(parts, axis=1))
         part = lax.dot_general(
             both,
-            columns[h * 256 : (h + 1) * 256, :],
+            jnp.concatenate(columns, axis=0).astype(bf16),
             (((1,), (1,)), ((), ())),
             preferred_element_type=f32,
         )
@@ -147,13 +155,13 @@
     mine = chosen // valence.shape[0] == lax.axis_index(COL)
     own = lax.dynamic_index_in_dim(valence, chosen % valence.shape[0], 0, keepdims=False)
     own = jnp.where(mine, own, 0).astype(bf16).reshape(32, LANES)
-    v = lax.psum(lax.psum(own, "zh"), "c")
+    v = lax.psum(lax.psum(own, "c"), "zh")
 
     half = call(
         pair_y_kernel,
         (N, 32, LANES),
         bf16,
-        [pltpu.VMEM((1024, LANES), f32), pltpu.VMEM((2048, LANES), f32)],
+        [pltpu.VMEM((BANDS * WIDE, LANES), f32), pltpu.VMEM((2 * N * NARROW, LANES), f32)],
         v,
         conduction.reshape(BANDS, N * N),
         jnp.asarray(y_table()).astype(bf16),
@@ -186,16 +194,18 @@
 
     values = lax.all_to_all(values, "zh", 0, 0, tiled=True)
     bands = lax.all_gather(values, "c")
-    own_cols = lax.dynamic_slice_in_dim(bands, N + 8 * core, 8, axis=2)
-    own_cols = (own_cols[0] + own_cols[1]).reshape(32, LANES)
+    cols = values[:, N:, :].reshape(4, 2, 8, LANES).transpose(1, 0, 2, 3)
+    cols = jnp.broadcast_to(cols[None], (4, 2, 4, 8, LANES)).reshape(8, 32, LANES)
+    cols = lax.all_to_all(cols, ("zl", "c"), 0, 0, tiled=True).reshape(4, 2, 32, LANES)
+    cols = (cols[:, 0] + cols[:, 1]).reshape(1, ROWS, LANES)
     columns = lax.all_to_all(
-        jnp.broadcast_to(own_cols[None], (N, 32, LANES)), GA, 0, 0, tiled=True
+        jnp.broadcast_to(cols, (16, ROWS, LANES)), ("y", "x"), 0, 0, tiled=True
     )
     return call(
         panel_kernel,
         (2, ROWS, 8 * N),
         f32,
-        [pltpu.VMEM((2048, LANES), f32), pltpu.VMEM((8 * N, 4 * LANES), bf16)],
+        [pltpu.VMEM((N * WIDE, LANES), f32)],
         bands,
         columns,
     )

time: 106 us -> 101 us (0.953)
  waiting for transfers between devices: 23.5 us -> 18.4 us
  blocking collectives: 52.3 us -> 55.4 us
  starting transfers between devices: 15.4 us -> 12.6 us
  Pallas kernels: 5.85 us -> 4.32 us
    all_to_all x1 -> x2, blocking collectives: 22.2 us -> 29.9 us  [the longest x1 18.1 us: shards(): values = lax.all_to_all(values, 'zh', 0, 0, tiled=True)]
    all_to_all x1, waiting for transfers between devices: 11.8 us -> 8.03 us  [shards(): lax.all_to_all(jnp.broadcast_to(cols, (16, ROWS, LANES)), ('y', 'x'), 0,...]
    all_to_all x1, starting transfers between devices: 6.36 us -> 3.57 us  [shards(): lax.all_to_all(jnp.broadcast_to(cols, (16, ROWS, LANES)), ('y', 'x'), 0,...]
    all_gather x1, blocking collectives: 5.11 us -> 2.51 us  [shards(): bands = lax.all_gather(values, 'c')]
    psum x2, blocking collectives: 25 us -> 23 us  [shards(): v = lax.psum(lax.psum(own, 'c'), 'zh')]
    pallas_call x3, Pallas kernels: 5.85 us -> 4.32 us  [call(): pl.pallas_call(kernel, out_shape=jax.ShapeDtypeStruct(shape, dtype), in_s...]
    all_to_all x1, waiting for transfers between devices: 11.8 us -> 10.4 us  [shards(): block = lax.all_to_all(half, GA, 0, 0, tiled=True)]
where the time goes in v3:
time: 101 us; the launch traced here: 100 us
  blocking collectives  55.4 us (55%)
  waiting for transfers between devices  18.4 us (18%)
  starting transfers between devices  12.6 us (12%)
  local copies, waits for them, and re-layouts  5.24 us (5%)
  Pallas kernels  4.32 us (4%)
  other arithmetic  3.25 us (3%)
    psum x2, blocking collectives, shards(): v = lax.psum(lax.psum(own, 'c'), 'zh')  23 us
    all_to_all x1, blocking collectives, shards(): values = lax.all_to_all(values, 'zh', 0, 0, tiled=True)  18.1 us
    all_to_all x1, blocking collectives, shards(): lax.all_to_all(cols, ('zl', 'c'), 0, 0, tiled=True).reshape(4, 2, 32, LANES)  11.7 us
    all_to_all x1, waiting for transfers between devices, shards(): block = lax.all_to_all(half, GA, 0, 0, tiled=True)  10.4 us
    all_to_all x1, starting transfers between devices, shards(): block = lax.all_to_all(half, GA, 0, 0, tiled=True)  9.01 us
    all_to_all x1, waiting for transfers between devices, shards(): lax.all_to_all(jnp.broadcast_to(cols, (16, ROWS, LANES)), ('y', 'x'), 0,...  8.03 us
    pallas_call x3, Pallas kernels, call(): pl.pallas_call(kernel, out_shape=jax.ShapeDtypeStruct(shape, dtype), in_s...  4.32 us
    all_to_all x1, starting transfers between devices, shards(): lax.all_to_all(jnp.broadcast_to(cols, (16, ROWS, LANES)), ('y', 'x'), 0,...  3.57 us
  transfers between devices with their start and end apart: 2, of which 2 were waited for; matrix products, arithmetic and copies ran while one was open for 3% of the time, Pallas kernels for 0%

profile of v3, /device:TPU:1, one launch (start us, length us, event | category | flops | bytes accessed | tf_op | source)
XLA Modules:
  0.0 100.0 jit_solution(13905074467683426120)
XLA Ops:
  0.7 0.0 copy-start.1
  0.7 0.9 fusion.27
  1.6 9.0 %psum.14 = bf16[32,128]{1,0:T(8,128)(2,1)S(1)} all-reduce(bf16[32,128]{1,0:T(8,128)(2,1)S(1)} %bitcast.23), channel_id=1, replica_groups=mesh['y'=4,'zl'=4,'x'=4,'zh'=4,'c'=2] {'c'}, use_global_device_ids=true, to_apply=%region_0.1 | all-reduce | flops 4096 | bytes 16384 | tf_op jit(solution)/shard_map/psum | solution.py:158
  10.7 14.0 %psum.15.v_ref = bf16[32,128]{1,0:T(8,128)(2,1)S(1)} all-reduce(bf16[32,128]{1,0:T(8,128)(2,1)S(1)} %psum.14), channel_id=1, replica_groups=mesh['y'=4,'zl'=4,'x'=4,'zh'=4,'c'=2] {'zh'}, use_global_device_ids=true, to_apply=%region_1.2 | all-reduce | flops 4096 | bytes 16384 | tf_op jit(solution)/shard_map/psum | solution.py:158
  24.6 0.0 copy-done.1
  24.7 0.0 copy-start
  24.7 0.9 copy-done
  25.6 1.4 %shard_map.91 = bf16[64,32,128]{2,1,0:T(8,128)(2,1)} custom-call(bf16[32,128]{1,0:T(8,128)(2,1)S(1)} %psum.15.v_ref, bf16[32,4096]{1,0:T(8,128)(2,1)S(1)} %bitcast.19, bf16[128,32]{1,0:T(8,128)(2,1)S(1)} %copy-done.1), custom_call_target="tpu_custom_call" | custom-call | tf_op jit(solution)/shard_map/pallas_call | solution.py:136
  27.0 9.0 %all-to-all-start = ((bf16[64,32,128]{2,1,0:T(8,128)(2,1)}), bf16[64,32,128]{2,1,0:T(8,128)(2,1)S(1)}, u32[]{:S(2)}, u32[]{:S(2)}) async-start(bf16[64,32,128]{2,1,0:T(8,128)(2,1)} %shard_map.91), calls=%async_computation | async-start | bytes 1048576 | tf_op jit(solution)/shard_map/all_to_all | solution.py:169
  36.1 0.0 copy-start.4
  36.1 0.6 copy-done.4
  36.7 0.7 dynamic_slice.8
  37.4 0.0 copy-start.2
  37.4 0.0 copy-start.3
  37.4 0.7 copy-done.2
  38.0 0.0 copy-done.3
  38.1 0.7 multiply_divide_fusion
  38.8 0.1 broadcast_in_dim_tile.3
  38.9 0.0 copy-start.5
  38.9 0.6 copy-done.5
  39.5 0.0 copy-start.6
  39.5 0.6 copy-done.6
  40.2 0.8 fusion.10
  41.1 0.8 fusion.24
  41.9 10.4 %all-to-all-done.r_ref = bf16[64,32,128]{2,1,0:T(8,128)(2,1)S(1)} async-done(((bf16[64,32,128]{2,1,0:T(8,128)(2,1)}), bf16[64,32,128]{2,1,0:T(8,128)(2,1)S(1)}, u32[]{:S(2)}, u32[]{:S(2)}) %all-to-all-start) | async-done | bytes 524320 | tf_op jit(solution)/shard_map/all_to_all | solution.py:169
  52.2 1.6 %shard_map.92 = bf16[4,80,128]{2,1,0:T(8,128)(2,1)S(1)} custom-call(bf16[64,32,128]{2,1,0:T(8,128)(2,1)S(1)} %all-to-all-done.r_ref, bf16[384,128]{1,0:T(8,128)(2,1)S(1)} %pad_maximum_fusion.e_ref, f32[192,128]{1,0:T(8,128)S(1)} %get-tuple-element.6.pc_ref, f32[192,128]{1,0:T(8,128)S(1)} %get-tuple-element.5.ps_ref, f32[2,128]{1,0:T(2,128)S(1)} %pad_maximum_fusion.1.w_ref), custom_call_target="tpu_custom_call" | custom-call | tf_op jit(solution)/shard_map/pallas_call | solution.py:136
  53.8 18.1 %all_to_all.20 = bf16[4,80,128]{2,1,0:T(8,128)(2,1)S(1)} all-to-all(bf16[4,80,128]{2,1,0:T(8,128)(2,1)S(1)} %shard_map.92), channel_id=1, replica_groups=mesh['y'=4,'zl'=4,'x'=4,'zh'=4,'c'=2] {'zh'}, dimensions={0} | all-to-all | bytes 163840 | tf_op jit(solution)/shard_map/all_to_all | solution.py:195
  72.0 11.7 %all_to_all.21 = bf16[8,32,128]{2,1,0:T(8,128)(2,1)S(1)} all-to-all(bf16[8,32,128]{2,1,0:T(8,128)(2,1)S(1)} %bitcast.20), channel_id=1, replica_groups=mesh['y'=4,'zl'=4,'x'=4,'zh'=4,'c'=2] {'zl','c'}, dimensions={0} | all-to-all | bytes 131072 | tf_op jit(solution)/shard_map/all_to_all | solution.py:199
  83.7 0.9 broadcast_in_dim.18
  84.6 3.6 %all-to-all-start.3 = ((bf16[16,128,128]{2,1,0:T(8,128)(2,1)}), bf16[16,128,128]{2,1,0:T(8,128)(2,1)S(1)}, u32[]{:S(2)}, u32[]{:S(2)}) async-start(bf16[16,128,128]{2,1,0:T(8,128)(2,1)} %broadcast_in_dim.18), calls=%async_computation.3 | async-start | bytes 1048576 | tf_op jit(solution)/shard_map/all_to_all | solution.py:201
  88.2 2.5 %all-gather = bf16[8,80,128]{2,1,0:T(8,128)(2,1)S(1)} all-gather(bf16[4,80,128]{2,1,0:T(8,128)(2,1)S(1)} %all_to_all.20), channel_id=2, replica_groups=mesh['y'=4,'zl'=4,'x'=4,'zh'=4,'c'=2] {'c'}, dimensions={0}, use_global_device_ids=true | all-gather | bytes 245760 | tf_op jit(solution)/shard_map/all_gather | solution.py:196
  90.7 8.0 %all-to-all-done.3.b_ref = bf16[16,128,128]{2,1,0:T(8,128)(2,1)S(1)} async-done(((bf16[16,128,128]{2,1,0:T(8,128)(2,1)}), bf16[16,128,128]{2,1,0:T(8,128)(2,1)S(1)}, u32[]{:S(2)}, u32[]{:S(2)}) %all-to-all-start.3) | async-done | bytes 524320 | tf_op jit(solution)/shard_map/all_to_all | solution.py:201
  98.8 1.3 %shard_map.93 = f32[2,128,512]{2,1,0:T(8,128)} custom-call(bf16[2,4,80,128]{3,2,1,0:T(8,128)(2,1)S(1)} %bitcast.18, bf16[16,128,128]{2,1,0:T(8,128)(2,1)S(1)} %all-to-all-done.3.b_ref), custom_call_target="tpu_custom_call" | custom-call | tf_op jit(solution)/shard_map/pallas_call | solution.py:136
  (15 shorter events, 0.1 us)
Async XLA Ops:
  0.7 24.0 %copy-start.1 = (bf16[128,32]{1,0:T(8,128)(2,1)S(1)}, bf16[128,32]{1,0:T(8,128)(2,1)}, u32[]{:S(2)}) copy-start(bf16[128,32]{1,0:T(8,128)(2,1)} %constant.155.e_ref) | copy-start | bytes 24580
  24.7 1.0 copy-start
  27.0 25.2 %all-to-all-start = ((bf16[64,32,128]{2,1,0:T(8,128)(2,1)}), bf16[64,32,128]{2,1,0:T(8,128)(2,1)S(1)}, u32[]{:S(2)}, u32[]{:S(2)}) async-start(bf16[64,32,128]{2,1,0:T(8,128)(2,1)} %shard_map.91), calls=%async_computation | async-start | bytes 1048576 | tf_op jit(solution)/shard_map/all_to_all | solution.py:169
  36.1 0.7 copy-start.4
  37.4 0.7 copy-start.2
  37.4 0.7 copy-start.3
  38.9 0.7 copy-start.5
  39.5 0.7 copy-start.6
  84.6 14.1 %all-to-all-start.3 = ((bf16[16,128,128]{2,1,0:T(8,128)(2,1)}), bf16[16,128,128]{2,1,0:T(8,128)(2,1)S(1)}, u32[]{:S(2)}, u32[]{:S(2)}) async-start(bf16[16,128,128]{2,1,0:T(8,128)(2,1)} %broadcast_in_dim.18), calls=%async_computation.3 | async-start | bytes 1048576 | tf_op jit(solution)/shard_map/all_to_all | solution.py:201

commit v4 on v3

--- a/solution.py
+++ b/solution.py
@@ -17,6 +17,7 @@
 LANES = 128
 WIDE = 40
 NARROW = 24
+PARTS = 4
 GA = ("y", "zl", "x")
 COL = ("zh", "c")
 
@@ -131,12 +132,13 @@
         out_ref[1, :, h * 256 : (h + 1) * 256] = part[ROWS:]
 
 
-def call(kernel, shape, dtype, scratch, *args):
+def call(kernel, shape, dtype, scratch, *args, in_hbm=()):
     vmem = pl.BlockSpec(memory_space=pltpu.VMEM)
+    hbm = pl.BlockSpec(memory_space=pltpu.HBM)
     return pl.pallas_call(
         kernel,
         out_shape=jax.ShapeDtypeStruct(shape, dtype),
-        in_specs=[vmem] * len(args),
+        in_specs=[hbm if i in in_hbm else vmem for i in range(len(args))],
         out_specs=vmem,
         scratch_shapes=scratch,
         compiler_params=pltpu.CompilerParams(vmem_limit_bytes=32 * 1024 * 1024),
@@ -155,13 +157,17 @@
     mine = chosen // valence.shape[0] == lax.axis_index(COL)
     own = lax.dynamic_index_in_dim(valence, chosen % valence.shape[0], 0, keepdims=False)
     own = jnp.where(mine, own, 0).astype(bf16).reshape(32, LANES)
-    v = lax.psum(lax.psum(own, "c"), "zh")
+    both = lax.all_gather(own, "c")
+    v = lax.psum(both[0] + both[1], "zh")
 
     half = call(
         pair_y_kernel,
         (N, 32, LANES),
         bf16,
-        [pltpu.VMEM((BANDS * WIDE, LANES), f32), pltpu.VMEM((2 * N * NARROW, LANES), f32)],
+        [
+            pltpu.VMEM((BANDS * WIDE, LANES), f32),
+            pltpu.VMEM((2 * N * NARROW, LANES), f32),
+        ],
         v,
         conduction.reshape(BANDS, N * N),
         jnp.asarray(y_table()).astype(bf16),
@@ -198,6 +204,7 @@
     cols = jnp.broadcast_to(cols[None], (4, 2, 4, 8, LANES)).reshape(8, 32, LANES)
     cols = lax.all_to_all(cols, ("zl", "c"), 0, 0, tiled=True).reshape(4, 2, 32, LANES)
     cols = (cols[:, 0] + cols[:, 1]).reshape(1, ROWS, LANES)
+    cols, bands = lax.optimization_barrier((cols, bands))
     columns = lax.all_to_all(
         jnp.broadcast_to(cols, (16, ROWS, LANES)), ("y", "x"), 0, 0, tiled=True
     )

time: 101 us -> 99.6 us (0.986)
  waiting for transfers between devices: 18.4 us -> 13.8 us
  starting transfers between devices: 12.6 us -> 16.6 us
    psum x2 -> x1, blocking collectives: 23 us -> 14 us  [shards(): v = lax.psum(both[0] + both[1], 'zh')]
    all_gather x0 -> x1, blocking collectives: none -> 8.37 us  [shards(): both = lax.all_gather(own, 'c')]
    all_to_all x1, waiting for transfers between devices: 8.03 us -> 3.19 us  [shards(): lax.all_to_all(cols, ('zl', 'c'), 0, 0, tiled=True).reshape(4, 2, 32, LANES)]
    all_to_all x1, starting transfers between devices: 3.57 us -> 7.54 us  [shards(): lax.all_to_all(cols, ('zl', 'c'), 0, 0, tiled=True).reshape(4, 2, 32, LANES)]
    all_to_all x1, blocking collectives: 11.7 us -> 13.1 us  [shards(): lax.all_to_all(jnp.broadcast_to(cols, (16, ROWS, LANES)), ('y', 'x'), 0,...]
where the time goes in v4:
time: 99.6 us; the launch traced here: 99.1 us
  blocking collectives  55.4 us (56%)
  starting transfers between devices  16.6 us (17%)
  waiting for transfers between devices  13.8 us (14%)
  local copies, waits for them, and re-layouts  5.04 us (5%)
  Pallas kernels  4.33 us (4%)
  other arithmetic  3.19 us (3%)
    all_to_all x1, blocking collectives, shards(): values = lax.all_to_all(values, 'zh', 0, 0, tiled=True)  18 us
    psum x1, blocking collectives, shards(): v = lax.psum(both[0] + both[1], 'zh')  14 us
    all_to_all x1, blocking collectives, shards(): lax.all_to_all(jnp.broadcast_to(cols, (16, ROWS, LANES)), ('y', 'x'), 0,...  13.1 us
    all_to_all x1, waiting for transfers between devices, shards(): block = lax.all_to_all(half, GA, 0, 0, tiled=True)  10.6 us
    all_to_all x1, starting transfers between devices, shards(): block = lax.all_to_all(half, GA, 0, 0, tiled=True)  9.02 us
    all_gather x1, blocking collectives, shards(): both = lax.all_gather(own, 'c')  8.37 us
    all_to_all x1, starting transfers between devices, shards(): lax.all_to_all(cols, ('zl', 'c'), 0, 0, tiled=True).reshape(4, 2, 32, LANES)  7.54 us
    pallas_call x3, Pallas kernels, call(): pl.pallas_call(kernel, out_shape=jax.ShapeDtypeStruct(shape, dtype), in_s...  4.33 us
  transfers between devices with their start and end apart: 2, of which 2 were waited for; matrix products, arithmetic and copies ran while one was open for 3% of the time, Pallas kernels for 0%

profile of v4, /device:TPU:1, one launch (start us, length us, event | category | flops | bytes accessed | tf_op | source)
XLA Modules:
  0.0 99.1 jit_solution(458930902012125704)
XLA Ops:
  0.7 0.9 fusion.27
  1.6 0.0 copy-start.1
  1.6 8.4 %all_gather.9 = bf16[2,32,128]{2,1,0:T(8,128)(2,1)S(1)} all-gather(bf16[1,32,128]{2,1,0:T(8,128)(2,1)S(1)} %bitcast.25), channel_id=1, replica_groups=mesh['y'=4,'zl'=4,'x'=4,'zh'=4,'c'=2] {'c'}, dimensions={0}, use_global_device_ids=true | all-gather | bytes 24576 | tf_op jit(solution)/shard_map/all_gather | solution.py:160
  10.0 14.0 %psum.7.v_ref = bf16[32,128]{1,0:T(8,128)(2,1)S(1)} all-reduce(bf16[32,128]{1,0:T(8,128)(2,1)S(1)} %fusion.28), channel_id=1, replica_groups=mesh['y'=4,'zl'=4,'x'=4,'zh'=4,'c'=2] {'zh'}, use_global_device_ids=true, to_apply=%region_0.1 | all-reduce | flops 4096 | bytes 16384 | tf_op jit(solution)/shard_map/psum | solution.py:161
  23.9 0.0 copy-done.1
  24.0 0.0 copy-start
  24.0 0.9 copy-done
  24.9 1.4 %shard_map.91 = bf16[64,32,128]{2,1,0:T(8,128)(2,1)} custom-call(bf16[32,128]{1,0:T(8,128)(2,1)S(1)} %psum.7.v_ref, bf16[32,4096]{1,0:T(8,128)(2,1)S(1)} %bitcast.22, bf16[128,32]{1,0:T(8,128)(2,1)S(1)} %copy-done.1), custom_call_target="tpu_custom_call" | custom-call | tf_op jit(solution)/shard_map/pallas_call | solution.py:138
  26.3 9.0 %all-to-all-start = ((bf16[64,32,128]{2,1,0:T(8,128)(2,1)}), bf16[64,32,128]{2,1,0:T(8,128)(2,1)S(1)}, u32[]{:S(2)}, u32[]{:S(2)}) async-start(bf16[64,32,128]{2,1,0:T(8,128)(2,1)} %shard_map.91), calls=%async_computation | async-start | bytes 1048576 | tf_op jit(solution)/shard_map/all_to_all | solution.py:175
  35.4 0.0 copy-start.4
  35.4 0.6 copy-done.4
  36.0 0.6 dynamic_slice.8
  36.7 0.0 copy-start.2
  36.7 0.0 copy-start.3
  36.7 0.7 copy-done.2
  37.3 0.0 copy-done.3
  37.3 0.6 multiply_divide_fusion
  38.0 0.1 broadcast_in_dim_tile.3
  38.1 0.0 copy-start.5
  38.1 0.6 copy-done.5
  38.7 0.0 copy-start.6
  38.8 0.6 copy-done.6
  39.4 0.8 fusion.10
  40.3 0.8 fusion.24
  41.1 10.6 %all-to-all-done.r_ref = bf16[64,32,128]{2,1,0:T(8,128)(2,1)S(1)} async-done(((bf16[64,32,128]{2,1,0:T(8,128)(2,1)}), bf16[64,32,128]{2,1,0:T(8,128)(2,1)S(1)}, u32[]{:S(2)}, u32[]{:S(2)}) %all-to-all-start) | async-done | bytes 524320 | tf_op jit(solution)/shard_map/all_to_all | solution.py:175
  51.6 1.6 %shard_map.92 = bf16[4,80,128]{2,1,0:T(8,128)(2,1)S(1)} custom-call(bf16[64,32,128]{2,1,0:T(8,128)(2,1)S(1)} %all-to-all-done.r_ref, bf16[384,128]{1,0:T(8,128)(2,1)S(1)} %pad_maximum_fusion.e_ref, f32[192,128]{1,0:T(8,128)S(1)} %get-tuple-element.10.pc_ref, f32[192,128]{1,0:T(8,128)S(1)} %get-tuple-element.9.ps_ref, f32[2,128]{1,0:T(2,128)S(1)} %pad_maximum_fusion.1.w_ref), custom_call_target="tpu_custom_call" | custom-call | tf_op jit(solution)/shard_map/pallas_call | solution.py:138
  53.3 18.0 %all_to_all.20 = bf16[4,80,128]{2,1,0:T(8,128)(2,1)S(1)} all-to-all(bf16[4,80,128]{2,1,0:T(8,128)(2,1)S(1)} %shard_map.92), channel_id=1, replica_groups=mesh['y'=4,'zl'=4,'x'=4,'zh'=4,'c'=2] {'zh'}, dimensions={0} | all-to-all | bytes 163840 | tf_op jit(solution)/shard_map/all_to_all | solution.py:201
  71.3 0.6 broadcast_in_dim.19
  71.9 7.5 %all-to-all-start.2 = ((bf16[8,32,128]{2,1,0:T(8,128)(2,1)}), bf16[8,32,128]{2,1,0:T(8,128)(2,1)S(1)}, u32[]{:S(2)}, u32[]{:S(2)}) async-start(bf16[8,32,128]{2,1,0:T(8,128)(2,1)} %bitcast.6), calls=%async_computation.2 | async-start | bytes 131072 | tf_op jit(solution)/shard_map/all_to_all | solution.py:205
  79.5 1.9 %all-gather = bf16[8,80,128]{2,1,0:T(8,128)(2,1)S(1)} all-gather(bf16[4,80,128]{2,1,0:T(8,128)(2,1)S(1)} %all_to_all.20), channel_id=2, replica_groups=mesh['y'=4,'zl'=4,'x'=4,'zh'=4,'c'=2] {'c'}, dimensions={0}, use_global_device_ids=true | all-gather | bytes 245760 | tf_op jit(solution)/shard_map/all_gather | solution.py:202
  81.4 3.2 %all-to-all-done.2 = bf16[8,32,128]{2,1,0:T(8,128)(2,1)S(1)} async-done(((bf16[8,32,128]{2,1,0:T(8,128)(2,1)}), bf16[8,32,128]{2,1,0:T(8,128)(2,1)S(1)}, u32[]{:S(2)}, u32[]{:S(2)}) %all-to-all-start.2) | async-done | bytes 65568 | tf_op jit(solution)/shard_map/all_to_all | solution.py:205
  84.6 0.1 broadcast_in_dim.21
  84.7 13.1 %all_to_all.21.b_ref = bf16[16,128,128]{2,1,0:T(8,128)(2,1)S(1)} all-to-all(bf16[16,128,128]{2,1,0:T(8,128)(2,1)S(1)} %broadcast_in_dim.21), channel_id=1, replica_groups=mesh['y'=4,'zl'=4,'x'=4,'zh'=4,'c'=2] {'y','x'}, dimensions={0} | all-to-all | bytes 1048576 | tf_op jit(solution)/shard_map/all_to_all | solution.py:208
  97.8 1.3 %shard_map.93 = f32[2,128,512]{2,1,0:T(8,128)} custom-call(bf16[2,4,80,128]{3,2,1,0:T(8,128)(2,1)S(1)} %bitcast.21, bf16[16,128,128]{2,1,0:T(8,128)(2,1)S(1)} %all_to_all.21.b_ref), custom_call_target="tpu_custom_call" | custom-call | tf_op jit(solution)/shard_map/pallas_call | solution.py:138
  (15 shorter events, 0.1 us)
Async XLA Ops:
  1.6 22.4 %copy-start.1 = (bf16[128,32]{1,0:T(8,128)(2,1)S(1)}, bf16[128,32]{1,0:T(8,128)(2,1)}, u32[]{:S(2)}) copy-start(bf16[128,32]{1,0:T(8,128)(2,1)} %constant.155.e_ref) | copy-start | bytes 24580
  24.0 1.0 copy-start
  26.3 25.3 %all-to-all-start = ((bf16[64,32,128]{2,1,0:T(8,128)(2,1)}), bf16[64,32,128]{2,1,0:T(8,128)(2,1)S(1)}, u32[]{:S(2)}, u32[]{:S(2)}) async-start(bf16[64,32,128]{2,1,0:T(8,128)(2,1)} %shard_map.91), calls=%async_computation | async-start | bytes 1048576 | tf_op jit(solution)/shard_map/all_to_all | solution.py:175
  35.4 0.7 copy-start.4
  36.7 0.7 copy-start.2
  36.7 0.7 copy-start.3
  38.1 0.7 copy-start.5
  38.7 0.7 copy-start.6
  71.9 12.6 %all-to-all-start.2 = ((bf16[8,32,128]{2,1,0:T(8,128)(2,1)}), bf16[8,32,128]{2,1,0:T(8,128)(2,1)S(1)}, u32[]{:S(2)}, u32[]{:S(2)}) async-start(bf16[8,32,128]{2,1,0:T(8,128)(2,1)} %bitcast.6), calls=%async_computation.2 | async-start | bytes 131072 | tf_op jit(solution)/shard_map/all_to_all | solution.py:205

commit v5 on v4

v5 whole, which is shorter than its diff:
```python
import jax
import jax.numpy as jnp
import numpy as np
from jax import lax
from jax.experimental import pallas as pl
from jax.experimental.pallas import tpu as pltpu
from jax.sharding import Mesh
from jax.sharding import PartitionSpec as P

N = 64
BANDS = 32
ROWS = 128
COLS = 64
SPOTS = ROWS + COLS
LANES = 128
WIDE = 40
PARTS = 4
GA = ("y", "zl", "x")
COL = ("zh", "c")

f32 = jnp.float32
bf16 = jnp.bfloat16


def dot(left, right):
    return jnp.dot(left, right, preferred_element_type=f32)


def lane_index(shape):
    return lax.broadcasted_iota(jnp.int32, shape, len(shape) - 1)


def y_table():
    parity = np.arange(2)[:, None, None, None]
    imag = np.arange(2)[None, :, None, None]
    ky = np.arange(N // 2)[None, None, :, None]
    half = np.arange(N // 2)[None, None, None, :]
    turn = (ky * (2 * half + parity) + 16 * imag) % N
    return wave(turn).reshape(LANES, N // 2)


def wave(turn):
    return (np.cos(2.0 * np.pi * (turn % N) / N) / 8.0).astype(np.float32)


def x_table():
    kx = np.arange(N)[:, None]
    lane = np.arange(LANES)[None, :]
    plane, imag = lane // 8, lane // 4 % 2
    x = 16 * (plane // 4) + 4 * (lane % 4) + plane % 4
    return np.concatenate([wave(kx * x - 16 * imag), wave(kx * x + 16 * (1 - imag))], axis=1)


def z_table():
    turn = np.arange(N)[:, None] * (np.arange(LANES)[None, :] % N)
    return np.concatenate([wave(turn), wave(turn - 16)], axis=1)


def pair_kernel(v_ref, c_ref, row_ref, col_ref, out_ref):
    v = v_ref[...].astype(f32)
    for i in range(N // 2):
        lanes = pl.ds(i * LANES, LANES)
        out_ref[:, lanes] = (c_ref[:, lanes].astype(f32) * v[i : i + 1, :]).astype(bf16)
    row = row_ref[...]
    col = jnp.concatenate([col_ref[...]] * 2, axis=1)
    spots = [row >> 6, row & (N - 1), col >> 6, col & (N - 1)]
    spots = jnp.concatenate(spots * 2, axis=0).astype(f32)
    out_ref[:, N * N :] = jnp.concatenate([spots] * 4, axis=0).astype(bf16)


def y_kernel(p_ref, e_ref, out_ref, by_row, by_ky):
    for i in range(N // 2):
        by_row[pl.ds(i, BANDS, stride=WIDE), :] = p_ref[:, i * LANES : (i + 1) * LANES].astype(f32)
    table = e_ref[...]
    low = lane_index((N, LANES)) < N
    half = N // 2
    for j in range(BANDS // 2):
        first = by_row[pl.ds(2 * WIDE * j, half), :]
        second = by_row[pl.ds(2 * WIDE * j + WIDE, half), :]
        both = dot(table, jnp.concatenate([first, second], axis=1).astype(bf16))
        even, odd = both[:N], both[N:]
        even = jnp.where(low, even[:, :LANES], pltpu.roll(even[:, LANES:], N, 1))
        odd = jnp.where(low, pltpu.roll(odd[:, :LANES], N, 1), odd[:, LANES:])
        at = 8 * (j % 4) + j // 4
        for start, value in ((at, even + odd), (half * WIDE + at, even - odd)):
            by_ky[pl.ds(start, half, stride=WIDE), :] = value[:half]
            by_ky[pl.ds(start + 4, half, stride=WIDE), :] = value[half:]
    for ky in range(N):
        y, zl, x = ky // 16, ky // 4 % 4, ky % 4
        out_ref[4 * y + x, 32 * zl : 32 * zl + 32, :] = by_ky[pl.ds(ky * WIDE, 32), :].astype(bf16)


def spots_kernel(r_ref, e_ref, p_ref, w_ref, out_ref):
    column = lane_index((2 * LANES, LANES))
    band = lax.broadcasted_iota(jnp.int32, (2 * LANES, LANES), 0) // N
    total = jnp.zeros((2 * SPOTS, LANES), f32)
    for g in range(4):
        planes = r_ref[:, 32 * g : 32 * g + 32, :].astype(f32)
        table = jnp.concatenate([e_ref[g, :, :LANES], e_ref[g, :, LANES:]], axis=0)
        cos_z = jnp.concatenate([p_ref[g, :, :LANES].astype(f32)] * 2, axis=1)
        sin_z = jnp.concatenate([p_ref[g, :, LANES:].astype(f32)] * 2, axis=1)
        for h in range(2):
            first = planes[:, 16 * h : 16 * h + 8, :].reshape(LANES, LANES)
            second = planes[:, 16 * h + 8 : 16 * h + 16, :].reshape(LANES, LANES)
            at_x = dot(table, jnp.concatenate([first, second], axis=1).astype(bf16))
            real, imag = at_x[:SPOTS], at_x[SPOTS:]
            real_z = real * cos_z + imag * sin_z
            imag_z = imag * cos_z - real * sin_z
            terms = jnp.concatenate([real_z, imag_z], axis=0).astype(bf16)
            ones = jnp.where(column == band + 16 * g + 4 * h, 1.0, 0.0).astype(bf16)
            total = total + dot(terms, ones)
    joined = total[:SPOTS] + pltpu.roll(total[SPOTS:], 8, 1)
    rows = (joined[:ROWS] * w_ref[...]).T
    for q in range(4):
        cols = joined[ROWS + 16 * q : ROWS + 16 * q + 16]
        cols = cols[:8] + pltpu.roll(cols[8:], N, 1)
        for g in range(4):
            block = [rows[16 * g : 16 * g + 16], cols]
            out_ref[4 * g + q] = jnp.concatenate(block, axis=0).astype(bf16)


def columns_kernel(v_ref, core_ref, out_ref):
    second = core_ref[...] > 0.5
    group = lane_index((32, LANES)) // 16
    rows = [jnp.zeros((32, LANES), f32)] * 4
    for s in range(8):
        core, zl = s // 4, s % 4
        cols = [v_ref[core, 4 * zl + q].astype(f32)[16:] for q in range(4)]
        cols = jnp.concatenate(cols, axis=0)
        cols = jnp.where(second, pltpu.roll(cols, N, 1), cols)
        for g in range(4):
            moved = cols if s == g else pltpu.roll(cols, 16 * (s - g) % LANES, 1)
            rows[g] = jnp.where(group == s, moved, rows[g])
    message = jnp.concatenate(rows, axis=0).astype(bf16)
    for i in range(16):
        out_ref[i] = message


def panel_kernel(a_ref, b_ref, out_ref, spread):
    for y in range(4):
        for x in range(4):
            for zl in range(4):
                at = (16 * y + 4 * zl + x) * WIDE
                spread[pl.ds(at, 32), :] = b_ref[4 * y + x, 32 * zl : 32 * zl + 32, :].astype(f32)
    real_lane = lane_index((ROWS, LANES)) % 16 < 8
    upper, lower = [], []
    for q in range(4):
        rows = [a_ref[s // 4, 4 * (s % 4) + q].astype(f32)[:16] for s in range(8)]
        rows = jnp.concatenate(rows, axis=0).T
        turned = jnp.where(real_lane, pltpu.roll(rows, LANES - 8, 1), -pltpu.roll(rows, 8, 1))
        upper.append(rows.astype(bf16))
        lower.append(turned.astype(bf16))
    both = jnp.concatenate(
        [jnp.concatenate(upper, axis=1), jnp.concatenate(lower, axis=1)], axis=0
    )
    for h in range(2):
        columns = []
        for j in range(4 * h, 4 * h + 4):
            parts = [spread[pl.ds(8 * q + j, N, stride=WIDE), :] for q in range(4)]
            columns.append(jnp.concatenate(parts, axis=1))
        part = lax.dot_general(
            both,
            jnp.concatenate(columns, axis=0).astype(bf16),
            (((1,), (1,)), ((), ())),
            preferred_element_type=f32,
        )
        part = part * (1.0 / 16.0)
        out_ref[0, :, h * 256 : (h + 1) * 256] = part[:ROWS]
        out_ref[1, :, h * 256 : (h + 1) * 256] = part[ROWS:]


def call(kernel, shape, dtype, scratch, *args, in_hbm=()):
    vmem = pl.BlockSpec(memory_space=pltpu.VMEM)
    hbm = pl.BlockSpec(memory_space=pltpu.HBM)
    return pl.pallas_call(
        kernel,
        out_shape=jax.ShapeDtypeStruct(shape, dtype),
        in_specs=[hbm if i in in_hbm else vmem for i in range(len(args))],
        out_specs=vmem,
        scratch_shapes=scratch,
        compiler_params=pltpu.CompilerParams(vmem_limit_bytes=32 * 1024 * 1024),
    )(*args)


def shards(
    valence, conduction, band_index, occ_valence, occ_conduction, gap_energy, row_map, col_map
):
    chosen = band_index[0]
    core = lax.axis_index("c")
    mine = chosen // valence.shape[0] == lax.axis_index(COL)
    own = lax.dynamic_index_in_dim(valence, chosen % valence.shape[0], 0, keepdims=False)
    own = jnp.where(mine, own, 0).astype(bf16).reshape(32, LANES)
    both = lax.all_gather(own, "c")
    v = lax.psum(both[0] + both[1], "zh")

    pairs = call(
        pair_kernel,
        (BANDS, N * N + LANES),
        bf16,
        [],
        v,
        conduction.reshape(BANDS, N * N),
        row_map[None],
        col_map[None],
    )
    pairs = pairs.reshape(4, 8, N * N + LANES)
    pairs = lax.all_to_all(pairs, "zl", 0, 0, tiled=True)

    half = call(
        y_kernel,
        (16, ROWS, LANES),
        bf16,
        [pltpu.VMEM((BANDS * WIDE, LANES), f32), pltpu.VMEM((N * WIDE, LANES), f32)],
        pairs.reshape(BANDS, N * N + LANES),
        jnp.asarray(y_table()).astype(bf16),
    )
    block = lax.all_to_all(half, ("y", "x"), 0, 0, tiled=True)

    spots = pairs[:, :4, N * N :]
    spots = jnp.concatenate([spots[:, :2], spots[:, 2:, :COLS]], axis=2)
    hot = (spots[..., None] == jnp.arange(N, dtype=bf16)).astype(bf16)
    table = dot(hot[:, 0], jnp.asarray(x_table()).astype(bf16)).astype(bf16)
    phase = dot(hot[:, 1], jnp.asarray(z_table()).astype(bf16)).astype(bf16)
    weight = 2.0 * (occ_conduction - occ_valence[chosen]).astype(f32) / gap_energy
    weight = lax.dynamic_slice_in_dim(weight, 8 * lax.axis_index("zl"), 8)
    values = call(
        spots_kernel,
        (16, 24, LANES),
        bf16,
        [],
        block,
        table,
        phase,
        jnp.tile(weight, 16)[None],
    )

    values = lax.all_to_all(values, ("zl", "zh"), 0, 0, tiled=True)
    values = lax.all_gather(values, "c")
    cols = call(
        columns_kernel,
        (16, ROWS, LANES),
        bf16,
        [],
        values,
        jnp.full((1, LANES), core, f32),
    )
    columns = lax.all_to_all(cols, ("y", "x"), 0, 0, tiled=True)
    return call(
        panel_kernel,
        (2, ROWS, 8 * N),
        f32,
        [pltpu.VMEM((N * WIDE, LANES), f32)],
        values,
        columns,
    )


def solution(mesh):
    fine = Mesh(mesh.devices.reshape(4, 4, 4, 4, 2), ("y", "zl", "x", "zh", "c"))
    return jax.shard_map(
        shards,
        mesh=fine,
        in_specs=(
            P(COL, GA, None),
            P(COL, GA, None),
            P(),
            P(),
            P(COL),
            P(COL),
            P(GA),
            P(GA),
        ),
        out_specs=P(None, GA, COL),
        check_vma=False,
    )
```

time: 99.6 us -> 97.5 us (0.979)
  blocking collectives: 55.4 us -> 43.9 us
  waiting for transfers between devices: 13.8 us -> 23.4 us
  other arithmetic: 3.19 us -> 1.63 us
  Pallas kernels: 4.33 us -> 5.88 us
  local copies, waits for them, and re-layouts: 5.04 us -> 3.54 us
    all_to_all x2 -> x1, blocking collectives: 31.1 us -> 13.8 us  [shards(): columns = lax.all_to_all(cols, ('y', 'x'), 0, 0, tiled=True)]
    all_to_all x2 -> x3, waiting for transfers between devices: 13.8 us -> 23.4 us  [the longest x1 12 us: shards(): values = lax.all_to_all(values, ('zl', 'zh'), 0, 0, tiled=True)]
    all_gather x1, blocking collectives: 1.91 us -> 7.8 us  [shards(): values = lax.all_gather(values, 'c')]
    pallas_call x3 -> x5, Pallas kernels: 4.33 us -> 5.88 us  [call(): pl.pallas_call(kernel, out_shape=jax.ShapeDtypeStruct(shape, dtype), in_s...]
    unnamed x15 -> x18, local copies, waits for them, and re-layouts: 3.56 us -> 2.71 us
    all_to_all x2 -> x3, starting transfers between devices: 16.6 us -> 17 us  [the longest x1 6.76 us: shards(): block = lax.all_to_all(half, ('y', 'x'), 0, 0, tiled=True)]
  transfers between devices with their start and end apart: 2 -> 3, of which waited for: 2 -> 3; matrix products, arithmetic and copies ran while one was open for 3% -> 2% of each run, Pallas kernels for 0% -> 0%
where the time goes in v5:
time: 97.5 us; the launch traced here: 96.8 us
  blocking collectives  43.9 us (45%)
  waiting for transfers between devices  23.4 us (24%)
  starting transfers between devices  17 us (17%)
  Pallas kernels  5.88 us (6%)
  local copies, waits for them, and re-layouts  3.54 us (4%)
  other arithmetic  1.63 us (2%)
    psum x1, blocking collectives, shards(): v = lax.psum(both[0] + both[1], 'zh')  14 us
    all_to_all x1, blocking collectives, shards(): columns = lax.all_to_all(cols, ('y', 'x'), 0, 0, tiled=True)  13.8 us
    all_to_all x1, waiting for transfers between devices, shards(): values = lax.all_to_all(values, ('zl', 'zh'), 0, 0, tiled=True)  12 us
    all_gather x1, blocking collectives, shards(): both = lax.all_gather(own, 'c')  8.37 us
    all_gather x1, blocking collectives, shards(): values = lax.all_gather(values, 'c')  7.8 us
    all_to_all x1, waiting for transfers between devices, shards(): block = lax.all_to_all(half, ('y', 'x'), 0, 0, tiled=True)  7.2 us
    all_to_all x1, starting transfers between devices, shards(): block = lax.all_to_all(half, ('y', 'x'), 0, 0, tiled=True)  6.76 us
    all_to_all x1, starting transfers between devices, shards(): values = lax.all_to_all(values, ('zl', 'zh'), 0, 0, tiled=True)  6.65 us
  transfers between devices with their start and end apart: 3, of which 3 were waited for; matrix products, arithmetic and copies ran while one was open for 2% of the time, Pallas kernels for 0%

profile of v5, /device:TPU:1, one launch (start us, length us, event | category | flops | bytes accessed | tf_op | source)
XLA Modules:
  0.0 96.8 jit_solution(2495428543990444841)
XLA Ops:
  0.7 0.9 fusion
  1.6 8.4 %all_gather.9 = bf16[2,32,128]{2,1,0:T(8,128)(2,1)S(1)} all-gather(bf16[1,32,128]{2,1,0:T(8,128)(2,1)S(1)} %bitcast.33), channel_id=1, replica_groups=mesh['y'=4,'zl'=4,'x'=4,'zh'=4,'c'=2] {'c'}, dimensions={0}, use_global_device_ids=true | all-gather | bytes 24576 | tf_op jit(solution)/shard_map/all_gather | solution.py:193
  10.0 14.0 %psum.7.v_ref = bf16[32,128]{1,0:T(8,128)(2,1)S(1)} all-reduce(bf16[32,128]{1,0:T(8,128)(2,1)S(1)} %fusion.1), channel_id=1, replica_groups=mesh['y'=4,'zl'=4,'x'=4,'zh'=4,'c'=2] {'zh'}, use_global_device_ids=true, to_apply=%region_0.1 | all-reduce | flops 4096 | bytes 16384 | tf_op jit(solution)/shard_map/psum | solution.py:194
  23.9 0.0 copy-start.2
  23.9 0.0 copy-start.3
  24.0 0.6 copy-done.2
  24.6 0.0 copy-done.3
  24.6 0.0 copy-start
  24.6 0.9 copy-done
  25.6 0.8 shard_map.109
  26.3 0.0 copy-start.8
  26.3 0.0 copy-start.6
  26.3 0.0 copy-start.7
  26.3 3.6 %all-to-all-start = ((bf16[4,8,4224]{2,1,0:T(8,128)(2,1)}), bf16[4,8,4224]{2,1,0:T(8,128)(2,1)S(1)}, u32[]{:S(2)}, u32[]{:S(2)}) async-start(bf16[4,8,4224]{2,1,0:T(8,128)(2,1)} %bitcast.5), calls=%async_computation | async-start | bytes 540672 | tf_op jit(solution)/shard_map/all_to_all | solution.py:207
  29.9 0.0 copy-start.1
  30.0 0.0 copy-done.8
  30.0 0.6 dynamic_slice.11
  30.6 0.0 copy-done.6
  30.6 0.0 copy-done.7
  30.6 0.6 multiply_divide_fusion
  31.3 0.1 dynamic_slice.12
  31.3 0.1 broadcast_in_dim_tile.3.w_ref
  31.4 4.2 %all-to-all-done = bf16[4,8,4224]{2,1,0:T(8,128)(2,1)S(1)} async-done(((bf16[4,8,4224]{2,1,0:T(8,128)(2,1)}), bf16[4,8,4224]{2,1,0:T(8,128)(2,1)S(1)}, u32[]{:S(2)}, u32[]{:S(2)}) %all-to-all-start) | async-done | bytes 270368 | tf_op jit(solution)/shard_map/all_to_all | solution.py:207
  35.6 0.0 copy-done.1
  35.6 1.5 %shard_map.110 = bf16[16,128,128]{2,1,0:T(8,128)(2,1)} custom-call(bf16[32,4224]{1,0:T(8,128)(2,1)S(1)} %bitcast.29, bf16[128,32]{1,0:T(8,128)(2,1)S(1)} %copy-done.1), custom_call_target="tpu_custom_call" | custom-call | tf_op jit(solution)/shard_map/pallas_call | solution.py:175
  37.1 6.8 %all-to-all-start.1 = ((bf16[16,128,128]{2,1,0:T(8,128)(2,1)}), bf16[16,128,128]{2,1,0:T(8,128)(2,1)S(1)}, u32[]{:S(2)}, u32[]{:S(2)}) async-start(bf16[16,128,128]{2,1,0:T(8,128)(2,1)} %shard_map.110), calls=%async_computation.1 | async-start | bytes 1048576 | tf_op jit(solution)/shard_map/all_to_all | solution.py:217
  43.9 0.0 copy-start.5
  44.0 0.1 iota_compare_fusion
  44.0 0.7 copy-done.5
  44.7 0.0 copy-start.4
  44.7 0.3 convolution_convert_fusion.1.e_ref
  45.0 0.4 copy-done.4
  45.5 0.3 convolution_convert_fusion.p_ref
  45.8 7.2 %all-to-all-done.1.r_ref = bf16[16,128,128]{2,1,0:T(8,128)(2,1)S(1)} async-done(((bf16[16,128,128]{2,1,0:T(8,128)(2,1)}), bf16[16,128,128]{2,1,0:T(8,128)(2,1)S(1)}, u32[]{:S(2)}, u32[]{:S(2)}) %all-to-all-start.1) | async-done | bytes 524320 | tf_op jit(solution)/shard_map/all_to_all | solution.py:217
  53.0 2.1 %shard_map.111 = bf16[16,24,128]{2,1,0:T(8,128)(2,1)} custom-call(bf16[16,128,128]{2,1,0:T(8,128)(2,1)S(1)} %all-to-all-done.1.r_ref, bf16[4,192,256]{2,1,0:T(8,128)(2,1)S(1)} %convolution_convert_fusion.1.e_ref, bf16[4,192,256]{2,1,0:T(8,128)(2,1)S(1)} %convolution_convert_fusion.p_ref, f32[1,128]{1,0:T(1,128)S(1)} %broadcast_in_dim_tile.3.w_ref), custom_call_target="tpu_custom_call" | custom-call | tf_op jit(solution)/shard_map/pallas_call | solution.py:175
  55.1 6.7 %all-to-all-start.2 = ((bf16[16,24,128]{2,1,0:T(8,128)(2,1)}), bf16[16,24,128]{2,1,0:T(8,128)(2,1)S(1)}, u32[]{:S(2)}, u32[]{:S(2)}) async-start(bf16[16,24,128]{2,1,0:T(8,128)(2,1)} %shard_map.111), calls=%async_computation.2 | async-start | bytes 196608 | tf_op jit(solution)/shard_map/all_to_all | solution.py:237
  61.7 12.0 %all-to-all-done.2 = bf16[16,24,128]{2,1,0:T(8,128)(2,1)S(1)} async-done(((bf16[16,24,128]{2,1,0:T(8,128)(2,1)}), bf16[16,24,128]{2,1,0:T(8,128)(2,1)S(1)}, u32[]{:S(2)}, u32[]{:S(2)}) %all-to-all-start.2) | async-done | bytes 98336 | tf_op jit(solution)/shard_map/all_to_all | solution.py:237
  73.7 7.8 %all-gather = bf16[32,24,128]{2,1,0:T(8,128)(2,1)S(1)} all-gather(bf16[16,24,128]{2,1,0:T(8,128)(2,1)S(1)} %all-to-all-done.2), channel_id=2, replica_groups=mesh['y'=4,'zl'=4,'x'=4,'zh'=4,'c'=2] {'c'}, dimensions={0}, use_global_device_ids=true | all-gather | bytes 294912 | tf_op jit(solution)/shard_map/all_gather | solution.py:238
  81.5 0.2 shard_map.112
  81.8 13.8 %all_to_all.20.b_ref = bf16[16,128,128]{2,1,0:T(8,128)(2,1)S(1)} all-to-all(bf16[16,128,128]{2,1,0:T(8,128)(2,1)S(1)} %shard_map.112), channel_id=1, replica_groups=mesh['y'=4,'zl'=4,'x'=4,'zh'=4,'c'=2] {'y','x'}, dimensions={0} | all-to-all | bytes 1048576 | tf_op jit(solution)/shard_map/all_to_all | solution.py:247
  95.5 1.3 %shard_map.113 = f32[2,128,512]{2,1,0:T(8,128)} custom-call(bf16[2,16,24,128]{3,2,1,0:T(8,128)(2,1)S(1)} %bitcast.28, bf16[16,128,128]{2,1,0:T(8,128)(2,1)S(1)} %all_to_all.20.b_ref), custom_call_target="tpu_custom_call" | custom-call | tf_op jit(solution)/shard_map/pallas_call | solution.py:175
  (7 shorter events, 0.0 us)
Async XLA Ops:
  23.9 0.7 copy-start.2
  23.9 0.7 copy-start.3
  24.6 0.9 copy-start
  26.3 3.6 %copy-start.8 = (s32[128]{0:T(128)S(1)}, s32[128]{0:T(128)}, u32[]{:S(2)}) copy-start(s32[128]{0:T(128)} %param.14) | copy-start | bytes 1540
  26.3 4.3 %copy-start.6 = (f32[32]{0:T(128)S(1)}, f32[32]{0:T(128)}, u32[]{:S(2)}) copy-start(f32[32]{0:T(128)} %param.16) | copy-start | bytes 388
  26.3 4.3 %copy-start.7 = (s32[32]{0:T(128)S(1)}, s32[32]{0:T(128)}, u32[]{:S(2)}) copy-start(s32[32]{0:T(128)} %param.15) | copy-start | bytes 388
  26.3 9.3 %all-to-all-start = ((bf16[4,8,4224]{2,1,0:T(8,128)(2,1)}), bf16[4,8,4224]{2,1,0:T(8,128)(2,1)S(1)}, u32[]{:S(2)}, u32[]{:S(2)}) async-start(bf16[4,8,4224]{2,1,0:T(8,128)(2,1)} %bitcast.5), calls=%async_computation | async-start | bytes 540672 | tf_op jit(solution)/shard_map/all_to_all | solution.py:207
  29.9 5.7 %copy-start.1 = (bf16[128,32]{1,0:T(8,128)(2,1)S(1)}, bf16[128,32]{1,0:T(8,128)(2,1)}, u32[]{:S(2)}) copy-start(bf16[128,32]{1,0:T(8,128)(2,1)} %constant.66.e_ref) | copy-start | bytes 24580
  37.1 15.9 %all-to-all-start.1 = ((bf16[16,128,128]{2,1,0:T(8,128)(2,1)}), bf16[16,128,128]{2,1,0:T(8,128)(2,1)S(1)}, u32[]{:S(2)}, u32[]{:S(2)}) async-start(bf16[16,128,128]{2,1,0:T(8,128)(2,1)} %shard_map.110), calls=%async_computation.1 | async-start | bytes 1048576 | tf_op jit(solution)/shard_map/all_to_all | solution.py:217
  43.9 0.8 copy-start.5
  44.7 0.8 copy-start.4
  55.1 18.7 %all-to-all-start.2 = ((bf16[16,24,128]{2,1,0:T(8,128)(2,1)}), bf16[16,24,128]{2,1,0:T(8,128)(2,1)S(1)}, u32[]{:S(2)}, u32[]{:S(2)}) async-start(bf16[16,24,128]{2,1,0:T(8,128)(2,1)} %shard_map.111), calls=%async_computation.2 | async-start | bytes 196608 | tf_op jit(solution)/shard_map/all_to_all | solution.py:237

commit v6 on v5

--- a/solution.py
+++ b/solution.py
@@ -14,7 +14,6 @@
 SPOTS = ROWS + COLS
 LANES = 128
 WIDE = 40
-PARTS = 4
 GA = ("y", "zl", "x")
 COL = ("zh", "c")
 
@@ -110,7 +109,7 @@
             ones = jnp.where(column == band + 16 * g + 4 * h, 1.0, 0.0).astype(bf16)
             total = total + dot(terms, ones)
     joined = total[:SPOTS] + pltpu.roll(total[SPOTS:], 8, 1)
-    rows = (joined[:ROWS] * w_ref[...]).T
+    rows = (joined[:ROWS] * w_ref[0:1, :]).T
     for q in range(4):
         cols = joined[ROWS + 16 * q : ROWS + 16 * q + 16]
         cols = cols[:8] + pltpu.roll(cols[8:], N, 1)
@@ -120,7 +119,7 @@
 
 
 def columns_kernel(v_ref, core_ref, out_ref):
-    second = core_ref[...] > 0.5
+    second = core_ref[1:2, :] > 0.5
     group = lane_index((32, LANES)) // 16
     rows = [jnp.zeros((32, LANES), f32)] * 4
     for s in range(8):
@@ -169,13 +168,12 @@
         out_ref[1, :, h * 256 : (h + 1) * 256] = part[ROWS:]
 
 
-def call(kernel, shape, dtype, scratch, *args, in_hbm=()):
+def call(kernel, shape, dtype, scratch, *args):
     vmem = pl.BlockSpec(memory_space=pltpu.VMEM)
-    hbm = pl.BlockSpec(memory_space=pltpu.HBM)
     return pl.pallas_call(
         kernel,
         out_shape=jax.ShapeDtypeStruct(shape, dtype),
-        in_specs=[hbm if i in in_hbm else vmem for i in range(len(args))],
+        in_specs=[vmem] * len(args),
         out_specs=vmem,
         scratch_shapes=scratch,
         compiler_params=pltpu.CompilerParams(vmem_limit_bytes=32 * 1024 * 1024),
@@ -205,6 +203,8 @@
     )
     pairs = pairs.reshape(4, 8, N * N + LANES)
     pairs = lax.all_to_all(pairs, "zl", 0, 0, tiled=True)
+    late = lax.optimization_barrier((pairs, occ_valence, occ_conduction, gap_energy))
+    pairs, occ_valence, occ_conduction, gap_energy = late
 
     half = call(
         y_kernel,
@@ -223,6 +223,7 @@
     phase = dot(hot[:, 1], jnp.asarray(z_table()).astype(bf16)).astype(bf16)
     weight = 2.0 * (occ_conduction - occ_valence[chosen]).astype(f32) / gap_energy
     weight = lax.dynamic_slice_in_dim(weight, 8 * lax.axis_index("zl"), 8)
+    scales = jnp.stack([jnp.tile(weight, 16), jnp.full((LANES,), core, f32)])
     values = call(
         spots_kernel,
         (16, 24, LANES),
@@ -231,7 +232,7 @@
         block,
         table,
         phase,
-        jnp.tile(weight, 16)[None],
+        scales,
     )
 
     values = lax.all_to_all(values, ("zl", "zh"), 0, 0, tiled=True)
@@ -242,7 +243,7 @@
         bf16,
         [],
         values,
-        jnp.full((1, LANES), core, f32),
+        scales,
     )
     columns = lax.all_to_all(cols, ("y", "x"), 0, 0, tiled=True)
     return call(

time: 97.5 us -> 96.5 us (0.990)
  blocking collectives: 43.9 us -> 62.3 us
  waiting for transfers between devices: 23.4 us -> 10.9 us
  starting transfers between devices: 17 us -> 10.2 us
    all_to_all x0 -> x1, blocking collectives: none -> 18.5 us  [shards(): values = lax.all_to_all(values, ('zl', 'zh'), 0, 0, tiled=True)]
    all_to_all x1 -> x0, waiting for transfers between devices: 12 us -> none  [shards(): values = lax.all_to_all(values, ('zl', 'zh'), 0, 0, tiled=True)]
    all_to_all x1 -> x0, starting transfers between devices: 6.65 us -> none  [shards(): values = lax.all_to_all(values, ('zl', 'zh'), 0, 0, tiled=True)]
    all_to_all x1, waiting for transfers between devices: 7.2 us -> 5.3 us  [shards(): block = lax.all_to_all(half, ('y', 'x'), 0, 0, tiled=True)]
    all_to_all x1, waiting for transfers between devices: 4.18 us -> 5.64 us  [shards(): pairs = lax.all_to_all(pairs, 'zl', 0, 0, tiled=True)]
  transfers between devices with their start and end apart: 3 -> 2, of which waited for: 3 -> 2; matrix products, arithmetic and copies ran while one was open for 2% -> 2% of each run, Pallas kernels for 0% -> 0%
where the time goes in v6:
time: 96.5 us; the launch traced here: 95.9 us
  blocking collectives  62.3 us (65%)
  waiting for transfers between devices  10.9 us (11%)
  starting transfers between devices  10.2 us (11%)
  Pallas kernels  5.26 us (5%)
  local copies, waits for them, and re-layouts  4.02 us (4%)
  other arithmetic  1.56 us (2%)
    all_to_all x1, blocking collectives, shards(): values = lax.all_to_all(values, ('zl', 'zh'), 0, 0, tiled=True)  18.5 us
    psum x1, blocking collectives, shards(): v = lax.psum(both[0] + both[1], 'zh')  14 us
    all_to_all x1, blocking collectives, shards(): columns = lax.all_to_all(cols, ('y', 'x'), 0, 0, tiled=True)  13.7 us
    all_gather x1, blocking collectives, shards(): both = lax.all_gather(own, 'c')  8.37 us
    all_gather x1, blocking collectives, shards(): values = lax.all_gather(values, 'c')  7.8 us
    all_to_all x1, starting transfers between devices, shards(): block = lax.all_to_all(half, ('y', 'x'), 0, 0, tiled=True)  6.75 us
    all_to_all x1, waiting for transfers between devices, shards(): pairs = lax.all_to_all(pairs, 'zl', 0, 0, tiled=True)  5.64 us
    all_to_all x1, waiting for transfers between devices, shards(): block = lax.all_to_all(half, ('y', 'x'), 0, 0, tiled=True)  5.3 us
  transfers between devices with their start and end apart: 2, of which 2 were waited for; matrix products, arithmetic and copies ran while one was open for 2% of the time, Pallas kernels for 0%

profile of v6, /device:TPU:1, one launch (start us, length us, event | category | flops | bytes accessed | tf_op | source)
XLA Modules:
  0.0 95.9 jit_solution(12766082337876138816)
XLA Ops:
  0.7 0.9 fusion
  1.6 8.4 %all_gather.9 = bf16[2,32,128]{2,1,0:T(8,128)(2,1)S(1)} all-gather(bf16[1,32,128]{2,1,0:T(8,128)(2,1)S(1)} %bitcast.33), channel_id=1, replica_groups=mesh['y'=4,'zl'=4,'x'=4,'zh'=4,'c'=2] {'c'}, dimensions={0}, use_global_device_ids=true | all-gather | bytes 24576 | tf_op jit(solution)/shard_map/all_gather | solution.py:191
  10.0 14.0 %psum.7.v_ref = bf16[32,128]{1,0:T(8,128)(2,1)S(1)} all-reduce(bf16[32,128]{1,0:T(8,128)(2,1)S(1)} %fusion.1), channel_id=1, replica_groups=mesh['y'=4,'zl'=4,'x'=4,'zh'=4,'c'=2] {'zh'}, use_global_device_ids=true, to_apply=%region_0.1 | all-reduce | flops 4096 | bytes 16384 | tf_op jit(solution)/shard_map/psum | solution.py:192
  23.9 0.0 copy-start.2
  23.9 0.0 copy-start.3
  24.0 0.6 copy-done.2
  24.6 0.0 copy-done.3
  24.6 0.0 copy-start
  24.6 0.9 copy-done
  25.6 0.8 shard_map.109
  26.3 3.4 %all-to-all-start = ((bf16[4,8,4224]{2,1,0:T(8,128)(2,1)}), bf16[4,8,4224]{2,1,0:T(8,128)(2,1)S(1)}, u32[]{:S(2)}, u32[]{:S(2)}) async-start(bf16[4,8,4224]{2,1,0:T(8,128)(2,1)} %bitcast.5), calls=%async_computation | async-start | bytes 540672 | tf_op jit(solution)/shard_map/all_to_all | solution.py:205
  29.8 0.0 copy-start.1
  29.8 5.6 %all-to-all-done = bf16[4,8,4224]{2,1,0:T(8,128)(2,1)S(1)} async-done(((bf16[4,8,4224]{2,1,0:T(8,128)(2,1)}), bf16[4,8,4224]{2,1,0:T(8,128)(2,1)S(1)}, u32[]{:S(2)}, u32[]{:S(2)}) %all-to-all-start) | async-done | bytes 270368 | tf_op jit(solution)/shard_map/all_to_all | solution.py:205
  35.5 0.0 copy-done.1
  35.5 1.5 %shard_map.110 = bf16[16,128,128]{2,1,0:T(8,128)(2,1)} custom-call(bf16[32,4224]{1,0:T(8,128)(2,1)S(1)} %bitcast.29, bf16[128,32]{1,0:T(8,128)(2,1)S(1)} %copy-done.1), custom_call_target="tpu_custom_call" | custom-call | tf_op jit(solution)/shard_map/pallas_call | solution.py:173
  37.0 6.7 %all-to-all-start.1 = ((bf16[16,128,128]{2,1,0:T(8,128)(2,1)}), bf16[16,128,128]{2,1,0:T(8,128)(2,1)S(1)}, u32[]{:S(2)}, u32[]{:S(2)}) async-start(bf16[16,128,128]{2,1,0:T(8,128)(2,1)} %shard_map.110), calls=%async_computation.1 | async-start | bytes 1048576 | tf_op jit(solution)/shard_map/all_to_all | solution.py:217
  43.8 0.0 copy-start.8
  43.8 0.0 copy-start.5
  43.8 0.1 iota_compare_fusion
  43.9 0.5 copy-done.8
  44.5 0.6 dynamic_slice.11
  45.0 0.0 copy-start.6
  45.0 0.0 copy-start.7
  45.0 0.7 copy-done.6
  45.7 0.0 copy-done.7
  45.7 0.6 multiply_divide_fusion
  46.3 0.1 dynamic_slice.12
  46.4 0.1 stack_tile.3
  46.5 0.0 copy-done.5
  46.5 0.0 copy-start.4
  46.5 0.3 convolution_convert_fusion.1.e_ref
  46.8 0.4 copy-done.4
  47.2 0.3 convolution_convert_fusion.p_ref
  47.6 5.3 %all-to-all-done.1.r_ref = bf16[16,128,128]{2,1,0:T(8,128)(2,1)S(1)} async-done(((bf16[16,128,128]{2,1,0:T(8,128)(2,1)}), bf16[16,128,128]{2,1,0:T(8,128)(2,1)S(1)}, u32[]{:S(2)}, u32[]{:S(2)}) %all-to-all-start.1) | async-done | bytes 524320 | tf_op jit(solution)/shard_map/all_to_all | solution.py:217
  52.9 1.4 %shard_map.111 = bf16[16,24,128]{2,1,0:T(8,128)(2,1)S(1)} custom-call(bf16[16,128,128]{2,1,0:T(8,128)(2,1)S(1)} %all-to-all-done.1.r_ref, bf16[4,192,256]{2,1,0:T(8,128)(2,1)S(1)} %convolution_convert_fusion.1.e_ref, bf16[4,192,256]{2,1,0:T(8,128)(2,1)S(1)} %convolution_convert_fusion.p_ref, f32[2,128]{1,0:T(2,128)S(1)} %stack.3.w_ref.core_ref), custom_call_target="tpu_custom_call" | custom-call | tf_op jit(solution)/shard_map/pallas_call | solution.py:173
  54.3 18.5 %all_to_all.20 = bf16[16,24,128]{2,1,0:T(8,128)(2,1)S(1)} all-to-all(bf16[16,24,128]{2,1,0:T(8,128)(2,1)S(1)} %shard_map.111), channel_id=1, replica_groups=mesh['y'=4,'zl'=4,'x'=4,'zh'=4,'c'=2] {'zl','zh'}, dimensions={0} | all-to-all | bytes 196608 | tf_op jit(solution)/shard_map/all_to_all | solution.py:238
  72.8 7.8 %all-gather = bf16[32,24,128]{2,1,0:T(8,128)(2,1)S(1)} all-gather(bf16[16,24,128]{2,1,0:T(8,128)(2,1)S(1)} %all_to_all.20), channel_id=2, replica_groups=mesh['y'=4,'zl'=4,'x'=4,'zh'=4,'c'=2] {'c'}, dimensions={0}, use_global_device_ids=true | all-gather | bytes 294912 | tf_op jit(solution)/shard_map/all_gather | solution.py:239
  80.6 0.2 shard_map.112
  80.8 13.7 %all_to_all.21.b_ref = bf16[16,128,128]{2,1,0:T(8,128)(2,1)S(1)} all-to-all(bf16[16,128,128]{2,1,0:T(8,128)(2,1)S(1)} %shard_map.112), channel_id=1, replica_groups=mesh['y'=4,'zl'=4,'x'=4,'zh'=4,'c'=2] {'y','x'}, dimensions={0} | all-to-all | bytes 1048576 | tf_op jit(solution)/shard_map/all_to_all | solution.py:248
  94.6 1.3 %shard_map.113 = f32[2,128,512]{2,1,0:T(8,128)} custom-call(bf16[2,16,24,128]{3,2,1,0:T(8,128)(2,1)S(1)} %bitcast.28, bf16[16,128,128]{2,1,0:T(8,128)(2,1)S(1)} %all_to_all.21.b_ref), custom_call_target="tpu_custom_call" | custom-call | tf_op jit(solution)/shard_map/pallas_call | solution.py:173
  (7 shorter events, 0.0 us)
Async XLA Ops:
  23.9 0.7 copy-start.2
  23.9 0.7 copy-start.3
  24.6 0.9 copy-start
  26.3 9.1 %all-to-all-start = ((bf16[4,8,4224]{2,1,0:T(8,128)(2,1)}), bf16[4,8,4224]{2,1,0:T(8,128)(2,1)S(1)}, u32[]{:S(2)}, u32[]{:S(2)}) async-start(bf16[4,8,4224]{2,1,0:T(8,128)(2,1)} %bitcast.5), calls=%async_computation | async-start | bytes 540672 | tf_op jit(solution)/shard_map/all_to_all | solution.py:205
  29.8 5.7 %copy-start.1 = (bf16[128,32]{1,0:T(8,128)(2,1)S(1)}, bf16[128,32]{1,0:T(8,128)(2,1)}, u32[]{:S(2)}) copy-start(bf16[128,32]{1,0:T(8,128)(2,1)} %constant.68.e_ref) | copy-start | bytes 24580
  37.0 15.9 %all-to-all-start.1 = ((bf16[16,128,128]{2,1,0:T(8,128)(2,1)}), bf16[16,128,128]{2,1,0:T(8,128)(2,1)S(1)}, u32[]{:S(2)}, u32[]{:S(2)}) async-start(bf16[16,128,128]{2,1,0:T(8,128)(2,1)} %shard_map.110), calls=%async_computation.1 | async-start | bytes 1048576 | tf_op jit(solution)/shard_map/all_to_all | solution.py:217
  43.8 0.7 copy-start.8
  43.8 2.7 %copy-start.5 = (bf16[64,256,1]{1,0,2:T(8,128)(2,1)S(1)}, bf16[64,256,1]{1,0,2:T(8,128)(2,1)}, u32[]{:S(2)}) copy-start(bf16[64,256,1]{1,0,2:T(8,128)(2,1)} %constant.71) | copy-start | bytes 98308
  45.0 0.7 copy-start.6
  45.0 0.7 copy-start.7
  46.5 0.8 copy-start.4

commit v7 on v6

--- a/solution.py
+++ b/solution.py
@@ -55,7 +55,7 @@
     return np.concatenate([wave(turn), wave(turn - 16)], axis=1)
 
 
-def pair_kernel(v_ref, c_ref, row_ref, col_ref, out_ref):
+def pair_kernel(v_ref, c_ref, row_ref, col_ref, e_ref, out_ref):
     v = v_ref[...].astype(f32)
     for i in range(N // 2):
         lanes = pl.ds(i * LANES, LANES)
@@ -115,7 +115,7 @@
         cols = cols[:8] + pltpu.roll(cols[8:], N, 1)
         for g in range(4):
             block = [rows[16 * g : 16 * g + 16], cols]
-            out_ref[4 * g + q] = jnp.concatenate(block, axis=0).astype(bf16)
+            out_ref[4 * q + g] = jnp.concatenate(block, axis=0).astype(bf16)
 
 
 def columns_kernel(v_ref, core_ref, out_ref):
@@ -124,7 +124,7 @@
     rows = [jnp.zeros((32, LANES), f32)] * 4
     for s in range(8):
         core, zl = s // 4, s % 4
-        cols = [v_ref[core, 4 * zl + q].astype(f32)[16:] for q in range(4)]
+        cols = [v_ref[core, 4 * q + zl].astype(f32)[16:] for q in range(4)]
         cols = jnp.concatenate(cols, axis=0)
         cols = jnp.where(second, pltpu.roll(cols, N, 1), cols)
         for g in range(4):
@@ -144,7 +144,7 @@
     real_lane = lane_index((ROWS, LANES)) % 16 < 8
     upper, lower = [], []
     for q in range(4):
-        rows = [a_ref[s // 4, 4 * (s % 4) + q].astype(f32)[:16] for s in range(8)]
+        rows = [a_ref[s // 4, 4 * q + s % 4].astype(f32)[:16] for s in range(8)]
         rows = jnp.concatenate(rows, axis=0).T
         turned = jnp.where(real_lane, pltpu.roll(rows, LANES - 8, 1), -pltpu.roll(rows, 8, 1))
         upper.append(rows.astype(bf16))
@@ -185,12 +185,12 @@
 ):
     chosen = band_index[0]
     core = lax.axis_index("c")
-    mine = chosen // valence.shape[0] == lax.axis_index(COL)
-    own = lax.dynamic_index_in_dim(valence, chosen % valence.shape[0], 0, keepdims=False)
-    own = jnp.where(mine, own, 0).astype(bf16).reshape(32, LANES)
-    both = lax.all_gather(own, "c")
-    v = lax.psum(both[0] + both[1], "zh")
-
+    local = lax.all_gather(valence.reshape(-1, N * N), "c", tiled=True)
+    own = lax.dynamic_index_in_dim(local, chosen % local.shape[0], 0, keepdims=False)
+    own = jnp.where(chosen // local.shape[0] == lax.axis_index("zh"), own, 0)
+    v = lax.psum(own.astype(bf16).reshape(32, LANES), "zh")
+
+    table_y = jnp.asarray(y_table()).astype(bf16)
     pairs = call(
         pair_kernel,
         (BANDS, N * N + LANES),
@@ -200,6 +200,7 @@
         conduction.reshape(BANDS, N * N),
         row_map[None],
         col_map[None],
+        table_y,
     )
     pairs = pairs.reshape(4, 8, N * N + LANES)
     pairs = lax.all_to_all(pairs, "zl", 0, 0, tiled=True)
@@ -212,7 +213,7 @@
         bf16,
         [pltpu.VMEM((BANDS * WIDE, LANES), f32), pltpu.VMEM((N * WIDE, LANES), f32)],
         pairs.reshape(BANDS, N * N + LANES),
-        jnp.asarray(y_table()).astype(bf16),
+        table_y,
     )
     block = lax.all_to_all(half, ("y", "x"), 0, 0, tiled=True)
 
@@ -235,7 +236,7 @@
         scales,
     )
 
-    values = lax.all_to_all(values, ("zl", "zh"), 0, 0, tiled=True)
+    values = lax.all_to_all(values, ("zh", "zl"), 0, 0, tiled=True)
     values = lax.all_gather(values, "c")
     cols = call(
         columns_kernel,

time: 96.5 us -> 94.7 us (0.981)
  local copies, waits for them, and re-layouts: 4.02 us -> 3.05 us
    unnamed x18, local copies, waits for them, and re-layouts: 3.25 us -> 2.28 us
where the time goes in v7:
time: 94.7 us; the launch traced here: 94.1 us
  blocking collectives  62.3 us (66%)
  waiting for transfers between devices  11 us (12%)
  starting transfers between devices  10.2 us (11%)
  Pallas kernels  5.29 us (6%)
  local copies, waits for them, and re-layouts  3.05 us (3%)
    all_to_all x1, blocking collectives, shards(): values = lax.all_to_all(values, ('zh', 'zl'), 0, 0, tiled=True)  18.3 us
    psum x1, blocking collectives, shards(): v = lax.psum(own.astype(bf16).reshape(32, LANES), 'zh')  14 us
    all_to_all x1, blocking collectives, shards(): columns = lax.all_to_all(cols, ('y', 'x'), 0, 0, tiled=True)  13.5 us
    all_gather x1, blocking collectives, shards(): local = lax.all_gather(valence.reshape(-1, N * N), 'c', tiled=True)  8.72 us
    all_gather x1, blocking collectives, shards(): values = lax.all_gather(values, 'c')  7.87 us
    all_to_all x1, starting transfers between devices, shards(): block = lax.all_to_all(half, ('y', 'x'), 0, 0, tiled=True)  6.77 us
    all_to_all x1, waiting for transfers between devices, shards(): pairs = lax.all_to_all(pairs, 'zl', 0, 0, tiled=True)  5.66 us
    all_to_all x1, waiting for transfers between devices, shards(): block = lax.all_to_all(half, ('y', 'x'), 0, 0, tiled=True)  5.3 us
  transfers between devices with their start and end apart: 2, of which 2 were waited for; matrix products, arithmetic and copies ran while one was open for 2% of the time, Pallas kernels for 0%

profile of v7, /device:TPU:1, one launch (start us, length us, event | category | flops | bytes accessed | tf_op | source)
XLA Modules:
  0.0 94.1 jit_solution(12812085462982922548)
XLA Ops:
  0.0 0.0 copy-start
  0.7 8.7 %all-gather = bf16[32,1,4096]{2,0,1:T(8,128)(2,1)S(1)} all-gather(bf16[16,1,4096]{2,0,1:T(8,128)(2,1)} %param.11), channel_id=2, replica_groups=mesh['y'=4,'zl'=4,'x'=4,'zh'=4,'c'=2] {'c'}, dimensions={0}, use_global_device_ids=true | all-gather | bytes 393216 | tf_op jit(solution)/shard_map/all_gather | solution.py:188
  9.5 0.0 copy-start.1
  9.5 0.1 fusion
  9.5 14.0 %psum.7.v_ref = bf16[32,128]{1,0:T(8,128)(2,1)S(1)} all-reduce(bf16[32,128]{1,0:T(8,128)(2,1)S(1)} %bitcast.31), channel_id=1, replica_groups=mesh['y'=4,'zl'=4,'x'=4,'zh'=4,'c'=2] {'zh'}, use_global_device_ids=true, to_apply=%region_0.1 | all-reduce | flops 4096 | bytes 16384 | tf_op jit(solution)/shard_map/psum | solution.py:191
  23.5 0.0 copy-start.2
  23.5 0.0 copy-start.3
  23.6 0.0 copy-done
  23.6 0.0 copy-done.1
  23.6 0.6 copy-done.2
  24.2 0.0 copy-done.3
  24.2 0.8 shard_map.109
  25.0 3.4 %all-to-all-start = ((bf16[4,8,4224]{2,1,0:T(8,128)(2,1)}), bf16[4,8,4224]{2,1,0:T(8,128)(2,1)S(1)}, u32[]{:S(2)}, u32[]{:S(2)}) async-start(bf16[4,8,4224]{2,1,0:T(8,128)(2,1)} %bitcast.4), calls=%async_computation | async-start | bytes 540672 | tf_op jit(solution)/shard_map/all_to_all | solution.py:206
  28.5 5.7 %all-to-all-done = bf16[4,8,4224]{2,1,0:T(8,128)(2,1)S(1)} async-done(((bf16[4,8,4224]{2,1,0:T(8,128)(2,1)}), bf16[4,8,4224]{2,1,0:T(8,128)(2,1)S(1)}, u32[]{:S(2)}, u32[]{:S(2)}) %all-to-all-start) | async-done | bytes 270368 | tf_op jit(solution)/shard_map/all_to_all | solution.py:206
  34.1 1.5 %shard_map.110 = bf16[16,128,128]{2,1,0:T(8,128)(2,1)} custom-call(bf16[32,4224]{1,0:T(8,128)(2,1)S(1)} %bitcast.27, bf16[128,32]{1,0:T(8,128)(2,1)S(1)} %copy-done.1), custom_call_target="tpu_custom_call" | custom-call | tf_op jit(solution)/shard_map/pallas_call | solution.py:173
  35.7 6.8 %all-to-all-start.1 = ((bf16[16,128,128]{2,1,0:T(8,128)(2,1)}), bf16[16,128,128]{2,1,0:T(8,128)(2,1)S(1)}, u32[]{:S(2)}, u32[]{:S(2)}) async-start(bf16[16,128,128]{2,1,0:T(8,128)(2,1)} %shard_map.110), calls=%async_computation.1 | async-start | bytes 1048576 | tf_op jit(solution)/shard_map/all_to_all | solution.py:218
  42.5 0.0 copy-start.8
  42.5 0.0 copy-start.5
  42.5 0.1 iota_compare_fusion
  42.6 0.5 copy-done.8
  43.1 0.6 dynamic_slice.11
  43.7 0.0 copy-start.6
  43.7 0.0 copy-start.7
  43.7 0.7 copy-done.6
  44.3 0.0 copy-done.7
  44.4 0.6 multiply_divide_fusion
  44.9 0.1 dynamic_slice.12
  45.0 0.1 stack_tile.3
  45.1 0.0 copy-done.5
  45.1 0.0 copy-start.4
  45.1 0.3 convolution_convert_fusion.1.e_ref
  45.5 0.4 copy-done.4
  45.9 0.3 convolution_convert_fusion.p_ref
  46.2 5.3 %all-to-all-done.1.r_ref = bf16[16,128,128]{2,1,0:T(8,128)(2,1)S(1)} async-done(((bf16[16,128,128]{2,1,0:T(8,128)(2,1)}), bf16[16,128,128]{2,1,0:T(8,128)(2,1)S(1)}, u32[]{:S(2)}, u32[]{:S(2)}) %all-to-all-start.1) | async-done | bytes 524320 | tf_op jit(solution)/shard_map/all_to_all | solution.py:218
  51.5 1.4 %shard_map.111 = bf16[16,24,128]{2,1,0:T(8,128)(2,1)S(1)} custom-call(bf16[16,128,128]{2,1,0:T(8,128)(2,1)S(1)} %all-to-all-done.1.r_ref, bf16[4,192,256]{2,1,0:T(8,128)(2,1)S(1)} %convolution_convert_fusion.1.e_ref, bf16[4,192,256]{2,1,0:T(8,128)(2,1)S(1)} %convolution_convert_fusion.p_ref, f32[2,128]{1,0:T(2,128)S(1)} %stack.3.w_ref.core_ref), custom_call_target="tpu_custom_call" | custom-call | tf_op jit(solution)/shard_map/pallas_call | solution.py:173
  53.0 18.3 %all_to_all.20 = bf16[16,24,128]{2,1,0:T(8,128)(2,1)S(1)} all-to-all(bf16[16,24,128]{2,1,0:T(8,128)(2,1)S(1)} %shard_map.111), channel_id=1, replica_groups=mesh['y'=4,'zl'=4,'x'=4,'zh'=4,'c'=2] {'zh','zl'}, dimensions={0} | all-to-all | bytes 196608 | tf_op jit(solution)/shard_map/all_to_all | solution.py:239
  71.2 7.9 %all-gather.1 = bf16[32,24,128]{2,1,0:T(8,128)(2,1)S(1)} all-gather(bf16[16,24,128]{2,1,0:T(8,128)(2,1)S(1)} %all_to_all.20), channel_id=3, replica_groups=mesh['y'=4,'zl'=4,'x'=4,'zh'=4,'c'=2] {'c'}, dimensions={0}, use_global_device_ids=true | all-gather | bytes 294912 | tf_op jit(solution)/shard_map/all_gather | solution.py:240
  79.1 0.2 shard_map.112
  79.3 13.5 %all_to_all.21.b_ref = bf16[16,128,128]{2,1,0:T(8,128)(2,1)S(1)} all-to-all(bf16[16,128,128]{2,1,0:T(8,128)(2,1)S(1)} %shard_map.112), channel_id=1, replica_groups=mesh['y'=4,'zl'=4,'x'=4,'zh'=4,'c'=2] {'y','x'}, dimensions={0} | all-to-all | bytes 1048576 | tf_op jit(solution)/shard_map/all_to_all | solution.py:249
  92.8 1.3 %shard_map.113 = f32[2,128,512]{2,1,0:T(8,128)} custom-call(bf16[2,16,24,128]{3,2,1,0:T(8,128)(2,1)S(1)} %bitcast.26, bf16[16,128,128]{2,1,0:T(8,128)(2,1)S(1)} %all_to_all.21.b_ref), custom_call_target="tpu_custom_call" | custom-call | tf_op jit(solution)/shard_map/pallas_call | solution.py:173
  (6 shorter events, 0.0 us)
Async XLA Ops:
  0.0 23.6 %copy-start = (bf16[32,1,4096]{2,0,1:T(8,128)(2,1)S(1)}, bf16[32,1,4096]{2,0,1:T(8,128)(2,1)}, u32[]{:S(2)}) copy-start(bf16[32,1,4096]{2,0,1:T(8,128)(2,1)} %param.12) | copy-start | bytes 786436
  9.5 14.1 %copy-start.1 = (bf16[128,32]{1,0:T(8,128)(2,1)S(1)}, bf16[128,32]{1,0:T(8,128)(2,1)}, u32[]{:S(2)}) copy-start(bf16[128,32]{1,0:T(8,128)(2,1)} %constant.64.e_ref) | copy-start | bytes 24580
  23.5 0.7 copy-start.2
  23.5 0.7 copy-start.3
  25.0 9.1 %all-to-all-start = ((bf16[4,8,4224]{2,1,0:T(8,128)(2,1)}), bf16[4,8,4224]{2,1,0:T(8,128)(2,1)S(1)}, u32[]{:S(2)}, u32[]{:S(2)}) async-start(bf16[4,8,4224]{2,1,0:T(8,128)(2,1)} %bitcast.4), calls=%async_computation | async-start | bytes 540672 | tf_op jit(solution)/shard_map/all_to_all | solution.py:206
  35.7 15.9 %all-to-all-start.1 = ((bf16[16,128,128]{2,1,0:T(8,128)(2,1)}), bf16[16,128,128]{2,1,0:T(8,128)(2,1)S(1)}, u32[]{:S(2)}, u32[]{:S(2)}) async-start(bf16[16,128,128]{2,1,0:T(8,128)(2,1)} %shard_map.110), calls=%async_computation.1 | async-start | bytes 1048576 | tf_op jit(solution)/shard_map/all_to_all | solution.py:218
  42.5 0.7 copy-start.8
  42.5 2.7 %copy-start.5 = (bf16[64,256,1]{1,0,2:T(8,128)(2,1)S(1)}, bf16[64,256,1]{1,0,2:T(8,128)(2,1)}, u32[]{:S(2)}) copy-start(bf16[64,256,1]{1,0,2:T(8,128)(2,1)} %constant.68) | copy-start | bytes 98308
  43.7 0.7 copy-start.6
  43.7 0.7 copy-start.7
  45.1 0.8 copy-start.4

commit v8 on v7

--- a/solution.py
+++ b/solution.py
@@ -44,9 +44,7 @@
 
 def x_table():
     kx = np.arange(N)[:, None]
-    lane = np.arange(LANES)[None, :]
-    plane, imag = lane // 8, lane // 4 % 2
-    x = 16 * (plane // 4) + 4 * (lane % 4) + plane % 4
+    x, imag = np.arange(LANES)[None, :] % N, np.arange(LANES)[None, :] // N
     return np.concatenate([wave(kx * x - 16 * imag), wave(kx * x + 16 * (1 - imag))], axis=1)
 
 
@@ -55,21 +53,12 @@
     return np.concatenate([wave(turn), wave(turn - 16)], axis=1)
 
 
-def pair_kernel(v_ref, c_ref, row_ref, col_ref, e_ref, out_ref):
+def pair_y_kernel(v_ref, c_ref, e_ref, out_ref, by_row, by_ky):
     v = v_ref[...].astype(f32)
     for i in range(N // 2):
-        lanes = pl.ds(i * LANES, LANES)
-        out_ref[:, lanes] = (c_ref[:, lanes].astype(f32) * v[i : i + 1, :]).astype(bf16)
-    row = row_ref[...]
-    col = jnp.concatenate([col_ref[...]] * 2, axis=1)
-    spots = [row >> 6, row & (N - 1), col >> 6, col & (N - 1)]
-    spots = jnp.concatenate(spots * 2, axis=0).astype(f32)
-    out_ref[:, N * N :] = jnp.concatenate([spots] * 4, axis=0).astype(bf16)
-
-
-def y_kernel(p_ref, e_ref, out_ref, by_row, by_ky):
-    for i in range(N // 2):
-        by_row[pl.ds(i, BANDS, stride=WIDE), :] = p_ref[:, i * LANES : (i + 1) * LANES].astype(f32)
+        bands = c_ref[:, i * LANES : (i + 1) * LANES].astype(f32)
+        pair = (bands * v[i : i + 1, :]).astype(bf16).astype(f32)
+        by_row[pl.ds(i, BANDS, stride=WIDE), :] = pair
     table = e_ref[...]
     low = lane_index((N, LANES)) < N
     half = N // 2
@@ -80,27 +69,43 @@
         even, odd = both[:N], both[N:]
         even = jnp.where(low, even[:, :LANES], pltpu.roll(even[:, LANES:], N, 1))
         odd = jnp.where(low, pltpu.roll(odd[:, :LANES], N, 1), odd[:, LANES:])
-        at = 8 * (j % 4) + j // 4
-        for start, value in ((at, even + odd), (half * WIDE + at, even - odd)):
+        for start, value in ((2 * j, even + odd), (half * WIDE + 2 * j, even - odd)):
             by_ky[pl.ds(start, half, stride=WIDE), :] = value[:half]
-            by_ky[pl.ds(start + 4, half, stride=WIDE), :] = value[half:]
-    for ky in range(N):
-        y, zl, x = ky // 16, ky // 4 % 4, ky % 4
-        out_ref[4 * y + x, 32 * zl : 32 * zl + 32, :] = by_ky[pl.ds(ky * WIDE, 32), :].astype(bf16)
-
-
-def spots_kernel(r_ref, e_ref, p_ref, w_ref, out_ref):
+            by_ky[pl.ds(start + 1, half, stride=WIDE), :] = value[half:]
+    for place in range(N):
+        first, zl = place // 16 * 16 + place % 4, place // 4 % 4
+        rows = [by_ky[pl.ds((first + 4 * k) * WIDE + 8 * zl, 8), :] for k in range(4)]
+        out_ref[place] = jnp.concatenate(rows, axis=0).astype(bf16)
+
+
+def weight_row(place_ref, occ_v_ref, occ_c_ref, gap_ref):
+    lane = lane_index((1, LANES))
+    chosen = jnp.where(lane == place_ref[0:1, :], occ_v_ref[...], 0).astype(f32)
+    filled = jnp.sum(chosen, axis=1, keepdims=True)
+    weight = 2.0 * (occ_c_ref[...].astype(f32) - filled) / gap_ref[...]
+    band = lax.broadcasted_iota(jnp.int32, (BANDS, LANES), 0)
+    pick = jnp.where(band == place_ref[1:2, :] + lane % 8, 1.0, 0.0)
+    return jnp.dot(weight, pick, precision=lax.Precision.HIGHEST, preferred_element_type=f32)
+
+
+def spots_kernel(
+    r_ref, e_ref, p_ref, place_ref, occ_v_ref, occ_c_ref, gap_ref, out_ref, planes
+):
+    for x in range(N):
+        planes[pl.ds(x * WIDE, 32), :] = r_ref[x].astype(f32)
     column = lane_index((2 * LANES, LANES))
     band = lax.broadcasted_iota(jnp.int32, (2 * LANES, LANES), 0) // N
     total = jnp.zeros((2 * SPOTS, LANES), f32)
     for g in range(4):
-        planes = r_ref[:, 32 * g : 32 * g + 32, :].astype(f32)
         table = jnp.concatenate([e_ref[g, :, :LANES], e_ref[g, :, LANES:]], axis=0)
         cos_z = jnp.concatenate([p_ref[g, :, :LANES].astype(f32)] * 2, axis=1)
         sin_z = jnp.concatenate([p_ref[g, :, LANES:].astype(f32)] * 2, axis=1)
         for h in range(2):
-            first = planes[:, 16 * h : 16 * h + 8, :].reshape(LANES, LANES)
-            second = planes[:, 16 * h + 8 : 16 * h + 16, :].reshape(LANES, LANES)
+            both = []
+            for row in (8 * g + 4 * h, 8 * g + 4 * h + 2):
+                parts = [planes[pl.ds(row + k, N, stride=WIDE), :] for k in range(2)]
+                both.append(jnp.concatenate(parts, axis=0))
+            first, second = both
             at_x = dot(table, jnp.concatenate([first, second], axis=1).astype(bf16))
             real, imag = at_x[:SPOTS], at_x[SPOTS:]
             real_z = real * cos_z + imag * sin_z
@@ -109,22 +114,22 @@
             ones = jnp.where(column == band + 16 * g + 4 * h, 1.0, 0.0).astype(bf16)
             total = total + dot(terms, ones)
     joined = total[:SPOTS] + pltpu.roll(total[SPOTS:], 8, 1)
-    rows = (joined[:ROWS] * w_ref[0:1, :]).T
+    rows = (joined[:ROWS] * weight_row(place_ref, occ_v_ref, occ_c_ref, gap_ref)).T
     for q in range(4):
         cols = joined[ROWS + 16 * q : ROWS + 16 * q + 16]
         cols = cols[:8] + pltpu.roll(cols[8:], N, 1)
         for g in range(4):
-            block = [rows[16 * g : 16 * g + 16], cols]
+            block = [rows[16 * g : 16 * g + 16], cols, jnp.zeros_like(cols)]
             out_ref[4 * q + g] = jnp.concatenate(block, axis=0).astype(bf16)
 
 
 def columns_kernel(v_ref, core_ref, out_ref):
-    second = core_ref[1:2, :] > 0.5
+    second = core_ref[2:3, :] > 0
     group = lane_index((32, LANES)) // 16
     rows = [jnp.zeros((32, LANES), f32)] * 4
     for s in range(8):
         core, zl = s // 4, s % 4
-        cols = [v_ref[core, 4 * q + zl].astype(f32)[16:] for q in range(4)]
+        cols = [v_ref[core, 4 * q + zl, 16:].astype(f32)[:8] for q in range(4)]
         cols = jnp.concatenate(cols, axis=0)
         cols = jnp.where(second, pltpu.roll(cols, N, 1), cols)
         for g in range(4):
@@ -144,7 +149,7 @@
     real_lane = lane_index((ROWS, LANES)) % 16 < 8
     upper, lower = [], []
     for q in range(4):
-        rows = [a_ref[s // 4, 4 * q + s % 4].astype(f32)[:16] for s in range(8)]
+        rows = [a_ref[s // 4, 4 * q + s % 4, :16].astype(f32) for s in range(8)]
         rows = jnp.concatenate(rows, axis=0).T
         turned = jnp.where(real_lane, pltpu.roll(rows, LANES - 8, 1), -pltpu.roll(rows, 8, 1))
         upper.append(rows.astype(bf16))
@@ -190,50 +195,37 @@
     own = jnp.where(chosen // local.shape[0] == lax.axis_index("zh"), own, 0)
     v = lax.psum(own.astype(bf16).reshape(32, LANES), "zh")
 
-    table_y = jnp.asarray(y_table()).astype(bf16)
-    pairs = call(
-        pair_kernel,
-        (BANDS, N * N + LANES),
+    half = call(
+        pair_y_kernel,
+        (N, 32, LANES),
         bf16,
-        [],
+        [pltpu.VMEM((BANDS * WIDE, LANES), f32), pltpu.VMEM((N * WIDE, LANES), f32)],
         v,
         conduction.reshape(BANDS, N * N),
-        row_map[None],
-        col_map[None],
-        table_y,
-    )
-    pairs = pairs.reshape(4, 8, N * N + LANES)
-    pairs = lax.all_to_all(pairs, "zl", 0, 0, tiled=True)
-    late = lax.optimization_barrier((pairs, occ_valence, occ_conduction, gap_energy))
-    pairs, occ_valence, occ_conduction, gap_energy = late
-
-    half = call(
-        y_kernel,
-        (16, ROWS, LANES),
-        bf16,
-        [pltpu.VMEM((BANDS * WIDE, LANES), f32), pltpu.VMEM((N * WIDE, LANES), f32)],
-        pairs.reshape(BANDS, N * N + LANES),
-        table_y,
-    )
-    block = lax.all_to_all(half, ("y", "x"), 0, 0, tiled=True)
-
-    spots = pairs[:, :4, N * N :]
-    spots = jnp.concatenate([spots[:, :2], spots[:, 2:, :COLS]], axis=2)
-    hot = (spots[..., None] == jnp.arange(N, dtype=bf16)).astype(bf16)
-    table = dot(hot[:, 0], jnp.asarray(x_table()).astype(bf16)).astype(bf16)
-    phase = dot(hot[:, 1], jnp.asarray(z_table()).astype(bf16)).astype(bf16)
-    weight = 2.0 * (occ_conduction - occ_valence[chosen]).astype(f32) / gap_energy
-    weight = lax.dynamic_slice_in_dim(weight, 8 * lax.axis_index("zl"), 8)
-    scales = jnp.stack([jnp.tile(weight, 16), jnp.full((LANES,), core, f32)])
+        jnp.asarray(y_table()).astype(bf16),
+    )
+    half, row_map, col_map = lax.optimization_barrier((half, row_map, col_map))
+    block = lax.all_to_all(half, GA, 0, 0, tiled=True)
+
+    spots = jnp.concatenate([row_map, col_map])
+    spots = lax.all_gather(spots, "zl")
+    grid = jnp.arange(N, dtype=jnp.int32)
+    table = dot(((spots >> 6)[..., None] == grid).astype(bf16), jnp.asarray(x_table()).astype(bf16))
+    phase = dot(((spots & 63)[..., None] == grid).astype(bf16), jnp.asarray(z_table()).astype(bf16))
+    places = jnp.stack([chosen, 8 * lax.axis_index("zl"), core])
+    places = jnp.broadcast_to(places[:, None], (3, LANES))
     values = call(
         spots_kernel,
-        (16, 24, LANES),
+        (16, 32, LANES),
         bf16,
-        [],
+        [pltpu.VMEM((N * WIDE, LANES), f32)],
         block,
-        table,
-        phase,
-        scales,
+        table.astype(bf16),
+        phase.astype(bf16),
+        places,
+        occ_valence[None],
+        occ_conduction[None],
+        gap_energy[None],
     )
 
     values = lax.all_to_all(values, ("zh", "zl"), 0, 0, tiled=True)
@@ -244,7 +236,7 @@
         bf16,
         [],
         values,
-        scales,
+        places,
     )
     columns = lax.all_to_all(cols, ("y", "x"), 0, 0, tiled=True)
     return call(

time: 94.7 us -> 93.3 us (0.985)
  blocking collectives: 62.3 us -> 72.2 us
  waiting for transfers between devices: 11 us -> 2.26 us
  starting transfers between devices: 10.2 us -> 9.13 us
    unnamed x0 -> x1, blocking collectives: none -> 10.6 us
    all_to_all x2 -> x1, waiting for transfers between devices: 11 us -> 2.26 us  [shards(): block = lax.all_to_all(half, GA, 0, 0, tiled=True)]
    all_gather x1, blocking collectives: 7.87 us -> 6.31 us  [shards(): values = lax.all_gather(values, 'c')]
    all_to_all x2 -> x1, starting transfers between devices: 10.2 us -> 9.13 us  [shards(): block = lax.all_to_all(half, GA, 0, 0, tiled=True)]
    pallas_call x5 -> x4, Pallas kernels: 5.29 us -> 4.36 us  [call(): pl.pallas_call(kernel, out_shape=jax.ShapeDtypeStruct(shape, dtype), in_s...]
    unnamed x18 -> x20, local copies, waits for them, and re-layouts: 2.28 us -> 2.33 us
  transfers between devices with their start and end apart: 2 -> 1, of which waited for: 2 -> 1; matrix products, arithmetic and copies ran while one was open for 2% -> 2% of each run, Pallas kernels for 0% -> 0%
where the time goes in v8:
time: 93.3 us; the launch traced here: 92.8 us
  blocking collectives  72.2 us (77%)
  starting transfers between devices  9.13 us (10%)
  Pallas kernels  4.36 us (5%)
  local copies, waits for them, and re-layouts  2.55 us (3%)
  waiting for transfers between devices  2.26 us (2%)
  between operations  1.41 us (2%)
    all_to_all x1, blocking collectives, shards(): values = lax.all_to_all(values, ('zh', 'zl'), 0, 0, tiled=True)  18.2 us
    all_to_all x1, blocking collectives, shards(): columns = lax.all_to_all(cols, ('y', 'x'), 0, 0, tiled=True)  14.3 us
    psum x1, blocking collectives, shards(): v = lax.psum(own.astype(bf16).reshape(32, LANES), 'zh')  14 us
    unnamed x1, blocking collectives  10.6 us
    all_to_all x1, starting transfers between devices, shards(): block = lax.all_to_all(half, GA, 0, 0, tiled=True)  9.13 us
    all_gather x1, blocking collectives, shards(): local = lax.all_gather(valence.reshape(-1, N * N), 'c', tiled=True)  8.72 us
    all_gather x1, blocking collectives, shards(): values = lax.all_gather(values, 'c')  6.31 us
    pallas_call x4, Pallas kernels, call(): pl.pallas_call(kernel, out_shape=jax.ShapeDtypeStruct(shape, dtype), in_s...  4.36 us
  transfers between devices with their start and end apart: 1, of which 1 were waited for; matrix products, arithmetic and copies ran while one was open for 2% of the time, Pallas kernels for 0%

profile of v8, /device:TPU:1, one launch (start us, length us, event | category | flops | bytes accessed | tf_op | source)
XLA Modules:
  0.0 92.8 jit_solution(14683966875147370162)
XLA Ops:
  0.0 0.0 copy-start
  0.7 8.7 %all-gather = bf16[32,1,4096]{2,0,1:T(8,128)(2,1)S(1)} all-gather(bf16[16,1,4096]{2,0,1:T(8,128)(2,1)} %param.11), channel_id=2, replica_groups=mesh['y'=4,'zl'=4,'x'=4,'zh'=4,'c'=2] {'c'}, dimensions={0}, use_global_device_ids=true | all-gather | bytes 393216 | tf_op jit(solution)/shard_map/all_gather | solution.py:193
  9.5 0.0 copy-start.1
  9.5 0.1 fusion.2
  9.5 14.0 %psum.7.v_ref = bf16[32,128]{1,0:T(8,128)(2,1)S(1)} all-reduce(bf16[32,128]{1,0:T(8,128)(2,1)S(1)} %bitcast.24), channel_id=1, replica_groups=mesh['y'=4,'zl'=4,'x'=4,'zh'=4,'c'=2] {'zh'}, use_global_device_ids=true, to_apply=%region_0.1 | all-reduce | flops 4096 | bytes 16384 | tf_op jit(solution)/shard_map/psum | solution.py:196
  23.5 0.0 copy-done
  23.5 0.0 copy-done.1
  23.6 1.4 %shard_map.109 = bf16[64,32,128]{2,1,0:T(8,128)(2,1)} custom-call(bf16[32,128]{1,0:T(8,128)(2,1)S(1)} %psum.7.v_ref, bf16[32,4096]{1,0:T(8,128)(2,1)S(1)} %bitcast.20, bf16[128,32]{1,0:T(8,128)(2,1)S(1)} %copy-done.1), custom_call_target="tpu_custom_call" | custom-call | tf_op jit(solution)/shard_map/pallas_call | solution.py:178
  25.0 0.0 copy-start.7
  25.0 0.0 copy-start.8
  25.0 9.1 %all-to-all-start = ((bf16[64,32,128]{2,1,0:T(8,128)(2,1)}), bf16[64,32,128]{2,1,0:T(8,128)(2,1)S(1)}, u32[]{:S(2)}, u32[]{:S(2)}) async-start(bf16[64,32,128]{2,1,0:T(8,128)(2,1)} %shard_map.109), calls=%async_computation | async-start | bytes 1048576 | tf_op jit(solution)/shard_map/all_to_all | solution.py:208
  34.1 0.0 copy-start.6
  34.1 1.3 %dynamic-slice.1 = u32[1]{0:T(128)} dynamic-slice(u32[512]{0:T(512)} %constant.68, u32[]{:T(128)S(6)} %add.13), dynamic_slice_sizes={1} | dynamic-slice | bytes 12
  36.0 0.0 copy-done.7
  36.0 0.0 copy-done.8
  36.0 0.1 add_dynamic-update-slice_fusion
  36.1 10.6 %all-reduce = s32[768]{0:T(1024)S(1)} all-reduce(s32[768]{0:T(1024)S(1)} %add_dynamic-update-slice_fusion), channel_id=3, replica_groups=mesh['y'=4,'zl'=4,'x'=4,'zh'=4,'c'=2] {'zl'}, use_global_device_ids=true, to_apply=%add | all-reduce | flops 768 | bytes 6144
  46.7 0.1 reshape.22
  46.8 0.1 reshape.20
  46.9 0.1 pad_add_fusion
  47.0 0.0 copy-done.6
  47.0 0.0 copy-start.5
  47.0 0.3 convolution_convert_fusion.1.e_ref
  47.3 0.4 copy-done.5
  47.7 0.3 convolution_convert_fusion.p_ref
  48.1 2.3 %all-to-all-done.r_ref = bf16[64,32,128]{2,1,0:T(8,128)(2,1)S(1)} async-done(((bf16[64,32,128]{2,1,0:T(8,128)(2,1)}), bf16[64,32,128]{2,1,0:T(8,128)(2,1)S(1)}, u32[]{:S(2)}, u32[]{:S(2)}) %all-to-all-start) | async-done | bytes 524320 | tf_op jit(solution)/shard_map/all_to_all | solution.py:208
  50.3 0.0 copy-start.2
  50.3 0.0 copy-start.3
  50.3 0.0 copy-start.4
  50.3 0.1 broadcast_in_dim.24.place_ref.core_ref
  50.4 0.6 copy-done.2
  51.0 0.0 copy-done.3
  51.0 0.0 copy-done.4
  51.0 1.4 %shard_map.110 = bf16[16,32,128]{2,1,0:T(8,128)(2,1)S(1)} custom-call(bf16[64,32,128]{2,1,0:T(8,128)(2,1)S(1)} %all-to-all-done.r_ref, bf16[4,192,256]{2,1,0:T(8,128)(2,1)S(1)} %convolution_convert_fusion.1.e_ref, bf16[4,192,256]{2,1,0:T(8,128)(2,1)S(1)} %convolution_convert_fusion.p_ref, s32[3,128]{1,0:T(4,128)S(1)} %broadcast_in_dim.24.place_ref.core_ref, ...), custom_call_target="tpu_custom_call" | custom-call | tf_op jit(solution)/shard_map/pallas_call | solution.py:178
  52.4 18.2 %all_to_all.15 = bf16[16,32,128]{2,1,0:T(8,128)(2,1)S(1)} all-to-all(bf16[16,32,128]{2,1,0:T(8,128)(2,1)S(1)} %shard_map.110), channel_id=1, replica_groups=mesh['y'=4,'zl'=4,'x'=4,'zh'=4,'c'=2] {'zh','zl'}, dimensions={0} | all-to-all | bytes 262144 | tf_op jit(solution)/shard_map/all_to_all | solution.py:231
  70.6 6.3 %all-gather.2 = bf16[32,32,128]{2,1,0:T(8,128)(2,1)S(1)} all-gather(bf16[16,32,128]{2,1,0:T(8,128)(2,1)S(1)} %all_to_all.15), channel_id=4, replica_groups=mesh['y'=4,'zl'=4,'x'=4,'zh'=4,'c'=2] {'c'}, dimensions={0}, use_global_device_ids=true | all-gather | bytes 393216 | tf_op jit(solution)/shard_map/all_gather | solution.py:232
  77.0 0.2 shard_map.111
  77.2 14.3 %all_to_all.16.b_ref = bf16[16,128,128]{2,1,0:T(8,128)(2,1)S(1)} all-to-all(bf16[16,128,128]{2,1,0:T(8,128)(2,1)S(1)} %shard_map.111), channel_id=1, replica_groups=mesh['y'=4,'zl'=4,'x'=4,'zh'=4,'c'=2] {'y','x'}, dimensions={0} | all-to-all | bytes 1048576 | tf_op jit(solution)/shard_map/all_to_all | solution.py:241
  91.5 1.3 %shard_map.112 = f32[2,128,512]{2,1,0:T(8,128)} custom-call(bf16[2,16,32,128]{3,2,1,0:T(8,128)(2,1)S(1)} %bitcast.19, bf16[16,128,128]{2,1,0:T(8,128)(2,1)S(1)} %all_to_all.16.b_ref), custom_call_target="tpu_custom_call" | custom-call | tf_op jit(solution)/shard_map/pallas_call | solution.py:178
  (2 shorter events, 0.0 us)
Async XLA Ops:
  0.0 23.5 %copy-start = (bf16[32,1,4096]{2,0,1:T(8,128)(2,1)S(1)}, bf16[32,1,4096]{2,0,1:T(8,128)(2,1)}, u32[]{:S(2)}) copy-start(bf16[32,1,4096]{2,0,1:T(8,128)(2,1)} %param.12) | copy-start | bytes 786436
  9.5 14.1 %copy-start.1 = (bf16[128,32]{1,0:T(8,128)(2,1)S(1)}, bf16[128,32]{1,0:T(8,128)(2,1)}, u32[]{:S(2)}) copy-start(bf16[128,32]{1,0:T(8,128)(2,1)} %constant.62.e_ref) | copy-start | bytes 24580
  25.0 11.0 %copy-start.7 = (s32[64]{0:T(128)S(1)}, s32[64]{0:T(128)}, u32[]{:S(2)}) copy-start(s32[64]{0:T(128)} %param.18) | copy-start | bytes 772
  25.0 11.0 %copy-start.8 = (s32[128]{0:T(128)S(1)}, s32[128]{0:T(128)}, u32[]{:S(2)}) copy-start(s32[128]{0:T(128)} %param.17) | copy-start | bytes 1540
  25.0 25.4 %all-to-all-start = ((bf16[64,32,128]{2,1,0:T(8,128)(2,1)}), bf16[64,32,128]{2,1,0:T(8,128)(2,1)S(1)}, u32[]{:S(2)}, u32[]{:S(2)}) async-start(bf16[64,32,128]{2,1,0:T(8,128)(2,1)} %shard_map.109), calls=%async_computation | async-start | bytes 1048576 | tf_op jit(solution)/shard_map/all_to_all | solution.py:208
  34.1 12.8 %copy-start.6 = (bf16[64,256,1]{1,0,2:T(8,128)(2,1)S(1)}, bf16[64,256,1]{1,0,2:T(8,128)(2,1)}, u32[]{:S(2)}) copy-start(bf16[64,256,1]{1,0,2:T(8,128)(2,1)} %constant.72) | copy-start | bytes 98308
  47.0 0.8 copy-start.5
  50.3 0.7 copy-start.2
  50.3 0.7 copy-start.3
  50.3 0.7 copy-start.4

commit v9 on v8

--- a/solution.py
+++ b/solution.py
@@ -78,19 +78,17 @@
         out_ref[place] = jnp.concatenate(rows, axis=0).astype(bf16)
 
 
-def weight_row(place_ref, occ_v_ref, occ_c_ref, gap_ref):
+def weight_row(fact_ref):
     lane = lane_index((1, LANES))
-    chosen = jnp.where(lane == place_ref[0:1, :], occ_v_ref[...], 0).astype(f32)
+    chosen = jnp.where(lane.astype(f32) == fact_ref[0:1, :], fact_ref[3:4, :], 0.0)
     filled = jnp.sum(chosen, axis=1, keepdims=True)
-    weight = 2.0 * (occ_c_ref[...].astype(f32) - filled) / gap_ref[...]
-    band = lax.broadcasted_iota(jnp.int32, (BANDS, LANES), 0)
-    pick = jnp.where(band == place_ref[1:2, :] + lane % 8, 1.0, 0.0)
+    weight = (2.0 * (fact_ref[4:5, :] - filled) / fact_ref[5:6, :])[:, :BANDS]
+    band = lax.broadcasted_iota(jnp.int32, (BANDS, LANES), 0).astype(f32)
+    pick = jnp.where(band == fact_ref[1:2, :] + (lane % 8).astype(f32), 1.0, 0.0)
     return jnp.dot(weight, pick, precision=lax.Precision.HIGHEST, preferred_element_type=f32)
 
 
-def spots_kernel(
-    r_ref, e_ref, p_ref, place_ref, occ_v_ref, occ_c_ref, gap_ref, out_ref, planes
-):
+def spots_kernel(r_ref, e_ref, p_ref, fact_ref, out_ref, planes):
     for x in range(N):
         planes[pl.ds(x * WIDE, 32), :] = r_ref[x].astype(f32)
     column = lane_index((2 * LANES, LANES))
@@ -114,7 +112,7 @@
             ones = jnp.where(column == band + 16 * g + 4 * h, 1.0, 0.0).astype(bf16)
             total = total + dot(terms, ones)
     joined = total[:SPOTS] + pltpu.roll(total[SPOTS:], 8, 1)
-    rows = (joined[:ROWS] * weight_row(place_ref, occ_v_ref, occ_c_ref, gap_ref)).T
+    rows = (joined[:ROWS] * weight_row(fact_ref)).T
     for q in range(4):
         cols = joined[ROWS + 16 * q : ROWS + 16 * q + 16]
         cols = cols[:8] + pltpu.roll(cols[8:], N, 1)
@@ -123,8 +121,8 @@
             out_ref[4 * q + g] = jnp.concatenate(block, axis=0).astype(bf16)
 
 
-def columns_kernel(v_ref, core_ref, out_ref):
-    second = core_ref[2:3, :] > 0
+def columns_kernel(v_ref, fact_ref, out_ref):
+    second = fact_ref[2:3, :] > 0.5
     group = lane_index((32, LANES)) // 16
     rows = [jnp.zeros((32, LANES), f32)] * 4
     for s in range(8):
@@ -204,16 +202,20 @@
         conduction.reshape(BANDS, N * N),
         jnp.asarray(y_table()).astype(bf16),
     )
-    half, row_map, col_map = lax.optimization_barrier((half, row_map, col_map))
+    late = (half, row_map, col_map, occ_valence, occ_conduction, gap_energy)
+    late = lax.optimization_barrier(late)
+    half, row_map, col_map, occ_valence, occ_conduction, gap_energy = late
     block = lax.all_to_all(half, GA, 0, 0, tiled=True)
 
-    spots = jnp.concatenate([row_map, col_map])
-    spots = lax.all_gather(spots, "zl")
+    mine = (jnp.arange(4) == lax.axis_index("zl"))[:, None]
+    spots = jnp.where(mine, jnp.concatenate([row_map, col_map])[None], 0)
+    spots = lax.psum(spots, "zl")
     grid = jnp.arange(N, dtype=jnp.int32)
     table = dot(((spots >> 6)[..., None] == grid).astype(bf16), jnp.asarray(x_table()).astype(bf16))
     phase = dot(((spots & 63)[..., None] == grid).astype(bf16), jnp.asarray(z_table()).astype(bf16))
-    places = jnp.stack([chosen, 8 * lax.axis_index("zl"), core])
-    places = jnp.broadcast_to(places[:, None], (3, LANES))
+    facts = [chosen, 8 * lax.axis_index("zl"), core]
+    facts = [jnp.full((LANES,), fact) for fact in facts] + [occ_valence, jnp.tile(occ_conduction, 4)]
+    facts = jnp.stack([fact.astype(f32) for fact in facts] + [jnp.tile(gap_energy, 4)])
     values = call(
         spots_kernel,
         (16, 32, LANES),
@@ -222,10 +224,7 @@
         block,
         table.astype(bf16),
         phase.astype(bf16),
-        places,
-        occ_valence[None],
-        occ_conduction[None],
-        gap_energy[None],
+        facts,
     )
 
     values = lax.all_to_all(values, ("zh", "zl"), 0, 0, tiled=True)
@@ -236,7 +235,7 @@
         bf16,
         [],
         values,
-        places,
+        facts,
     )
     columns = lax.all_to_all(cols, ("y", "x"), 0, 0, tiled=True)
     return call(

time: 93.3 us -> 92.4 us (level)
    psum x0 -> x1, blocking collectives: none -> 11.2 us  [shards(): spots = lax.psum(spots, 'zl')]
    unnamed x1 -> x0, blocking collectives: 10.6 us -> none
    unnamed x20 -> x18, local copies, waits for them, and re-layouts: 2.33 us -> 1.51 us
  transfers between devices with their start and end apart: 1 -> 1, of which waited for: 1 -> 1; matrix products, arithmetic and copies ran while one was open for 2% -> 1% of each run, Pallas kernels for 0% -> 0%
where the time goes in v9:
time: 92.4 us; the launch traced here: 91.9 us
  blocking collectives  72.5 us (78%)
  starting transfers between devices  9.13 us (10%)
  Pallas kernels  4.36 us (5%)
  waiting for transfers between devices  2.5 us (3%)
  local copies, waits for them, and re-layouts  1.71 us (2%)
    all_to_all x1, blocking collectives, shards(): values = lax.all_to_all(values, ('zh', 'zl'), 0, 0, tiled=True)  18.2 us
    all_to_all x1, blocking collectives, shards(): columns = lax.all_to_all(cols, ('y', 'x'), 0, 0, tiled=True)  14.1 us
    psum x1, blocking collectives, shards(): v = lax.psum(own.astype(bf16).reshape(32, LANES), 'zh')  14 us
    psum x1, blocking collectives, shards(): spots = lax.psum(spots, 'zl')  11.2 us
    all_to_all x1, starting transfers between devices, shards(): block = lax.all_to_all(half, GA, 0, 0, tiled=True)  9.13 us
    all_gather x1, blocking collectives, shards(): local = lax.all_gather(valence.reshape(-1, N * N), 'c', tiled=True)  8.72 us
    all_gather x1, blocking collectives, shards(): values = lax.all_gather(values, 'c')  6.31 us
    pallas_call x4, Pallas kernels, call(): pl.pallas_call(kernel, out_shape=jax.ShapeDtypeStruct(shape, dtype), in_s...  4.36 us
  transfers between devices with their start and end apart: 1, of which 1 were waited for; matrix products, arithmetic and copies ran while one was open for 1% of the time, Pallas kernels for 0%

profile of v9, /device:TPU:1, one launch (start us, length us, event | category | flops | bytes accessed | tf_op | source)
XLA Modules:
  0.0 91.9 jit_solution(9163299597548712798)
XLA Ops:
  0.0 0.0 copy-start
  0.7 8.7 %all-gather = bf16[32,1,4096]{2,0,1:T(8,128)(2,1)S(1)} all-gather(bf16[16,1,4096]{2,0,1:T(8,128)(2,1)} %param.11), channel_id=2, replica_groups=mesh['y'=4,'zl'=4,'x'=4,'zh'=4,'c'=2] {'c'}, dimensions={0}, use_global_device_ids=true | all-gather | bytes 393216 | tf_op jit(solution)/shard_map/all_gather | solution.py:191
  9.5 0.0 copy-start.1
  9.5 0.1 fusion.2
  9.5 14.0 %psum.14.v_ref = bf16[32,128]{1,0:T(8,128)(2,1)S(1)} all-reduce(bf16[32,128]{1,0:T(8,128)(2,1)S(1)} %bitcast.18), channel_id=1, replica_groups=mesh['y'=4,'zl'=4,'x'=4,'zh'=4,'c'=2] {'zh'}, use_global_device_ids=true, to_apply=%region_0.1 | all-reduce | flops 4096 | bytes 16384 | tf_op jit(solution)/shard_map/psum | solution.py:194
  23.5 0.0 copy-done
  23.5 0.0 copy-done.1
  23.5 1.4 %shard_map.109 = bf16[64,32,128]{2,1,0:T(8,128)(2,1)} custom-call(bf16[32,128]{1,0:T(8,128)(2,1)S(1)} %psum.14.v_ref, bf16[32,4096]{1,0:T(8,128)(2,1)S(1)} %bitcast.17, bf16[128,32]{1,0:T(8,128)(2,1)S(1)} %copy-done.1), custom_call_target="tpu_custom_call" | custom-call | tf_op jit(solution)/shard_map/pallas_call | solution.py:176
  25.0 0.0 copy-start.7
  25.0 0.0 copy-start.4
  25.0 9.1 %all-to-all-start = ((bf16[64,32,128]{2,1,0:T(8,128)(2,1)}), bf16[64,32,128]{2,1,0:T(8,128)(2,1)S(1)}, u32[]{:S(2)}, u32[]{:S(2)}) async-start(bf16[64,32,128]{2,1,0:T(8,128)(2,1)} %shard_map.109), calls=%async_computation | async-start | bytes 1048576 | tf_op jit(solution)/shard_map/all_to_all | solution.py:208
  34.1 0.0 copy-start.8
  34.1 0.0 copy-start.3
  34.1 0.0 copy-done.7
  34.2 0.1 convert_element_type.58
  34.3 0.0 copy-done.4
  34.3 0.1 stack_tile.3
  34.3 0.4 copy-done.8
  34.8 0.0 copy-start.5
  34.8 0.0 copy-start.6
  34.8 0.6 copy-done.5
  35.5 0.0 copy-done.6
  35.5 0.1 broadcast_select_fusion.1
  35.6 11.2 %psum.15 = s32[4,192]{1,0:T(4,128)S(1)} all-reduce(s32[4,192]{1,0:T(4,128)S(1)} %broadcast_select_fusion.1), channel_id=1, replica_groups=mesh['y'=4,'zl'=4,'x'=4,'zh'=4,'c'=2] {'zl'}, use_global_device_ids=true, to_apply=%region_1.2 | all-reduce | flops 768 | bytes 6144 | tf_op jit(solution)/shard_map/psum | solution.py:212
  46.7 0.0 copy-done.3
  46.7 0.0 copy-start.2
  46.7 0.3 convolution_convert_fusion.p_ref
  47.1 0.4 copy-done.2
  47.5 0.3 convolution_convert_fusion.1.e_ref
  47.8 2.5 %all-to-all-done.r_ref = bf16[64,32,128]{2,1,0:T(8,128)(2,1)S(1)} async-done(((bf16[64,32,128]{2,1,0:T(8,128)(2,1)}), bf16[64,32,128]{2,1,0:T(8,128)(2,1)S(1)}, u32[]{:S(2)}, u32[]{:S(2)}) %all-to-all-start) | async-done | bytes 524320 | tf_op jit(solution)/shard_map/all_to_all | solution.py:208
  50.3 1.4 %shard_map.110 = bf16[16,32,128]{2,1,0:T(8,128)(2,1)S(1)} custom-call(bf16[64,32,128]{2,1,0:T(8,128)(2,1)S(1)} %all-to-all-done.r_ref, bf16[4,192,256]{2,1,0:T(8,128)(2,1)S(1)} %convolution_convert_fusion.1.e_ref, bf16[4,192,256]{2,1,0:T(8,128)(2,1)S(1)} %convolution_convert_fusion.p_ref, f32[6,128]{1,0:T(8,128)S(1)} %stack.20.fact_ref), custom_call_target="tpu_custom_call" | custom-call | tf_op jit(solution)/shard_map/pallas_call | solution.py:176
  51.7 18.2 %all_to_all.15 = bf16[16,32,128]{2,1,0:T(8,128)(2,1)S(1)} all-to-all(bf16[16,32,128]{2,1,0:T(8,128)(2,1)S(1)} %shard_map.110), channel_id=1, replica_groups=mesh['y'=4,'zl'=4,'x'=4,'zh'=4,'c'=2] {'zh','zl'}, dimensions={0} | all-to-all | bytes 262144 | tf_op jit(solution)/shard_map/all_to_all | solution.py:230
  70.0 6.3 %all-gather.1 = bf16[32,32,128]{2,1,0:T(8,128)(2,1)S(1)} all-gather(bf16[16,32,128]{2,1,0:T(8,128)(2,1)S(1)} %all_to_all.15), channel_id=3, replica_groups=mesh['y'=4,'zl'=4,'x'=4,'zh'=4,'c'=2] {'c'}, dimensions={0}, use_global_device_ids=true | all-gather | bytes 393216 | tf_op jit(solution)/shard_map/all_gather | solution.py:231
  76.3 0.2 shard_map.111
  76.5 14.1 %all_to_all.16.b_ref = bf16[16,128,128]{2,1,0:T(8,128)(2,1)S(1)} all-to-all(bf16[16,128,128]{2,1,0:T(8,128)(2,1)S(1)} %shard_map.111), channel_id=1, replica_groups=mesh['y'=4,'zl'=4,'x'=4,'zh'=4,'c'=2] {'y','x'}, dimensions={0} | all-to-all | bytes 1048576 | tf_op jit(solution)/shard_map/all_to_all | solution.py:240
  90.6 1.3 %shard_map.112 = f32[2,128,512]{2,1,0:T(8,128)} custom-call(bf16[2,16,32,128]{3,2,1,0:T(8,128)(2,1)S(1)} %bitcast.16, bf16[16,128,128]{2,1,0:T(8,128)(2,1)S(1)} %all_to_all.16.b_ref), custom_call_target="tpu_custom_call" | custom-call | tf_op jit(solution)/shard_map/pallas_call | solution.py:176
  (11 shorter events, 0.1 us)
Async XLA Ops:
  0.0 23.5 %copy-start = (bf16[32,1,4096]{2,0,1:T(8,128)(2,1)S(1)}, bf16[32,1,4096]{2,0,1:T(8,128)(2,1)}, u32[]{:S(2)}) copy-start(bf16[32,1,4096]{2,0,1:T(8,128)(2,1)} %param.12) | copy-start | bytes 786436
  9.5 14.1 %copy-start.1 = (bf16[128,32]{1,0:T(8,128)(2,1)S(1)}, bf16[128,32]{1,0:T(8,128)(2,1)}, u32[]{:S(2)}) copy-start(bf16[128,32]{1,0:T(8,128)(2,1)} %constant.62.e_ref) | copy-start | bytes 24580
  25.0 9.2 %copy-start.7 = (s32[32]{0:T(128)S(1)}, s32[32]{0:T(128)}, u32[]{:S(2)}) copy-start(s32[32]{0:T(128)} %param.15) | copy-start | bytes 388
  25.0 9.3 %copy-start.4 = (f32[32]{0:T(128)S(1)}, f32[32]{0:T(128)}, u32[]{:S(2)}) copy-start(f32[32]{0:T(128)} %param.16) | copy-start | bytes 388
  25.0 25.4 %all-to-all-start = ((bf16[64,32,128]{2,1,0:T(8,128)(2,1)}), bf16[64,32,128]{2,1,0:T(8,128)(2,1)S(1)}, u32[]{:S(2)}, u32[]{:S(2)}) async-start(bf16[64,32,128]{2,1,0:T(8,128)(2,1)} %shard_map.109), calls=%async_computation | async-start | bytes 1048576 | tf_op jit(solution)/shard_map/all_to_all | solution.py:208
  34.1 0.7 copy-start.8
  34.1 12.6 %copy-start.3 = (bf16[64,256,1]{1,0,2:T(8,128)(2,1)S(1)}, bf16[64,256,1]{1,0,2:T(8,128)(2,1)}, u32[]{:S(2)}) copy-start(bf16[64,256,1]{1,0,2:T(8,128)(2,1)} %constant.67) | copy-start | bytes 98308
  34.8 0.7 copy-start.5
  34.8 0.7 copy-start.6
  46.7 0.8 copy-start.2

commit v10 on v9

--- a/solution.py
+++ b/solution.py
@@ -117,7 +117,7 @@
         cols = joined[ROWS + 16 * q : ROWS + 16 * q + 16]
         cols = cols[:8] + pltpu.roll(cols[8:], N, 1)
         for g in range(4):
-            block = [rows[16 * g : 16 * g + 16], cols, jnp.zeros_like(cols)]
+            block = [rows[16 * g : 16 * g + 16], cols]
             out_ref[4 * q + g] = jnp.concatenate(block, axis=0).astype(bf16)
 
 
@@ -127,7 +127,7 @@
     rows = [jnp.zeros((32, LANES), f32)] * 4
     for s in range(8):
         core, zl = s // 4, s % 4
-        cols = [v_ref[core, 4 * q + zl, 16:].astype(f32)[:8] for q in range(4)]
+        cols = [v_ref[core, 4 * q + zl].astype(f32)[16:] for q in range(4)]
         cols = jnp.concatenate(cols, axis=0)
         cols = jnp.where(second, pltpu.roll(cols, N, 1), cols)
         for g in range(4):
@@ -143,11 +143,11 @@
         for x in range(4):
             for zl in range(4):
                 at = (16 * y + 4 * zl + x) * WIDE
-                spread[pl.ds(at, 32), :] = b_ref[4 * y + x, 32 * zl : 32 * zl + 32, :].astype(f32)
+                spread[pl.ds(at, 32), :] = b_ref[4 * x + y, 32 * zl : 32 * zl + 32, :].astype(f32)
     real_lane = lane_index((ROWS, LANES)) % 16 < 8
     upper, lower = [], []
     for q in range(4):
-        rows = [a_ref[s // 4, 4 * q + s % 4, :16].astype(f32) for s in range(8)]
+        rows = [a_ref[s // 4, 4 * q + s % 4].astype(f32)[:16] for s in range(8)]
         rows = jnp.concatenate(rows, axis=0).T
         turned = jnp.where(real_lane, pltpu.roll(rows, LANES - 8, 1), -pltpu.roll(rows, 8, 1))
         upper.append(rows.astype(bf16))
@@ -189,8 +189,8 @@
     chosen = band_index[0]
     core = lax.axis_index("c")
     local = lax.all_gather(valence.reshape(-1, N * N), "c", tiled=True)
-    own = lax.dynamic_index_in_dim(local, chosen % local.shape[0], 0, keepdims=False)
-    own = jnp.where(chosen // local.shape[0] == lax.axis_index("zh"), own, 0)
+    band = lax.broadcasted_iota(jnp.int32, local.shape, 0) + local.shape[0] * lax.axis_index("zh")
+    own = jnp.sum(jnp.where(band == band_index, local, 0).astype(f32), axis=0)
     v = lax.psum(own.astype(bf16).reshape(32, LANES), "zh")
 
     half = call(
@@ -218,7 +218,7 @@
     facts = jnp.stack([fact.astype(f32) for fact in facts] + [jnp.tile(gap_energy, 4)])
     values = call(
         spots_kernel,
-        (16, 32, LANES),
+        (16, 24, LANES),
         bf16,
         [pltpu.VMEM((N * WIDE, LANES), f32)],
         block,
@@ -237,7 +237,7 @@
         values,
         facts,
     )
-    columns = lax.all_to_all(cols, ("y", "x"), 0, 0, tiled=True)
+    columns = lax.all_to_all(cols, ("x", "y"), 0, 0, tiled=True)
     return call(
         panel_kernel,
         (2, ROWS, 8 * N),

time: 92.4 us -> 91.9 us (level)
  no operation moved by 1% of the time
where the time goes in v10:
time: 91.9 us; the launch traced here: 91.5 us
  blocking collectives  72 us (78%)
  starting transfers between devices  9.13 us (10%)
  Pallas kernels  4.36 us (5%)
  waiting for transfers between devices  2.5 us (3%)
  local copies, waits for them, and re-layouts  1.71 us (2%)
    all_to_all x1, blocking collectives, shards(): values = lax.all_to_all(values, ('zh', 'zl'), 0, 0, tiled=True)  18.1 us
    psum x1, blocking collectives, shards(): v = lax.psum(own.astype(bf16).reshape(32, LANES), 'zh')  14 us
    all_to_all x1, blocking collectives, shards(): columns = lax.all_to_all(cols, ('x', 'y'), 0, 0, tiled=True)  13.6 us
    psum x1, blocking collectives, shards(): spots = lax.psum(spots, 'zl')  11.2 us
    all_to_all x1, starting transfers between devices, shards(): block = lax.all_to_all(half, GA, 0, 0, tiled=True)  9.13 us
    all_gather x1, blocking collectives, shards(): local = lax.all_gather(valence.reshape(-1, N * N), 'c', tiled=True)  8.85 us
    all_gather x1, blocking collectives, shards(): values = lax.all_gather(values, 'c')  6.27 us
    pallas_call x4, Pallas kernels, call(): pl.pallas_call(kernel, out_shape=jax.ShapeDtypeStruct(shape, dtype), in_s...  4.36 us
  transfers between devices with their start and end apart: 1, of which 1 were waited for; matrix products, arithmetic and copies ran while one was open for 1% of the time, Pallas kernels for 0%

profile of v10, /device:TPU:1, one launch (start us, length us, event | category | flops | bytes accessed | tf_op | source)
XLA Modules:
  0.0 91.5 jit_solution(15487189751783646643)
XLA Ops:
  0.7 0.0 copy-start
  0.7 8.9 %all-gather = bf16[32,1,4096]{2,0,1:T(8,128)(2,1)S(1)} all-gather(bf16[16,1,4096]{2,0,1:T(8,128)(2,1)} %param.11), channel_id=2, replica_groups=mesh['y'=4,'zl'=4,'x'=4,'zh'=4,'c'=2] {'c'}, dimensions={0}, use_global_device_ids=true | all-gather | bytes 393216 | tf_op jit(solution)/shard_map/all_gather | solution.py:191
  9.5 0.0 copy-start.1
  9.5 0.2 fusion
  9.7 14.0 %psum.14.v_ref = bf16[32,128]{1,0:T(8,128)(2,1)S(1)} all-reduce(bf16[32,128]{1,0:T(8,128)(2,1)S(1)} %bitcast.19), channel_id=1, replica_groups=mesh['y'=4,'zl'=4,'x'=4,'zh'=4,'c'=2] {'zh'}, use_global_device_ids=true, to_apply=%region_1.2 | all-reduce | flops 4096 | bytes 16384 | tf_op jit(solution)/shard_map/psum | solution.py:194
  23.7 0.0 copy-done
  23.7 0.0 copy-done.1
  23.7 1.4 %shard_map.109 = bf16[64,32,128]{2,1,0:T(8,128)(2,1)} custom-call(bf16[32,128]{1,0:T(8,128)(2,1)S(1)} %psum.14.v_ref, bf16[32,4096]{1,0:T(8,128)(2,1)S(1)} %bitcast.18, bf16[128,32]{1,0:T(8,128)(2,1)S(1)} %copy-done.1), custom_call_target="tpu_custom_call" | custom-call | tf_op jit(solution)/shard_map/pallas_call | solution.py:176
  25.1 0.0 copy-start.7
  25.1 0.0 copy-start.4
  25.1 9.1 %all-to-all-start = ((bf16[64,32,128]{2,1,0:T(8,128)(2,1)}), bf16[64,32,128]{2,1,0:T(8,128)(2,1)S(1)}, u32[]{:S(2)}, u32[]{:S(2)}) async-start(bf16[64,32,128]{2,1,0:T(8,128)(2,1)} %shard_map.109), calls=%async_computation | async-start | bytes 1048576 | tf_op jit(solution)/shard_map/all_to_all | solution.py:208
  34.3 0.0 copy-start.8
  34.3 0.0 copy-start.3
  34.3 0.0 copy-done.7
  34.3 0.1 convert_element_type.60
  34.4 0.0 copy-done.4
  34.4 0.1 stack_tile.3
  34.5 0.4 copy-done.8
  35.0 0.0 copy-start.5
  35.0 0.0 copy-start.6
  35.0 0.6 copy-done.5
  35.6 0.0 copy-done.6
  35.6 0.1 broadcast_select_fusion
  35.7 11.2 %psum.15 = s32[4,192]{1,0:T(4,128)S(1)} all-reduce(s32[4,192]{1,0:T(4,128)S(1)} %broadcast_select_fusion), channel_id=1, replica_groups=mesh['y'=4,'zl'=4,'x'=4,'zh'=4,'c'=2] {'zl'}, use_global_device_ids=true, to_apply=%region_2.3 | all-reduce | flops 768 | bytes 6144 | tf_op jit(solution)/shard_map/psum | solution.py:212
  46.9 0.0 copy-done.3
  46.9 0.0 copy-start.2
  46.9 0.3 convolution_convert_fusion.p_ref
  47.2 0.4 copy-done.2
  47.6 0.3 convolution_convert_fusion.1.e_ref
  48.0 2.5 %all-to-all-done.r_ref = bf16[64,32,128]{2,1,0:T(8,128)(2,1)S(1)} async-done(((bf16[64,32,128]{2,1,0:T(8,128)(2,1)}), bf16[64,32,128]{2,1,0:T(8,128)(2,1)S(1)}, u32[]{:S(2)}, u32[]{:S(2)}) %all-to-all-start) | async-done | bytes 524320 | tf_op jit(solution)/shard_map/all_to_all | solution.py:208
  50.5 1.4 %shard_map.110 = bf16[16,24,128]{2,1,0:T(8,128)(2,1)S(1)} custom-call(bf16[64,32,128]{2,1,0:T(8,128)(2,1)S(1)} %all-to-all-done.r_ref, bf16[4,192,256]{2,1,0:T(8,128)(2,1)S(1)} %convolution_convert_fusion.1.e_ref, bf16[4,192,256]{2,1,0:T(8,128)(2,1)S(1)} %convolution_convert_fusion.p_ref, f32[6,128]{1,0:T(8,128)S(1)} %stack.20.fact_ref), custom_call_target="tpu_custom_call" | custom-call | tf_op jit(solution)/shard_map/pallas_call | solution.py:176
  51.9 18.1 %all_to_all.15 = bf16[16,24,128]{2,1,0:T(8,128)(2,1)S(1)} all-to-all(bf16[16,24,128]{2,1,0:T(8,128)(2,1)S(1)} %shard_map.110), channel_id=1, replica_groups=mesh['y'=4,'zl'=4,'x'=4,'zh'=4,'c'=2] {'zh','zl'}, dimensions={0} | all-to-all | bytes 196608 | tf_op jit(solution)/shard_map/all_to_all | solution.py:230
  70.0 6.3 %all-gather.1 = bf16[32,24,128]{2,1,0:T(8,128)(2,1)S(1)} all-gather(bf16[16,24,128]{2,1,0:T(8,128)(2,1)S(1)} %all_to_all.15), channel_id=3, replica_groups=mesh['y'=4,'zl'=4,'x'=4,'zh'=4,'c'=2] {'c'}, dimensions={0}, use_global_device_ids=true | all-gather | bytes 294912 | tf_op jit(solution)/shard_map/all_gather | solution.py:231
  76.3 0.2 shard_map.111
  76.5 13.6 %all_to_all.16.b_ref = bf16[16,128,128]{2,1,0:T(8,128)(2,1)S(1)} all-to-all(bf16[16,128,128]{2,1,0:T(8,128)(2,1)S(1)} %shard_map.111), channel_id=1, replica_groups=mesh['y'=4,'zl'=4,'x'=4,'zh'=4,'c'=2] {'x','y'}, dimensions={0} | all-to-all | bytes 1048576 | tf_op jit(solution)/shard_map/all_to_all | solution.py:240
  90.1 1.3 %shard_map.112 = f32[2,128,512]{2,1,0:T(8,128)} custom-call(bf16[2,16,24,128]{3,2,1,0:T(8,128)(2,1)S(1)} %bitcast.17, bf16[16,128,128]{2,1,0:T(8,128)(2,1)S(1)} %all_to_all.16.b_ref), custom_call_target="tpu_custom_call" | custom-call | tf_op jit(solution)/shard_map/pallas_call | solution.py:176
  (12 shorter events, 0.1 us)
Async XLA Ops:
  0.7 23.0 %copy-start = (bf16[32,1,4096]{2,0,1:T(8,128)(2,1)S(1)}, bf16[32,1,4096]{2,0,1:T(8,128)(2,1)}, u32[]{:S(2)}) copy-start(bf16[32,1,4096]{2,0,1:T(8,128)(2,1)} %param.12) | copy-start | bytes 786436
  9.5 14.2 %copy-start.1 = (bf16[128,32]{1,0:T(8,128)(2,1)S(1)}, bf16[128,32]{1,0:T(8,128)(2,1)}, u32[]{:S(2)}) copy-start(bf16[128,32]{1,0:T(8,128)(2,1)} %constant.37.e_ref) | copy-start | bytes 24580
  25.1 9.2 %copy-start.7 = (s32[32]{0:T(128)S(1)}, s32[32]{0:T(128)}, u32[]{:S(2)}) copy-start(s32[32]{0:T(128)} %param.15) | copy-start | bytes 388
  25.1 9.3 %copy-start.4 = (f32[32]{0:T(128)S(1)}, f32[32]{0:T(128)}, u32[]{:S(2)}) copy-start(f32[32]{0:T(128)} %param.16) | copy-start | bytes 388
  25.1 25.4 %all-to-all-start = ((bf16[64,32,128]{2,1,0:T(8,128)(2,1)}), bf16[64,32,128]{2,1,0:T(8,128)(2,1)S(1)}, u32[]{:S(2)}, u32[]{:S(2)}) async-start(bf16[64,32,128]{2,1,0:T(8,128)(2,1)} %shard_map.109), calls=%async_computation | async-start | bytes 1048576 | tf_op jit(solution)/shard_map/all_to_all | solution.py:208
  34.3 0.7 copy-start.8
  34.3 12.6 %copy-start.3 = (bf16[64,256,1]{1,0,2:T(8,128)(2,1)S(1)}, bf16[64,256,1]{1,0,2:T(8,128)(2,1)}, u32[]{:S(2)}) copy-start(bf16[64,256,1]{1,0,2:T(8,128)(2,1)} %constant.41) | copy-start | bytes 98308
  35.0 0.7 copy-start.5
  35.0 0.7 copy-start.6
  46.9 0.8 copy-start.2

commit v11 on v10

--- a/solution.py
+++ b/solution.py
@@ -53,7 +53,7 @@
     return np.concatenate([wave(turn), wave(turn - 16)], axis=1)
 
 
-def pair_y_kernel(v_ref, c_ref, e_ref, out_ref, by_row, by_ky):
+def pair_y_kernel(v_ref, c_ref, e_ref, out_hbm, by_row, by_ky, out_ref, sent):
     v = v_ref[...].astype(f32)
     for i in range(N // 2):
         bands = c_ref[:, i * LANES : (i + 1) * LANES].astype(f32)
@@ -72,10 +72,17 @@
         for start, value in ((2 * j, even + odd), (half * WIDE + 2 * j, even - odd)):
             by_ky[pl.ds(start, half, stride=WIDE), :] = value[:half]
             by_ky[pl.ds(start + 1, half, stride=WIDE), :] = value[half:]
+    copies = []
     for place in range(N):
         first, zl = place // 16 * 16 + place % 4, place // 4 % 4
         rows = [by_ky[pl.ds((first + 4 * k) * WIDE + 8 * zl, 8), :] for k in range(4)]
         out_ref[place] = jnp.concatenate(rows, axis=0).astype(bf16)
+        if place % 16 == 15:
+            part = pl.ds(place - 15, 16)
+            copies.append(pltpu.make_async_copy(out_ref.at[part], out_hbm.at[part], sent.at[place // 16]))
+            copies[-1].start()
+    for copy in copies:
+        copy.wait()
 
 
 def weight_row(fact_ref):
@@ -171,13 +178,13 @@
         out_ref[1, :, h * 256 : (h + 1) * 256] = part[ROWS:]
 
 
-def call(kernel, shape, dtype, scratch, *args):
+def call(kernel, shape, dtype, scratch, *args, out_space=pltpu.VMEM):
     vmem = pl.BlockSpec(memory_space=pltpu.VMEM)
     return pl.pallas_call(
         kernel,
         out_shape=jax.ShapeDtypeStruct(shape, dtype),
         in_specs=[vmem] * len(args),
-        out_specs=vmem,
+        out_specs=pl.BlockSpec(memory_space=out_space),
         scratch_shapes=scratch,
         compiler_params=pltpu.CompilerParams(vmem_limit_bytes=32 * 1024 * 1024),
     )(*args)
@@ -197,10 +204,16 @@
         pair_y_kernel,
         (N, 32, LANES),
         bf16,
-        [pltpu.VMEM((BANDS * WIDE, LANES), f32), pltpu.VMEM((N * WIDE, LANES), f32)],
+        [
+            pltpu.VMEM((BANDS * WIDE, LANES), f32),
+            pltpu.VMEM((N * WIDE, LANES), f32),
+            pltpu.VMEM((N, 32, LANES), bf16),
+            pltpu.SemaphoreType.DMA((4,)),
+        ],
         v,
         conduction.reshape(BANDS, N * N),
         jnp.asarray(y_table()).astype(bf16),
+        out_space=pl.ANY,
     )
     late = (half, row_map, col_map, occ_valence, occ_conduction, gap_energy)
     late = lax.optimization_barrier(late)

time: 91.9 us -> 91.9 us (level)
  no operation moved by 1% of the time
where the time goes in v11:
time: 91.9 us; the launch traced here: 91.4 us
  blocking collectives  72 us (78%)
  starting transfers between devices  9.01 us (10%)
  Pallas kernels  4.39 us (5%)
  waiting for transfers between devices  2.5 us (3%)
  local copies, waits for them, and re-layouts  1.72 us (2%)
    all_to_all x1, blocking collectives, shards(): values = lax.all_to_all(values, ('zh', 'zl'), 0, 0, tiled=True)  18.1 us
    psum x1, blocking collectives, shards(): v = lax.psum(own.astype(bf16).reshape(32, LANES), 'zh')  14 us
    all_to_all x1, blocking collectives, shards(): columns = lax.all_to_all(cols, ('x', 'y'), 0, 0, tiled=True)  13.6 us
    psum x1, blocking collectives, shards(): spots = lax.psum(spots, 'zl')  11.2 us
    all_to_all x1, starting transfers between devices, shards(): block = lax.all_to_all(half, GA, 0, 0, tiled=True)  9.01 us
    all_gather x1, blocking collectives, shards(): local = lax.all_gather(valence.reshape(-1, N * N), 'c', tiled=True)  8.85 us
    all_gather x1, blocking collectives, shards(): values = lax.all_gather(values, 'c')  6.28 us
    pallas_call x4, Pallas kernels, call(): pl.pallas_call(kernel, out_shape=jax.ShapeDtypeStruct(shape, dtype), in_s...  4.39 us
  transfers between devices with their start and end apart: 1, of which 1 were waited for; matrix products, arithmetic and copies ran while one was open for 1% of the time, Pallas kernels for 0%

profile of v11, /device:TPU:1, one launch (start us, length us, event | category | flops | bytes accessed | tf_op | source)
XLA Modules:
  0.0 91.4 jit_solution(3768156811168601726)
XLA Ops:
  0.7 0.0 copy-start
  0.7 8.9 %all-gather = bf16[32,1,4096]{2,0,1:T(8,128)(2,1)S(1)} all-gather(bf16[16,1,4096]{2,0,1:T(8,128)(2,1)} %param.11), channel_id=2, replica_groups=mesh['y'=4,'zl'=4,'x'=4,'zh'=4,'c'=2] {'c'}, dimensions={0}, use_global_device_ids=true | all-gather | bytes 393216 | tf_op jit(solution)/shard_map/all_gather | solution.py:198
  9.5 0.0 copy-start.1
  9.5 0.2 fusion
  9.7 14.0 %psum.14.v_ref = bf16[32,128]{1,0:T(8,128)(2,1)S(1)} all-reduce(bf16[32,128]{1,0:T(8,128)(2,1)S(1)} %bitcast.19), channel_id=1, replica_groups=mesh['y'=4,'zl'=4,'x'=4,'zh'=4,'c'=2] {'zh'}, use_global_device_ids=true, to_apply=%region_1.2 | all-reduce | flops 4096 | bytes 16384 | tf_op jit(solution)/shard_map/psum | solution.py:201
  23.7 0.0 copy-done
  23.7 0.0 copy-done.1
  23.7 1.4 %shard_map.109 = bf16[64,32,128]{2,1,0:T(8,128)(2,1)} custom-call(bf16[32,128]{1,0:T(8,128)(2,1)S(1)} %psum.14.v_ref, bf16[32,4096]{1,0:T(8,128)(2,1)S(1)} %bitcast.18, bf16[128,32]{1,0:T(8,128)(2,1)S(1)} %copy-done.1), custom_call_target="tpu_custom_call" | custom-call | tf_op jit(solution)/shard_map/pallas_call | solution.py:183
  25.2 0.0 copy-start.7
  25.2 0.0 copy-start.4
  25.2 9.0 %all-to-all-start = ((bf16[64,32,128]{2,1,0:T(8,128)(2,1)}), bf16[64,32,128]{2,1,0:T(8,128)(2,1)S(1)}, u32[]{:S(2)}, u32[]{:S(2)}) async-start(bf16[64,32,128]{2,1,0:T(8,128)(2,1)} %shard_map.109), calls=%async_computation | async-start | bytes 1048576 | tf_op jit(solution)/shard_map/all_to_all | solution.py:221
  34.2 0.0 copy-start.8
  34.2 0.0 copy-start.3
  34.2 0.0 copy-done.7
  34.3 0.1 convert_element_type.60
  34.3 0.0 copy-done.4
  34.3 0.1 stack_tile.3
  34.4 0.4 copy-done.8
  34.9 0.0 copy-start.5
  34.9 0.0 copy-start.6
  34.9 0.6 copy-done.5
  35.6 0.0 copy-done.6
  35.6 0.1 broadcast_select_fusion
  35.7 11.2 %psum.15 = s32[4,192]{1,0:T(4,128)S(1)} all-reduce(s32[4,192]{1,0:T(4,128)S(1)} %broadcast_select_fusion), channel_id=1, replica_groups=mesh['y'=4,'zl'=4,'x'=4,'zh'=4,'c'=2] {'zl'}, use_global_device_ids=true, to_apply=%region_2.3 | all-reduce | flops 768 | bytes 6144 | tf_op jit(solution)/shard_map/psum | solution.py:225
  46.8 0.0 copy-done.3
  46.8 0.0 copy-start.2
  46.8 0.3 convolution_convert_fusion.p_ref
  47.2 0.4 copy-done.2
  47.6 0.3 convolution_convert_fusion.1.e_ref
  47.9 2.5 %all-to-all-done.r_ref = bf16[64,32,128]{2,1,0:T(8,128)(2,1)S(1)} async-done(((bf16[64,32,128]{2,1,0:T(8,128)(2,1)}), bf16[64,32,128]{2,1,0:T(8,128)(2,1)S(1)}, u32[]{:S(2)}, u32[]{:S(2)}) %all-to-all-start) | async-done | bytes 524320 | tf_op jit(solution)/shard_map/all_to_all | solution.py:221
  50.4 1.4 %shard_map.110 = bf16[16,24,128]{2,1,0:T(8,128)(2,1)S(1)} custom-call(bf16[64,32,128]{2,1,0:T(8,128)(2,1)S(1)} %all-to-all-done.r_ref, bf16[4,192,256]{2,1,0:T(8,128)(2,1)S(1)} %convolution_convert_fusion.1.e_ref, bf16[4,192,256]{2,1,0:T(8,128)(2,1)S(1)} %convolution_convert_fusion.p_ref, f32[6,128]{1,0:T(8,128)S(1)} %stack.20.fact_ref), custom_call_target="tpu_custom_call" | custom-call | tf_op jit(solution)/shard_map/pallas_call | solution.py:183
  51.8 18.1 %all_to_all.15 = bf16[16,24,128]{2,1,0:T(8,128)(2,1)S(1)} all-to-all(bf16[16,24,128]{2,1,0:T(8,128)(2,1)S(1)} %shard_map.110), channel_id=1, replica_groups=mesh['y'=4,'zl'=4,'x'=4,'zh'=4,'c'=2] {'zh','zl'}, dimensions={0} | all-to-all | bytes 196608 | tf_op jit(solution)/shard_map/all_to_all | solution.py:243
  69.9 6.3 %all-gather.1 = bf16[32,24,128]{2,1,0:T(8,128)(2,1)S(1)} all-gather(bf16[16,24,128]{2,1,0:T(8,128)(2,1)S(1)} %all_to_all.15), channel_id=3, replica_groups=mesh['y'=4,'zl'=4,'x'=4,'zh'=4,'c'=2] {'c'}, dimensions={0}, use_global_device_ids=true | all-gather | bytes 294912 | tf_op jit(solution)/shard_map/all_gather | solution.py:244
  76.2 0.2 shard_map.111
  76.4 13.6 %all_to_all.16.b_ref = bf16[16,128,128]{2,1,0:T(8,128)(2,1)S(1)} all-to-all(bf16[16,128,128]{2,1,0:T(8,128)(2,1)S(1)} %shard_map.111), channel_id=1, replica_groups=mesh['y'=4,'zl'=4,'x'=4,'zh'=4,'c'=2] {'x','y'}, dimensions={0} | all-to-all | bytes 1048576 | tf_op jit(solution)/shard_map/all_to_all | solution.py:253
  90.1 1.3 %shard_map.112 = f32[2,128,512]{2,1,0:T(8,128)} custom-call(bf16[2,16,24,128]{3,2,1,0:T(8,128)(2,1)S(1)} %bitcast.17, bf16[16,128,128]{2,1,0:T(8,128)(2,1)S(1)} %all_to_all.16.b_ref), custom_call_target="tpu_custom_call" | custom-call | tf_op jit(solution)/shard_map/pallas_call | solution.py:183
  (12 shorter events, 0.1 us)
Async XLA Ops:
  0.7 23.0 %copy-start = (bf16[32,1,4096]{2,0,1:T(8,128)(2,1)S(1)}, bf16[32,1,4096]{2,0,1:T(8,128)(2,1)}, u32[]{:S(2)}) copy-start(bf16[32,1,4096]{2,0,1:T(8,128)(2,1)} %param.12) | copy-start | bytes 786436
  9.5 14.2 %copy-start.1 = (bf16[128,32]{1,0:T(8,128)(2,1)S(1)}, bf16[128,32]{1,0:T(8,128)(2,1)}, u32[]{:S(2)}) copy-start(bf16[128,32]{1,0:T(8,128)(2,1)} %constant.37.e_ref) | copy-start | bytes 24580
  25.2 9.1 %copy-start.7 = (s32[32]{0:T(128)S(1)}, s32[32]{0:T(128)}, u32[]{:S(2)}) copy-start(s32[32]{0:T(128)} %param.15) | copy-start | bytes 388
  25.2 9.2 %copy-start.4 = (f32[32]{0:T(128)S(1)}, f32[32]{0:T(128)}, u32[]{:S(2)}) copy-start(f32[32]{0:T(128)} %param.16) | copy-start | bytes 388
  25.2 25.2 %all-to-all-start = ((bf16[64,32,128]{2,1,0:T(8,128)(2,1)}), bf16[64,32,128]{2,1,0:T(8,128)(2,1)S(1)}, u32[]{:S(2)}, u32[]{:S(2)}) async-start(bf16[64,32,128]{2,1,0:T(8,128)(2,1)} %shard_map.109), calls=%async_computation | async-start | bytes 1048576 | tf_op jit(solution)/shard_map/all_to_all | solution.py:221
  34.2 0.7 copy-start.8
  34.2 12.6 %copy-start.3 = (bf16[64,256,1]{1,0,2:T(8,128)(2,1)S(1)}, bf16[64,256,1]{1,0,2:T(8,128)(2,1)}, u32[]{:S(2)}) copy-start(bf16[64,256,1]{1,0,2:T(8,128)(2,1)} %constant.41) | copy-start | bytes 98308
  34.9 0.7 copy-start.5
  34.9 0.7 copy-start.6
  46.8 0.8 copy-start.2

commit v12 on v11

--- a/solution.py
+++ b/solution.py
@@ -74,7 +74,7 @@
             by_ky[pl.ds(start + 1, half, stride=WIDE), :] = value[half:]
     copies = []
     for place in range(N):
-        first, zl = place // 16 * 16 + place % 4, place // 4 % 4
+        first, zl = place // 4 % 4 * 16 + place % 4, place // 16
         rows = [by_ky[pl.ds((first + 4 * k) * WIDE + 8 * zl, 8), :] for k in range(4)]
         out_ref[place] = jnp.concatenate(rows, axis=0).astype(bf16)
         if place % 16 == 15:
@@ -97,7 +97,8 @@
 
 def spots_kernel(r_ref, e_ref, p_ref, fact_ref, out_ref, planes):
     for x in range(N):
-        planes[pl.ds(x * WIDE, 32), :] = r_ref[x].astype(f32)
+        place = x // 4 % 4 * 16 + x // 16 * 4 + x % 4
+        planes[pl.ds(x * WIDE, 32), :] = r_ref[place].astype(f32)
     column = lane_index((2 * LANES, LANES))
     band = lax.broadcasted_iota(jnp.int32, (2 * LANES, LANES), 0) // N
     total = jnp.zeros((2 * SPOTS, LANES), f32)
@@ -218,7 +219,7 @@
     late = (half, row_map, col_map, occ_valence, occ_conduction, gap_energy)
     late = lax.optimization_barrier(late)
     half, row_map, col_map, occ_valence, occ_conduction, gap_energy = late
-    block = lax.all_to_all(half, GA, 0, 0, tiled=True)
+    block = lax.all_to_all(half, ("zl", "y", "x"), 0, 0, tiled=True)
 
     mine = (jnp.arange(4) == lax.axis_index("zl"))[:, None]
     spots = jnp.where(mine, jnp.concatenate([row_map, col_map])[None], 0)

time: 91.9 us -> 91.8 us (level)
  blocking collectives: 72 us -> 74 us
  waiting for transfers between devices: 2.5 us -> 0.62 us
    all_to_all x1, waiting for transfers between devices: 2.5 us -> 0.62 us  [shards(): block = lax.all_to_all(half, ('zl', 'y', 'x'), 0, 0, tiled=True)]
    all_to_all x1, blocking collectives: 18.1 us -> 19.8 us  [shards(): values = lax.all_to_all(values, ('zh', 'zl'), 0, 0, tiled=True)]
where the time goes in v12:
time: 91.8 us; the launch traced here: 91.4 us
  blocking collectives  74 us (81%)
  starting transfers between devices  9.01 us (10%)
  Pallas kernels  4.26 us (5%)
  local copies, waits for them, and re-layouts  1.72 us (2%)
    all_to_all x1, blocking collectives, shards(): values = lax.all_to_all(values, ('zh', 'zl'), 0, 0, tiled=True)  19.8 us
    psum x1, blocking collectives, shards(): v = lax.psum(own.astype(bf16).reshape(32, LANES), 'zh')  14 us
    all_to_all x1, blocking collectives, shards(): columns = lax.all_to_all(cols, ('x', 'y'), 0, 0, tiled=True)  13.9 us
    psum x1, blocking collectives, shards(): spots = lax.psum(spots, 'zl')  11 us
    all_to_all x1, starting transfers between devices, shards(): block = lax.all_to_all(half, ('zl', 'y', 'x'), 0, 0, tiled=True)  9.01 us
    all_gather x1, blocking collectives, shards(): local = lax.all_gather(valence.reshape(-1, N * N), 'c', tiled=True)  8.85 us
    all_gather x1, blocking collectives, shards(): values = lax.all_gather(values, 'c')  6.36 us
    pallas_call x4, Pallas kernels, call(): pl.pallas_call(kernel, out_shape=jax.ShapeDtypeStruct(shape, dtype), in_s...  4.26 us
  transfers between devices with their start and end apart: 1, of which 1 were waited for; matrix products, arithmetic and copies ran while one was open for 1% of the time, Pallas kernels for 0%

profile of v12, /device:TPU:1, one launch (start us, length us, event | category | flops | bytes accessed | tf_op | source)
XLA Modules:
  0.0 91.4 jit_solution(4706827930994270354)
XLA Ops:
  0.7 0.0 copy-start
  0.7 8.9 %all-gather = bf16[32,1,4096]{2,0,1:T(8,128)(2,1)S(1)} all-gather(bf16[16,1,4096]{2,0,1:T(8,128)(2,1)} %param.11), channel_id=2, replica_groups=mesh['y'=4,'zl'=4,'x'=4,'zh'=4,'c'=2] {'c'}, dimensions={0}, use_global_device_ids=true | all-gather | bytes 393216 | tf_op jit(solution)/shard_map/all_gather | solution.py:199
  9.5 0.0 copy-start.1
  9.5 0.2 fusion
  9.7 14.0 %psum.14.v_ref = bf16[32,128]{1,0:T(8,128)(2,1)S(1)} all-reduce(bf16[32,128]{1,0:T(8,128)(2,1)S(1)} %bitcast.19), channel_id=1, replica_groups=mesh['y'=4,'zl'=4,'x'=4,'zh'=4,'c'=2] {'zh'}, use_global_device_ids=true, to_apply=%region_1.2 | all-reduce | flops 4096 | bytes 16384 | tf_op jit(solution)/shard_map/psum | solution.py:202
  23.7 0.0 copy-done
  23.7 0.0 copy-done.1
  23.7 1.3 %shard_map.109 = bf16[64,32,128]{2,1,0:T(8,128)(2,1)} custom-call(bf16[32,128]{1,0:T(8,128)(2,1)S(1)} %psum.14.v_ref, bf16[32,4096]{1,0:T(8,128)(2,1)S(1)} %bitcast.18, bf16[128,32]{1,0:T(8,128)(2,1)S(1)} %copy-done.1), custom_call_target="tpu_custom_call" | custom-call | tf_op jit(solution)/shard_map/pallas_call | solution.py:184
  25.0 0.0 copy-start.7
  25.0 0.0 copy-start.4
  25.1 9.0 %all-to-all-start = ((bf16[64,32,128]{2,1,0:T(8,128)(2,1)}), bf16[64,32,128]{2,1,0:T(8,128)(2,1)S(1)}, u32[]{:S(2)}, u32[]{:S(2)}) async-start(bf16[64,32,128]{2,1,0:T(8,128)(2,1)} %shard_map.109), calls=%async_computation | async-start | bytes 1048576 | tf_op jit(solution)/shard_map/all_to_all | solution.py:222
  34.1 0.0 copy-start.8
  34.1 0.0 copy-start.3
  34.1 0.0 copy-done.7
  34.1 0.1 convert_element_type.60
  34.2 0.0 copy-done.4
  34.2 0.1 stack_tile.3
  34.3 0.4 copy-done.8
  34.8 0.0 copy-start.5
  34.8 0.0 copy-start.6
  34.8 0.6 copy-done.5
  35.4 0.0 copy-done.6
  35.4 0.1 broadcast_select_fusion
  35.5 11.0 %psum.15 = s32[4,192]{1,0:T(4,128)S(1)} all-reduce(s32[4,192]{1,0:T(4,128)S(1)} %broadcast_select_fusion), channel_id=1, replica_groups=mesh['y'=4,'zl'=4,'x'=4,'zh'=4,'c'=2] {'zl'}, use_global_device_ids=true, to_apply=%region_2.3 | all-reduce | flops 768 | bytes 6144 | tf_op jit(solution)/shard_map/psum | solution.py:226
  46.6 0.0 copy-done.3
  46.6 0.0 copy-start.2
  46.6 0.3 convolution_convert_fusion.p_ref
  46.9 0.4 copy-done.2
  47.3 0.3 convolution_convert_fusion.1.e_ref
  47.7 0.6 all-to-all-done.r_ref
  48.3 1.4 %shard_map.110 = bf16[16,24,128]{2,1,0:T(8,128)(2,1)S(1)} custom-call(bf16[64,32,128]{2,1,0:T(8,128)(2,1)S(1)} %all-to-all-done.r_ref, bf16[4,192,256]{2,1,0:T(8,128)(2,1)S(1)} %convolution_convert_fusion.1.e_ref, bf16[4,192,256]{2,1,0:T(8,128)(2,1)S(1)} %convolution_convert_fusion.p_ref, f32[6,128]{1,0:T(8,128)S(1)} %stack.20.fact_ref), custom_call_target="tpu_custom_call" | custom-call | tf_op jit(solution)/shard_map/pallas_call | solution.py:184
  49.7 19.8 %all_to_all.15 = bf16[16,24,128]{2,1,0:T(8,128)(2,1)S(1)} all-to-all(bf16[16,24,128]{2,1,0:T(8,128)(2,1)S(1)} %shard_map.110), channel_id=1, replica_groups=mesh['y'=4,'zl'=4,'x'=4,'zh'=4,'c'=2] {'zh','zl'}, dimensions={0} | all-to-all | bytes 196608 | tf_op jit(solution)/shard_map/all_to_all | solution.py:244
  69.5 6.4 %all-gather.1 = bf16[32,24,128]{2,1,0:T(8,128)(2,1)S(1)} all-gather(bf16[16,24,128]{2,1,0:T(8,128)(2,1)S(1)} %all_to_all.15), channel_id=3, replica_groups=mesh['y'=4,'zl'=4,'x'=4,'zh'=4,'c'=2] {'c'}, dimensions={0}, use_global_device_ids=true | all-gather | bytes 294912 | tf_op jit(solution)/shard_map/all_gather | solution.py:245
  75.9 0.2 shard_map.111
  76.1 13.9 %all_to_all.16.b_ref = bf16[16,128,128]{2,1,0:T(8,128)(2,1)S(1)} all-to-all(bf16[16,128,128]{2,1,0:T(8,128)(2,1)S(1)} %shard_map.111), channel_id=1, replica_groups=mesh['y'=4,'zl'=4,'x'=4,'zh'=4,'c'=2] {'x','y'}, dimensions={0} | all-to-all | bytes 1048576 | tf_op jit(solution)/shard_map/all_to_all | solution.py:254
  90.0 1.3 %shard_map.112 = f32[2,128,512]{2,1,0:T(8,128)} custom-call(bf16[2,16,24,128]{3,2,1,0:T(8,128)(2,1)S(1)} %bitcast.17, bf16[16,128,128]{2,1,0:T(8,128)(2,1)S(1)} %all_to_all.16.b_ref), custom_call_target="tpu_custom_call" | custom-call | tf_op jit(solution)/shard_map/pallas_call | solution.py:184
  (12 shorter events, 0.1 us)
Async XLA Ops:
  0.7 23.0 %copy-start = (bf16[32,1,4096]{2,0,1:T(8,128)(2,1)S(1)}, bf16[32,1,4096]{2,0,1:T(8,128)(2,1)}, u32[]{:S(2)}) copy-start(bf16[32,1,4096]{2,0,1:T(8,128)(2,1)} %param.12) | copy-start | bytes 786436
  9.5 14.2 %copy-start.1 = (bf16[128,32]{1,0:T(8,128)(2,1)S(1)}, bf16[128,32]{1,0:T(8,128)(2,1)}, u32[]{:S(2)}) copy-start(bf16[128,32]{1,0:T(8,128)(2,1)} %constant.37.e_ref) | copy-start | bytes 24580
  25.0 9.1 %copy-start.7 = (s32[32]{0:T(128)S(1)}, s32[32]{0:T(128)}, u32[]{:S(2)}) copy-start(s32[32]{0:T(128)} %param.15) | copy-start | bytes 388
  25.0 9.2 %copy-start.4 = (f32[32]{0:T(128)S(1)}, f32[32]{0:T(128)}, u32[]{:S(2)}) copy-start(f32[32]{0:T(128)} %param.16) | copy-start | bytes 388
  25.1 23.2 %all-to-all-start = ((bf16[64,32,128]{2,1,0:T(8,128)(2,1)}), bf16[64,32,128]{2,1,0:T(8,128)(2,1)S(1)}, u32[]{:S(2)}, u32[]{:S(2)}) async-start(bf16[64,32,128]{2,1,0:T(8,128)(2,1)} %shard_map.109), calls=%async_computation | async-start | bytes 1048576 | tf_op jit(solution)/shard_map/all_to_all | solution.py:222
  34.1 0.7 copy-start.8
  34.1 12.5 %copy-start.3 = (bf16[64,256,1]{1,0,2:T(8,128)(2,1)S(1)}, bf16[64,256,1]{1,0,2:T(8,128)(2,1)}, u32[]{:S(2)}) copy-start(bf16[64,256,1]{1,0,2:T(8,128)(2,1)} %constant.41) | copy-start | bytes 98308
  34.8 0.7 copy-start.5
  34.8 0.7 copy-start.6
  46.6 0.8 copy-start.2

commit v13 on v11

--- a/solution.py
+++ b/solution.py
@@ -145,7 +145,7 @@
         out_ref[i] = message
 
 
-def panel_kernel(a_ref, b_ref, out_ref, spread):
+def panel_kernel(a_ref, b_ref, out_hbm, spread, out_ref, sent):
     for y in range(4):
         for x in range(4):
             for zl in range(4):
@@ -162,6 +162,7 @@
     both = jnp.concatenate(
         [jnp.concatenate(upper, axis=1), jnp.concatenate(lower, axis=1)], axis=0
     )
+    copies = []
     for h in range(2):
         columns = []
         for j in range(4 * h, 4 * h + 4):
@@ -174,8 +175,14 @@
             preferred_element_type=f32,
         )
         part = part * (1.0 / 16.0)
-        out_ref[0, :, h * 256 : (h + 1) * 256] = part[:ROWS]
-        out_ref[1, :, h * 256 : (h + 1) * 256] = part[ROWS:]
+        lanes = pl.ds(h * 256, 256)
+        for k in range(2):
+            out_ref[k, :, lanes] = part[k * ROWS : (k + 1) * ROWS]
+            ends = out_ref.at[k, :, lanes], out_hbm.at[k, :, lanes]
+            copies.append(pltpu.make_async_copy(*ends, sent.at[2 * h + k]))
+            copies[-1].start()
+    for copy in copies:
+        copy.wait()
 
 
 def call(kernel, shape, dtype, scratch, *args, out_space=pltpu.VMEM):
@@ -255,9 +262,14 @@
         panel_kernel,
         (2, ROWS, 8 * N),
         f32,
-        [pltpu.VMEM((N * WIDE, LANES), f32)],
+        [
+            pltpu.VMEM((N * WIDE, LANES), f32),
+            pltpu.VMEM((2, ROWS, 8 * N), f32),
+            pltpu.SemaphoreType.DMA((4,)),
+        ],
         values,
         columns,
+        out_space=pl.ANY,
     )
 
 

time: 91.9 us -> 91.8 us (level)
  no operation moved by 1% of the time
where the time goes in v13:
time: 91.8 us; the launch traced here: 91.4 us
  blocking collectives  72 us (78%)
  starting transfers between devices  9.01 us (10%)
  Pallas kernels  4.36 us (5%)
  waiting for transfers between devices  2.5 us (3%)
  local copies, waits for them, and re-layouts  1.72 us (2%)
    all_to_all x1, blocking collectives, shards(): values = lax.all_to_all(values, ('zh', 'zl'), 0, 0, tiled=True)  18.1 us
    psum x1, blocking collectives, shards(): v = lax.psum(own.astype(bf16).reshape(32, LANES), 'zh')  14 us
    all_to_all x1, blocking collectives, shards(): columns = lax.all_to_all(cols, ('x', 'y'), 0, 0, tiled=True)  13.6 us
    psum x1, blocking collectives, shards(): spots = lax.psum(spots, 'zl')  11.2 us
    all_to_all x1, starting transfers between devices, shards(): block = lax.all_to_all(half, GA, 0, 0, tiled=True)  9.01 us
    all_gather x1, blocking collectives, shards(): local = lax.all_gather(valence.reshape(-1, N * N), 'c', tiled=True)  8.85 us
    all_gather x1, blocking collectives, shards(): values = lax.all_gather(values, 'c')  6.28 us
    pallas_call x4, Pallas kernels, call(): pl.pallas_call(kernel, out_shape=jax.ShapeDtypeStruct(shape, dtype), in_s...  4.36 us
  transfers between devices with their start and end apart: 1, of which 1 were waited for; matrix products, arithmetic and copies ran while one was open for 1% of the time, Pallas kernels for 0%

profile of v13, /device:TPU:1, one launch (start us, length us, event | category | flops | bytes accessed | tf_op | source)
XLA Modules:
  0.0 91.4 jit_solution(16449368153126821847)
XLA Ops:
  0.7 0.0 copy-start
  0.7 8.9 %all-gather = bf16[32,1,4096]{2,0,1:T(8,128)(2,1)S(1)} all-gather(bf16[16,1,4096]{2,0,1:T(8,128)(2,1)} %param.11), channel_id=2, replica_groups=mesh['y'=4,'zl'=4,'x'=4,'zh'=4,'c'=2] {'c'}, dimensions={0}, use_global_device_ids=true | all-gather | bytes 393216 | tf_op jit(solution)/shard_map/all_gather | solution.py:205
  9.5 0.0 copy-start.1
  9.5 0.2 fusion
  9.7 14.0 %psum.14.v_ref = bf16[32,128]{1,0:T(8,128)(2,1)S(1)} all-reduce(bf16[32,128]{1,0:T(8,128)(2,1)S(1)} %bitcast.19), channel_id=1, replica_groups=mesh['y'=4,'zl'=4,'x'=4,'zh'=4,'c'=2] {'zh'}, use_global_device_ids=true, to_apply=%region_1.2 | all-reduce | flops 4096 | bytes 16384 | tf_op jit(solution)/shard_map/psum | solution.py:208
  23.7 0.0 copy-done
  23.7 0.0 copy-done.1
  23.7 1.4 %shard_map.109 = bf16[64,32,128]{2,1,0:T(8,128)(2,1)} custom-call(bf16[32,128]{1,0:T(8,128)(2,1)S(1)} %psum.14.v_ref, bf16[32,4096]{1,0:T(8,128)(2,1)S(1)} %bitcast.18, bf16[128,32]{1,0:T(8,128)(2,1)S(1)} %copy-done.1), custom_call_target="tpu_custom_call" | custom-call | tf_op jit(solution)/shard_map/pallas_call | solution.py:190
  25.2 0.0 copy-start.7
  25.2 0.0 copy-start.4
  25.2 9.0 %all-to-all-start = ((bf16[64,32,128]{2,1,0:T(8,128)(2,1)}), bf16[64,32,128]{2,1,0:T(8,128)(2,1)S(1)}, u32[]{:S(2)}, u32[]{:S(2)}) async-start(bf16[64,32,128]{2,1,0:T(8,128)(2,1)} %shard_map.109), calls=%async_computation | async-start | bytes 1048576 | tf_op jit(solution)/shard_map/all_to_all | solution.py:228
  34.2 0.0 copy-start.8
  34.2 0.0 copy-start.3
  34.2 0.0 copy-done.7
  34.3 0.1 convert_element_type.60
  34.3 0.0 copy-done.4
  34.3 0.1 stack_tile.3
  34.4 0.4 copy-done.8
  34.9 0.0 copy-start.5
  34.9 0.0 copy-start.6
  34.9 0.6 copy-done.5
  35.6 0.0 copy-done.6
  35.6 0.1 broadcast_select_fusion
  35.7 11.2 %psum.15 = s32[4,192]{1,0:T(4,128)S(1)} all-reduce(s32[4,192]{1,0:T(4,128)S(1)} %broadcast_select_fusion), channel_id=1, replica_groups=mesh['y'=4,'zl'=4,'x'=4,'zh'=4,'c'=2] {'zl'}, use_global_device_ids=true, to_apply=%region_2.3 | all-reduce | flops 768 | bytes 6144 | tf_op jit(solution)/shard_map/psum | solution.py:232
  46.8 0.0 copy-done.3
  46.8 0.0 copy-start.2
  46.8 0.3 convolution_convert_fusion.p_ref
  47.2 0.4 copy-done.2
  47.6 0.3 convolution_convert_fusion.1.e_ref
  47.9 2.5 %all-to-all-done.r_ref = bf16[64,32,128]{2,1,0:T(8,128)(2,1)S(1)} async-done(((bf16[64,32,128]{2,1,0:T(8,128)(2,1)}), bf16[64,32,128]{2,1,0:T(8,128)(2,1)S(1)}, u32[]{:S(2)}, u32[]{:S(2)}) %all-to-all-start) | async-done | bytes 524320 | tf_op jit(solution)/shard_map/all_to_all | solution.py:228
  50.4 1.4 %shard_map.110 = bf16[16,24,128]{2,1,0:T(8,128)(2,1)S(1)} custom-call(bf16[64,32,128]{2,1,0:T(8,128)(2,1)S(1)} %all-to-all-done.r_ref, bf16[4,192,256]{2,1,0:T(8,128)(2,1)S(1)} %convolution_convert_fusion.1.e_ref, bf16[4,192,256]{2,1,0:T(8,128)(2,1)S(1)} %convolution_convert_fusion.p_ref, f32[6,128]{1,0:T(8,128)S(1)} %stack.20.fact_ref), custom_call_target="tpu_custom_call" | custom-call | tf_op jit(solution)/shard_map/pallas_call | solution.py:190
  51.8 18.1 %all_to_all.15 = bf16[16,24,128]{2,1,0:T(8,128)(2,1)S(1)} all-to-all(bf16[16,24,128]{2,1,0:T(8,128)(2,1)S(1)} %shard_map.110), channel_id=1, replica_groups=mesh['y'=4,'zl'=4,'x'=4,'zh'=4,'c'=2] {'zh','zl'}, dimensions={0} | all-to-all | bytes 196608 | tf_op jit(solution)/shard_map/all_to_all | solution.py:250
  69.9 6.3 %all-gather.1 = bf16[32,24,128]{2,1,0:T(8,128)(2,1)S(1)} all-gather(bf16[16,24,128]{2,1,0:T(8,128)(2,1)S(1)} %all_to_all.15), channel_id=3, replica_groups=mesh['y'=4,'zl'=4,'x'=4,'zh'=4,'c'=2] {'c'}, dimensions={0}, use_global_device_ids=true | all-gather | bytes 294912 | tf_op jit(solution)/shard_map/all_gather | solution.py:251
  76.2 0.2 shard_map.111
  76.4 13.6 %all_to_all.16.b_ref = bf16[16,128,128]{2,1,0:T(8,128)(2,1)S(1)} all-to-all(bf16[16,128,128]{2,1,0:T(8,128)(2,1)S(1)} %shard_map.111), channel_id=1, replica_groups=mesh['y'=4,'zl'=4,'x'=4,'zh'=4,'c'=2] {'x','y'}, dimensions={0} | all-to-all | bytes 1048576 | tf_op jit(solution)/shard_map/all_to_all | solution.py:260
  90.1 1.3 %shard_map.112 = f32[2,128,512]{2,1,0:T(8,128)} custom-call(bf16[2,16,24,128]{3,2,1,0:T(8,128)(2,1)S(1)} %bitcast.17, bf16[16,128,128]{2,1,0:T(8,128)(2,1)S(1)} %all_to_all.16.b_ref), custom_call_target="tpu_custom_call" | custom-call | tf_op jit(solution)/shard_map/pallas_call | solution.py:190
  (12 shorter events, 0.1 us)
Async XLA Ops:
  0.7 23.0 %copy-start = (bf16[32,1,4096]{2,0,1:T(8,128)(2,1)S(1)}, bf16[32,1,4096]{2,0,1:T(8,128)(2,1)}, u32[]{:S(2)}) copy-start(bf16[32,1,4096]{2,0,1:T(8,128)(2,1)} %param.12) | copy-start | bytes 786436
  9.5 14.2 %copy-start.1 = (bf16[128,32]{1,0:T(8,128)(2,1)S(1)}, bf16[128,32]{1,0:T(8,128)(2,1)}, u32[]{:S(2)}) copy-start(bf16[128,32]{1,0:T(8,128)(2,1)} %constant.37.e_ref) | copy-start | bytes 24580
  25.2 9.1 %copy-start.7 = (s32[32]{0:T(128)S(1)}, s32[32]{0:T(128)}, u32[]{:S(2)}) copy-start(s32[32]{0:T(128)} %param.15) | copy-start | bytes 388
  25.2 9.2 %copy-start.4 = (f32[32]{0:T(128)S(1)}, f32[32]{0:T(128)}, u32[]{:S(2)}) copy-start(f32[32]{0:T(128)} %param.16) | copy-start | bytes 388
  25.2 25.2 %all-to-all-start = ((bf16[64,32,128]{2,1,0:T(8,128)(2,1)}), bf16[64,32,128]{2,1,0:T(8,128)(2,1)S(1)}, u32[]{:S(2)}, u32[]{:S(2)}) async-start(bf16[64,32,128]{2,1,0:T(8,128)(2,1)} %shard_map.109), calls=%async_computation | async-start | bytes 1048576 | tf_op jit(solution)/shard_map/all_to_all | solution.py:228
  34.2 0.7 copy-start.8
  34.2 12.6 %copy-start.3 = (bf16[64,256,1]{1,0,2:T(8,128)(2,1)S(1)}, bf16[64,256,1]{1,0,2:T(8,128)(2,1)}, u32[]{:S(2)}) copy-start(bf16[64,256,1]{1,0,2:T(8,128)(2,1)} %constant.41) | copy-start | bytes 98308
  34.9 0.7 copy-start.5
  34.9 0.7 copy-start.6
  46.8 0.8 copy-start.2

commit v14 on v11

--- a/solution.py
+++ b/solution.py
@@ -77,9 +77,9 @@
         first, zl = place // 16 * 16 + place % 4, place // 4 % 4
         rows = [by_ky[pl.ds((first + 4 * k) * WIDE + 8 * zl, 8), :] for k in range(4)]
         out_ref[place] = jnp.concatenate(rows, axis=0).astype(bf16)
-        if place % 16 == 15:
-            part = pl.ds(place - 15, 16)
-            copies.append(pltpu.make_async_copy(out_ref.at[part], out_hbm.at[part], sent.at[place // 16]))
+        if place % 8 == 7:
+            part = pl.ds(place - 7, 8)
+            copies.append(pltpu.make_async_copy(out_ref.at[part], out_hbm.at[part], sent.at[place // 8]))
             copies[-1].start()
     for copy in copies:
         copy.wait()
@@ -208,7 +208,7 @@
             pltpu.VMEM((BANDS * WIDE, LANES), f32),
             pltpu.VMEM((N * WIDE, LANES), f32),
             pltpu.VMEM((N, 32, LANES), bf16),
-            pltpu.SemaphoreType.DMA((4,)),
+            pltpu.SemaphoreType.DMA((8,)),
         ],
         v,
         conduction.reshape(BANDS, N * N),

time: 91.9 us -> 91.9 us (level)
  no operation moved by 1% of the time
where the time goes in v14:
time: 91.9 us; the launch traced here: 91.4 us
  blocking collectives  72.1 us (78%)
  starting transfers between devices  9.01 us (10%)
  Pallas kernels  4.39 us (5%)
  waiting for transfers between devices  2.49 us (3%)
  local copies, waits for them, and re-layouts  1.72 us (2%)
    all_to_all x1, blocking collectives, shards(): values = lax.all_to_all(values, ('zh', 'zl'), 0, 0, tiled=True)  18.1 us
    psum x1, blocking collectives, shards(): v = lax.psum(own.astype(bf16).reshape(32, LANES), 'zh')  14 us
    all_to_all x1, blocking collectives, shards(): columns = lax.all_to_all(cols, ('x', 'y'), 0, 0, tiled=True)  13.7 us
    psum x1, blocking collectives, shards(): spots = lax.psum(spots, 'zl')  11.2 us
    all_to_all x1, starting transfers between devices, shards(): block = lax.all_to_all(half, GA, 0, 0, tiled=True)  9.01 us
    all_gather x1, blocking collectives, shards(): local = lax.all_gather(valence.reshape(-1, N * N), 'c', tiled=True)  8.85 us
    all_gather x1, blocking collectives, shards(): values = lax.all_gather(values, 'c')  6.17 us
    pallas_call x4, Pallas kernels, call(): pl.pallas_call(kernel, out_shape=jax.ShapeDtypeStruct(shape, dtype), in_s...  4.39 us
  transfers between devices with their start and end apart: 1, of which 1 were waited for; matrix products, arithmetic and copies ran while one was open for 1% of the time, Pallas kernels for 0%

profile of v14, /device:TPU:1, one launch (start us, length us, event | category | flops | bytes accessed | tf_op | source)
XLA Modules:
  0.0 91.4 jit_solution(6561592907432718071)
XLA Ops:
  0.7 0.0 copy-start
  0.7 8.9 %all-gather = bf16[32,1,4096]{2,0,1:T(8,128)(2,1)S(1)} all-gather(bf16[16,1,4096]{2,0,1:T(8,128)(2,1)} %param.11), channel_id=2, replica_groups=mesh['y'=4,'zl'=4,'x'=4,'zh'=4,'c'=2] {'c'}, dimensions={0}, use_global_device_ids=true | all-gather | bytes 393216 | tf_op jit(solution)/shard_map/all_gather | solution.py:198
  9.5 0.0 copy-start.1
  9.5 0.2 fusion
  9.7 14.0 %psum.14.v_ref = bf16[32,128]{1,0:T(8,128)(2,1)S(1)} all-reduce(bf16[32,128]{1,0:T(8,128)(2,1)S(1)} %bitcast.19), channel_id=1, replica_groups=mesh['y'=4,'zl'=4,'x'=4,'zh'=4,'c'=2] {'zh'}, use_global_device_ids=true, to_apply=%region_1.2 | all-reduce | flops 4096 | bytes 16384 | tf_op jit(solution)/shard_map/psum | solution.py:201
  23.7 0.0 copy-done
  23.7 0.0 copy-done.1
  23.7 1.4 %shard_map.109 = bf16[64,32,128]{2,1,0:T(8,128)(2,1)} custom-call(bf16[32,128]{1,0:T(8,128)(2,1)S(1)} %psum.14.v_ref, bf16[32,4096]{1,0:T(8,128)(2,1)S(1)} %bitcast.18, bf16[128,32]{1,0:T(8,128)(2,1)S(1)} %copy-done.1), custom_call_target="tpu_custom_call" | custom-call | tf_op jit(solution)/shard_map/pallas_call | solution.py:183
  25.2 0.0 copy-start.7
  25.2 0.0 copy-start.4
  25.2 9.0 %all-to-all-start = ((bf16[64,32,128]{2,1,0:T(8,128)(2,1)}), bf16[64,32,128]{2,1,0:T(8,128)(2,1)S(1)}, u32[]{:S(2)}, u32[]{:S(2)}) async-start(bf16[64,32,128]{2,1,0:T(8,128)(2,1)} %shard_map.109), calls=%async_computation | async-start | bytes 1048576 | tf_op jit(solution)/shard_map/all_to_all | solution.py:221
  34.2 0.0 copy-start.8
  34.2 0.0 copy-start.3
  34.2 0.0 copy-done.7
  34.3 0.1 convert_element_type.60
  34.3 0.0 copy-done.4
  34.3 0.1 stack_tile.3
  34.4 0.4 copy-done.8
  34.9 0.0 copy-start.5
  34.9 0.0 copy-start.6
  34.9 0.6 copy-done.5
  35.6 0.0 copy-done.6
  35.6 0.1 broadcast_select_fusion
  35.7 11.2 %psum.15 = s32[4,192]{1,0:T(4,128)S(1)} all-reduce(s32[4,192]{1,0:T(4,128)S(1)} %broadcast_select_fusion), channel_id=1, replica_groups=mesh['y'=4,'zl'=4,'x'=4,'zh'=4,'c'=2] {'zl'}, use_global_device_ids=true, to_apply=%region_2.3 | all-reduce | flops 768 | bytes 6144 | tf_op jit(solution)/shard_map/psum | solution.py:225
  46.8 0.0 copy-done.3
  46.8 0.0 copy-start.2
  46.8 0.3 convolution_convert_fusion.p_ref
  47.2 0.4 copy-done.2
  47.6 0.3 convolution_convert_fusion.1.e_ref
  47.9 2.5 %all-to-all-done.r_ref = bf16[64,32,128]{2,1,0:T(8,128)(2,1)S(1)} async-done(((bf16[64,32,128]{2,1,0:T(8,128)(2,1)}), bf16[64,32,128]{2,1,0:T(8,128)(2,1)S(1)}, u32[]{:S(2)}, u32[]{:S(2)}) %all-to-all-start) | async-done | bytes 524320 | tf_op jit(solution)/shard_map/all_to_all | solution.py:221
  50.4 1.4 %shard_map.110 = bf16[16,24,128]{2,1,0:T(8,128)(2,1)S(1)} custom-call(bf16[64,32,128]{2,1,0:T(8,128)(2,1)S(1)} %all-to-all-done.r_ref, bf16[4,192,256]{2,1,0:T(8,128)(2,1)S(1)} %convolution_convert_fusion.1.e_ref, bf16[4,192,256]{2,1,0:T(8,128)(2,1)S(1)} %convolution_convert_fusion.p_ref, f32[6,128]{1,0:T(8,128)S(1)} %stack.20.fact_ref), custom_call_target="tpu_custom_call" | custom-call | tf_op jit(solution)/shard_map/pallas_call | solution.py:183
  51.8 18.1 %all_to_all.15 = bf16[16,24,128]{2,1,0:T(8,128)(2,1)S(1)} all-to-all(bf16[16,24,128]{2,1,0:T(8,128)(2,1)S(1)} %shard_map.110), channel_id=1, replica_groups=mesh['y'=4,'zl'=4,'x'=4,'zh'=4,'c'=2] {'zh','zl'}, dimensions={0} | all-to-all | bytes 196608 | tf_op jit(solution)/shard_map/all_to_all | solution.py:243
  69.9 6.2 %all-gather.1 = bf16[32,24,128]{2,1,0:T(8,128)(2,1)S(1)} all-gather(bf16[16,24,128]{2,1,0:T(8,128)(2,1)S(1)} %all_to_all.15), channel_id=3, replica_groups=mesh['y'=4,'zl'=4,'x'=4,'zh'=4,'c'=2] {'c'}, dimensions={0}, use_global_device_ids=true | all-gather | bytes 294912 | tf_op jit(solution)/shard_map/all_gather | solution.py:244
  76.1 0.2 shard_map.111
  76.4 13.7 %all_to_all.16.b_ref = bf16[16,128,128]{2,1,0:T(8,128)(2,1)S(1)} all-to-all(bf16[16,128,128]{2,1,0:T(8,128)(2,1)S(1)} %shard_map.111), channel_id=1, replica_groups=mesh['y'=4,'zl'=4,'x'=4,'zh'=4,'c'=2] {'x','y'}, dimensions={0} | all-to-all | bytes 1048576 | tf_op jit(solution)/shard_map/all_to_all | solution.py:253
  90.1 1.3 %shard_map.112 = f32[2,128,512]{2,1,0:T(8,128)} custom-call(bf16[2,16,24,128]{3,2,1,0:T(8,128)(2,1)S(1)} %bitcast.17, bf16[16,128,128]{2,1,0:T(8,128)(2,1)S(1)} %all_to_all.16.b_ref), custom_call_target="tpu_custom_call" | custom-call | tf_op jit(solution)/shard_map/pallas_call | solution.py:183
  (12 shorter events, 0.1 us)
Async XLA Ops:
  0.7 23.0 %copy-start = (bf16[32,1,4096]{2,0,1:T(8,128)(2,1)S(1)}, bf16[32,1,4096]{2,0,1:T(8,128)(2,1)}, u32[]{:S(2)}) copy-start(bf16[32,1,4096]{2,0,1:T(8,128)(2,1)} %param.12) | copy-start | bytes 786436
  9.5 14.2 %copy-start.1 = (bf16[128,32]{1,0:T(8,128)(2,1)S(1)}, bf16[128,32]{1,0:T(8,128)(2,1)}, u32[]{:S(2)}) copy-start(bf16[128,32]{1,0:T(8,128)(2,1)} %constant.37.e_ref) | copy-start | bytes 24580
  25.2 9.1 %copy-start.7 = (s32[32]{0:T(128)S(1)}, s32[32]{0:T(128)}, u32[]{:S(2)}) copy-start(s32[32]{0:T(128)} %param.15) | copy-start | bytes 388
  25.2 9.2 %copy-start.4 = (f32[32]{0:T(128)S(1)}, f32[32]{0:T(128)}, u32[]{:S(2)}) copy-start(f32[32]{0:T(128)} %param.16) | copy-start | bytes 388
  25.2 25.2 %all-to-all-start = ((bf16[64,32,128]{2,1,0:T(8,128)(2,1)}), bf16[64,32,128]{2,1,0:T(8,128)(2,1)S(1)}, u32[]{:S(2)}, u32[]{:S(2)}) async-start(bf16[64,32,128]{2,1,0:T(8,128)(2,1)} %shard_map.109), calls=%async_computation | async-start | bytes 1048576 | tf_op jit(solution)/shard_map/all_to_all | solution.py:221
  34.2 0.7 copy-start.8
  34.2 12.6 %copy-start.3 = (bf16[64,256,1]{1,0,2:T(8,128)(2,1)S(1)}, bf16[64,256,1]{1,0,2:T(8,128)(2,1)}, u32[]{:S(2)}) copy-start(bf16[64,256,1]{1,0,2:T(8,128)(2,1)} %constant.41) | copy-start | bytes 98308
  34.9 0.7 copy-start.5
  34.9 0.7 copy-start.6
  46.8 0.8 copy-start.2
